TPU v7x, 32 devices: a whole 2x2x4 slice. The times are simulated.
32 devices in a mesh: dp: 16 (over z, y, core), expert: 2 (over x).
Axes of the slice: x: 2, y: 2, z: 4, core: 2. Of those that a mesh axis runs over, the one named last changes fastest.
Arguments:
- tokens: bfloat16 [8192, 1536], P(('dp', 'expert')), may hold values from -6 to 6
- norm1_gain: bfloat16 [1536], P('dp'), may hold values from 0.5 to 1.5
- w_query: bfloat16 [1536, 1536], P('dp'), may hold values from -0.15625 to 0.15625
- w_key: bfloat16 [1536, 256], P('dp'), may hold values from -0.15625 to 0.15625
- w_value: bfloat16 [1536, 256], P('dp'), may hold values from -0.15625 to 0.15625
- w_out: bfloat16 [1536, 1536], P('dp'), may hold values from -0.625 to 0.625
- norm2_gain: bfloat16 [1536], P('dp'), may hold values from 0.5 to 1.5
- w_router: bfloat16 [1536, 8], P('dp'), may hold values from -0.06982422 to 0.06982422
- w_gate: bfloat16 [8, 1536, 768], P('expert'), may hold values from -0.15625 to 0.15625
- w_up: bfloat16 [8, 1536, 768], P('expert'), may hold values from -0.15625 to 0.15625
- w_down: bfloat16 [8, 768, 1536], P('expert'), may hold values from -0.44921875 to 0.44921875
- expert_ids: int32 [8192, 4], P(('dp', 'expert')), may hold values from 0 to 7, all different within a row; in each aligned block of 128 rows (0 to 127, 128 to 255, ...) at most 96 rows name the same one
- prefix_len: int32 [32], P(('dp', 'expert')), may hold values from 25 to 128
- out_grad: bfloat16 [8192, 1536], P(('dp', 'expert')), may hold values from -6 to 6
Outputs:
- block_out: bfloat16 [8192, 1536], P(('dp', 'expert'))
- tokens_grad: bfloat16 [8192, 1536], P(('dp', 'expert'))
- norm1_grad: float32 [1536], P('dp')
- query_grad: float32 [1536, 1536], P('dp')
- key_grad: float32 [1536, 256], P('dp')
- value_grad: float32 [1536, 256], P('dp')
- outproj_grad: float32 [1536, 1536], P('dp')
- norm2_grad: float32 [1536], P('dp')
- router_grad: float32 [1536, 8], P('dp')
- gate_grad: float32 [8, 1536, 768], P('expert', 'dp')
- up_grad: float32 [8, 1536, 768], P('expert', 'dp')
- down_grad: float32 [8, 768, 1536], P('expert', None, 'dp')
Inputs may be any that keep to these rules, and one draw needn't show every extreme that they name: `expert_ids`: each row names 4 different experts. Within the rows of one device's micro-batch (aligned blocks of 128 rows) no expert is named by more than 96 rows, and some block reaches 96.
All inputs are finite; a program needn't handle non-finite values.
Results may differ from a plain program's by a relative error of at most 0.024.
Values may be sent and summed in bfloat16 or wider, within the bound.
No kernel may reach another device: no remote copies, remote signals or barrier semaphores. Data moves between devices by JAX's collectives and lax.ppermute only.
A program may use at most 192 MiB of HBM per device.

v0:
```python
import math

import jax
import jax.numpy as jnp
from jax import lax
from jax.sharding import PartitionSpec as P

HQ = 12
HK = 2
HD = 128
MICRO = 2


def rms_scale(values, gain_vec):
    inverse = lax.rsqrt(jnp.mean(values * values, axis=-1, keepdims=True) + 1e-06)
    return values * inverse * gain_vec


def angles(length, head_size):
    positions = jnp.arange(length).astype(jnp.float32)
    freq_rates = jnp.exp(
        -(2.0 * jnp.arange(head_size // 2).astype(jnp.float32) / head_size) * math.log(1000000.0)
    )
    angle_tab = positions[:, None] * freq_rates[None, :]
    return (jnp.cos(angle_tab)[:, None, :], jnp.sin(angle_tab)[:, None, :])


def rotary(values, cosine_tab, sine_tab):
    half_dim = values.shape[-1] // 2
    first_half = values[..., :half_dim]
    second_half = values[..., half_dim:]
    return jnp.concatenate(
        [
            first_half * cosine_tab - second_half * sine_tab,
            second_half * cosine_tab + first_half * sine_tab,
        ],
        axis=-1,
    )


def expert_act(gate_pre, up_pre):
    return jax.nn.gelu(gate_pre, approximate=True) * up_pre


def left_product(left_mat, right_mat):
    return lax.dot_general(
        left_mat, right_mat, (((0,), (0,)), ((), ())), preferred_element_type=jnp.float32
    )


def local(
    tokens,
    norm1_gain,
    w_query,
    w_key,
    w_value,
    w_out,
    norm2_gain,
    w_router,
    w_gate,
    w_up,
    w_down,
    expert_ids,
    prefix_len,
    out_grad,
):
    gathered = (
        lax.all_gather(norm1_gain, "dp", axis=0, tiled=True),
        lax.all_gather(w_query, "dp", axis=0, tiled=True),
        lax.all_gather(w_key, "dp", axis=0, tiled=True),
        lax.all_gather(w_value, "dp", axis=0, tiled=True),
        lax.all_gather(w_out, "dp", axis=0, tiled=True),
        lax.all_gather(norm2_gain, "dp", axis=0, tiled=True),
        lax.all_gather(w_router, "dp", axis=0, tiled=True),
    )
    gain_one, query_w, key_w, value_w, output_w, gain_two, router_w = gathered
    length, model_width = tokens.shape
    experts_all = router_w.shape[1]
    local_count = w_gate.shape[0]
    owners = lax.axis_size("expert")
    top_count = expert_ids.shape[1]
    block_rows = length // MICRO
    capacity = 3 * block_rows * top_count // (2 * experts_all)
    assigned = block_rows * top_count
    group_size = HQ // HK
    score_scale = HD ** (-0.5)
    cosine_tab, sine_tab = angles(length, HD)
    expert_range = jnp.arange(experts_all, dtype=jnp.int32)
    inputs_f = tokens.astype(jnp.float32)
    gain_onef = gain_one.astype(jnp.float32)
    first_in = rms_scale(inputs_f, gain_onef).astype(jnp.bfloat16)
    query_pre = jnp.dot(first_in, query_w, preferred_element_type=jnp.float32).reshape(
        length, HQ, HD
    )
    queries = (
        rotary(query_pre, cosine_tab, sine_tab)
        .astype(jnp.bfloat16)
        .reshape(length, HK, group_size, HD)
    )
    key_pre = jnp.dot(first_in, key_w, preferred_element_type=jnp.float32).reshape(length, HK, HD)
    keys_rot = rotary(key_pre, cosine_tab, sine_tab).astype(jnp.bfloat16)
    values_b = (
        jnp.dot(first_in, value_w, preferred_element_type=jnp.float32)
        .astype(jnp.bfloat16)
        .reshape(length, HK, HD)
    )
    positions = jnp.arange(length)
    allowed = (positions[None, :] <= positions[:, None]) | (positions[None, :] < prefix_len[0])

    def masked_scores():
        scores = (
            jnp.einsum("ihrd,jhd->hrij", queries, keys_rot, preferred_element_type=jnp.float32)
            * score_scale
        )
        return jnp.where(allowed, scores, -1e30)

    masked = masked_scores()
    row_peak = jnp.max(masked, axis=-1, keepdims=True)
    log_total = row_peak + jnp.log(jnp.sum(jnp.exp(masked - row_peak), axis=-1, keepdims=True))
    prob_bf = jnp.exp(masked - log_total).astype(jnp.bfloat16)
    attended = jnp.einsum("hrij,jhd->ihrd", prob_bf, values_b, preferred_element_type=jnp.float32)
    attended = attended.reshape(length, HQ * HD).astype(jnp.bfloat16)
    resid = inputs_f + jnp.dot(attended, output_w, preferred_element_type=jnp.float32)
    gain_twof = gain_two.astype(jnp.float32)
    second_in = rms_scale(resid, gain_twof).astype(jnp.bfloat16)
    logits = jnp.dot(second_in, router_w, preferred_element_type=jnp.float32)
    onehot = (expert_ids[:, :, None] == expert_range[None, None, :]).astype(jnp.float32)
    chosen = jnp.sum(onehot * logits[:, None, :], axis=-1)
    gate_probs = jax.nn.softmax(chosen, axis=-1)
    padding_row = jnp.zeros((1, model_width), jnp.bfloat16)
    stored = []
    mixtures = []
    for block_idx in range(MICRO):
        row_start = block_idx * block_rows
        ids_flat = expert_ids[row_start : row_start + block_rows].reshape(-1)
        hot_int = (ids_flat[:, None] == expert_range[None, :]).astype(jnp.int32)
        position = jnp.sum(jnp.cumsum(hot_int, axis=0) * hot_int, axis=1) - 1
        slot_ids = ids_flat * capacity + position
        source = (
            jnp.full((experts_all * capacity,), assigned, jnp.int32)
            .at[slot_ids]
            .set(jnp.arange(assigned, dtype=jnp.int32))
        )
        rows_in = jnp.concatenate(
            [second_in[row_start : row_start + block_rows], padding_row], axis=0
        )
        outgoing = rows_in[source // top_count].reshape(owners, local_count, capacity, model_width)
        received = lax.all_to_all(outgoing, "expert", split_axis=0, concat_axis=0, tiled=True)
        gate_pre = jnp.einsum(
            "secd,edf->secf", received, w_gate, preferred_element_type=jnp.float32
        )
        up_pre = jnp.einsum("secd,edf->secf", received, w_up, preferred_element_type=jnp.float32)
        hidden = expert_act(gate_pre, up_pre).astype(jnp.bfloat16)
        expert_out = jnp.einsum(
            "secf,efd->secd", hidden, w_down, preferred_element_type=jnp.float32
        ).astype(jnp.bfloat16)
        returned = lax.all_to_all(
            expert_out, "expert", split_axis=0, concat_axis=0, tiled=True
        ).reshape(experts_all * capacity, model_width)
        picked = returned[slot_ids].reshape(block_rows, top_count, model_width).astype(jnp.float32)
        gate_block = gate_probs[row_start : row_start + block_rows]
        mixtures.append(jnp.sum(gate_block[:, :, None] * picked, axis=1))
        stored.append((slot_ids, source, received, picked, gate_pre, up_pre, hidden))
    block_out = (resid + jnp.concatenate(mixtures, axis=0)).astype(jnp.bfloat16)
    regathered = (
        lax.all_gather(norm1_gain, "dp", axis=0, tiled=True),
        lax.all_gather(w_query, "dp", axis=0, tiled=True),
        lax.all_gather(w_key, "dp", axis=0, tiled=True),
        lax.all_gather(w_value, "dp", axis=0, tiled=True),
        lax.all_gather(w_out, "dp", axis=0, tiled=True),
        lax.all_gather(norm2_gain, "dp", axis=0, tiled=True),
        lax.all_gather(w_router, "dp", axis=0, tiled=True),
    )
    gain_one, query_w, key_w, value_w, output_w, gain_two, router_w = regathered
    cotangent = out_grad.astype(jnp.float32)
    gate_acc = jnp.zeros(w_gate.shape, jnp.float32)
    up_acc = jnp.zeros(w_up.shape, jnp.float32)
    down_acc = jnp.zeros(w_down.shape, jnp.float32)
    chosen_parts = []
    second_parts = []
    for block_idx in range(MICRO):
        row_start = block_idx * block_rows
        slot_ids, source, received, picked, gate_pre, up_pre, hidden = stored[block_idx]
        cot_block = cotangent[row_start : row_start + block_rows]
        gate_block = gate_probs[row_start : row_start + block_rows]
        gate_signal = jnp.sum(cot_block[:, None, :] * picked, axis=-1)
        chosen_parts.append(
            gate_block * (gate_signal - jnp.sum(gate_block * gate_signal, axis=-1, keepdims=True))
        )
        out_back = (
            (gate_block[:, :, None] * cot_block[:, None, :])
            .astype(jnp.bfloat16)
            .reshape(assigned, model_width)
        )
        rows_back = jnp.concatenate([out_back, padding_row], axis=0)[source]
        rows_back = rows_back.reshape(owners, local_count, capacity, model_width)
        grad_in = lax.all_to_all(rows_back, "expert", split_axis=0, concat_axis=0, tiled=True)
        hidden_grad = jnp.einsum(
            "secd,efd->secf", grad_in, w_down, preferred_element_type=jnp.float32
        )
        down_acc = down_acc + jnp.einsum(
            "secf,secd->efd", hidden, grad_in, preferred_element_type=jnp.float32
        )
        _, act_pull = jax.vjp(expert_act, gate_pre, up_pre)
        gate_pgrad, up_pgrad = act_pull(hidden_grad)
        gate_pgrad = gate_pgrad.astype(jnp.bfloat16)
        up_pgrad = up_pgrad.astype(jnp.bfloat16)
        gate_acc = gate_acc + jnp.einsum(
            "secd,secf->edf", received, gate_pgrad, preferred_element_type=jnp.float32
        )
        up_acc = up_acc + jnp.einsum(
            "secd,secf->edf", received, up_pgrad, preferred_element_type=jnp.float32
        )
        rows_grad = jnp.einsum(
            "secf,edf->secd", gate_pgrad, w_gate, preferred_element_type=jnp.float32
        )
        rows_grad = rows_grad + jnp.einsum(
            "secf,edf->secd", up_pgrad, w_up, preferred_element_type=jnp.float32
        )
        back_grad = (
            lax.all_to_all(
                rows_grad.astype(jnp.bfloat16), "expert", split_axis=0, concat_axis=0, tiled=True
            )
            .astype(rows_grad.dtype)
            .reshape(experts_all * capacity, model_width)
        )
        second_parts.append(
            jnp.sum(back_grad[slot_ids].reshape(block_rows, top_count, model_width), axis=1)
        )
    chosen_grad = jnp.concatenate(chosen_parts, axis=0)
    logit_grad = jnp.sum(onehot * chosen_grad[:, :, None], axis=1).astype(jnp.bfloat16)
    router_acc = left_product(second_in, logit_grad)
    second_grad = jnp.concatenate(second_parts, axis=0) + jnp.dot(
        logit_grad, router_w.T, preferred_element_type=jnp.float32
    )
    _, norm_two_pull = jax.vjp(rms_scale, resid, gain_two.astype(jnp.float32))
    resid_norm_grad, gain_two_grad = norm_two_pull(second_grad)
    resid_grad = cotangent + resid_norm_grad
    branch_grad = resid_grad.astype(jnp.bfloat16)
    output_acc = left_product(attended, branch_grad)
    attended_grad = jnp.dot(branch_grad, output_w.T, preferred_element_type=jnp.float32).astype(
        jnp.bfloat16
    )
    attended_grad = attended_grad.reshape(length, HK, group_size, HD)
    masked = masked_scores()
    prob_full = jnp.exp(masked - log_total)
    prob_bf = prob_full.astype(jnp.bfloat16)
    prob_grad = jnp.einsum(
        "ihrd,jhd->hrij", attended_grad, values_b, preferred_element_type=jnp.float32
    )
    row_inner = jnp.sum(prob_full * prob_grad, axis=-1, keepdims=True)
    score_grad = (prob_full * (prob_grad - row_inner)).astype(jnp.bfloat16)
    query_rot_grad = (
        jnp.einsum("hrij,jhd->ihrd", score_grad, keys_rot, preferred_element_type=jnp.float32)
        * score_scale
    )
    query_back = rotary(query_rot_grad.reshape(length, HQ, HD), cosine_tab, -sine_tab)
    query_back = query_back.astype(jnp.bfloat16).reshape(length, HQ * HD)
    key_rot_grad = (
        jnp.einsum("hrij,ihrd->jhd", score_grad, queries, preferred_element_type=jnp.float32)
        * score_scale
    )
    key_back = (
        rotary(key_rot_grad, cosine_tab, -sine_tab).astype(jnp.bfloat16).reshape(length, HK * HD)
    )
    value_back = jnp.einsum(
        "hrij,ihrd->jhd", prob_bf, attended_grad, preferred_element_type=jnp.float32
    )
    value_back = value_back.astype(jnp.bfloat16).reshape(length, HK * HD)
    query_acc = left_product(first_in, query_back)
    key_acc = left_product(first_in, key_back)
    value_acc = left_product(first_in, value_back)
    first_grad = jnp.dot(query_back, query_w.T, preferred_element_type=jnp.float32)
    first_grad = first_grad + jnp.dot(key_back, key_w.T, preferred_element_type=jnp.float32)
    first_grad = first_grad + jnp.dot(value_back, value_w.T, preferred_element_type=jnp.float32)
    _, norm_one_pull = jax.vjp(rms_scale, inputs_f, gain_one.astype(jnp.float32))
    input_norm_grad, gain_one_grad = norm_one_pull(first_grad)
    tokens_grad = (resid_grad + input_norm_grad).astype(jnp.bfloat16)
    dense_shares = (
        lax.psum_scatter(
            gain_one_grad.astype(jnp.bfloat16), "dp", scatter_dimension=0, tiled=True
        ).astype(jnp.float32),
        lax.psum_scatter(
            query_acc.astype(jnp.bfloat16), "dp", scatter_dimension=0, tiled=True
        ).astype(jnp.float32),
        lax.psum_scatter(
            key_acc.astype(jnp.bfloat16), "dp", scatter_dimension=0, tiled=True
        ).astype(jnp.float32),
        lax.psum_scatter(
            value_acc.astype(jnp.bfloat16), "dp", scatter_dimension=0, tiled=True
        ).astype(jnp.float32),
        lax.psum_scatter(
            output_acc.astype(jnp.bfloat16), "dp", scatter_dimension=0, tiled=True
        ).astype(jnp.float32),
        lax.psum_scatter(
            gain_two_grad.astype(jnp.bfloat16), "dp", scatter_dimension=0, tiled=True
        ).astype(jnp.float32),
        lax.psum_scatter(
            router_acc.astype(jnp.bfloat16), "dp", scatter_dimension=0, tiled=True
        ).astype(jnp.float32),
    )
    dense_sums = (
        lax.psum(dense_shares[0].astype(jnp.bfloat16), "expert").astype(jnp.float32),
        lax.psum(dense_shares[1].astype(jnp.bfloat16), "expert").astype(jnp.float32),
        lax.psum(dense_shares[2].astype(jnp.bfloat16), "expert").astype(jnp.float32),
        lax.psum(dense_shares[3].astype(jnp.bfloat16), "expert").astype(jnp.float32),
        lax.psum(dense_shares[4].astype(jnp.bfloat16), "expert").astype(jnp.float32),
        lax.psum(dense_shares[5].astype(jnp.bfloat16), "expert").astype(jnp.float32),
        lax.psum(dense_shares[6].astype(jnp.bfloat16), "expert").astype(jnp.float32),
    )
    expert_sums = (
        lax.psum_scatter(
            gate_acc.astype(jnp.bfloat16), "dp", scatter_dimension=1, tiled=True
        ).astype(jnp.float32),
        lax.psum_scatter(up_acc.astype(jnp.bfloat16), "dp", scatter_dimension=1, tiled=True).astype(
            jnp.float32
        ),
        lax.psum_scatter(
            down_acc.astype(jnp.bfloat16), "dp", scatter_dimension=2, tiled=True
        ).astype(jnp.float32),
    )
    return (
        block_out,
        tokens_grad,
        dense_sums[0],
        dense_sums[1],
        dense_sums[2],
        dense_sums[3],
        dense_sums[4],
        dense_sums[5],
        dense_sums[6],
        expert_sums[0],
        expert_sums[1],
        expert_sums[2],
    )


def solution(mesh):
    placed = (
        P(("dp", "expert"), None),
        P("dp"),
        P("dp", None),
        P("dp", None),
        P("dp", None),
        P("dp", None),
        P("dp"),
        P("dp", None),
        P("expert", None, None),
        P("expert", None, None),
        P("expert", None, None),
        P(("dp", "expert"), None),
        P(("dp", "expert")),
        P(("dp", "expert"), None),
    )
    return jax.shard_map(
        local,
        mesh=mesh,
        in_specs=placed,
        out_specs=(
            P(("dp", "expert"), None),
            P(("dp", "expert"), None),
            P("dp"),
            P("dp", None),
            P("dp", None),
            P("dp", None),
            P("dp", None),
            P("dp"),
            P("dp", None),
            P("expert", "dp", None),
            P("expert", "dp", None),
            P("expert", None, "dp"),
        ),
        check_vma=False,
    )
```

profile of v0, /device:TPU:0, one launch (start us, length us, event | category | flops | bytes accessed | tf_op | source)
XLA Modules:
  0.0 1196.4 jit_solution(16795612409781016356)
XLA Ops:
  14.4 36.2 %all-reduce.8 = (bf16[1536]{0:T(1024)(128)(2,1)S(1)}, bf16[1536]{0:T(1024)(128)(2,1)S(1)}) all-reduce(bf16[1536]{0:T(1024)(128)(2,1)S(1)} %dynamic-update-slice, bf16[1536]{0:T(1024)(128)(2,1)S(1)} %dynamic-update-slice.1), channel_id=1, replica_groups=mesh['dp'=16,'expert'=2] {'dp'}, use_global_device_ids=true, to_apply=%add.3 | all-reduce | flops 3072 | bytes 12288
  50.7 17.7 %all-gather = bf16[16,96,8]{1,2,0:T(8,128)(2,1)S(1)} all-gather(bf16[1,96,8]{1,2,0:T(8,128)(2,1)} %bitcast.322), channel_id=1, replica_groups=mesh['dp'=16,'expert'=2] {'dp'}, dimensions={0}, use_global_device_ids=true | all-gather | bytes 26112 | tf_op jit(solution)/shard_map/all_gather | solution.py:74
  74.1 23.7 %all_gather.30 = bf16[1536,256]{1,0:T(8,128)(2,1)S(1)} all-gather(bf16[96,256]{1,0:T(8,128)(2,1)S(1)} %copy-done.67), channel_id=1, replica_groups=mesh['dp'=16,'expert'=2] {'dp'}, dimensions={0}, use_global_device_ids=true | all-gather | bytes 835584 | tf_op jit(solution)/shard_map/all_gather | solution.py:70
  102.9 4.9 mul.723
  109.9 5.0 mul.740
  121.6 20.1 %all_gather.29 = bf16[1536,256]{1,0:T(8,128)(2,1)S(1)} all-gather(bf16[96,256]{1,0:T(8,128)(2,1)S(1)} %copy-done.68), channel_id=1, replica_groups=mesh['dp'=16,'expert'=2] {'dp'}, dimensions={0}, use_global_device_ids=true | all-gather | bytes 835584 | tf_op jit(solution)/shard_map/all_gather | solution.py:71
  161.6 5.0 all-to-all-start
  174.3 20.8 %all-to-all-done = bf16[2,4,96,1536]{3,2,1,0:T(8,128)(2,1)} async-done(((bf16[2,4,96,1536]{3,2,1,0:T(8,128)(2,1)}), bf16[2,4,96,1536]{3,2,1,0:T(8,128)(2,1)}, u32[]{:S(2)}, u32[]{:S(2)}) %all-to-all-start) | async-done | bytes 2359328 | tf_op jit(solution)/shard_map/all_to_all | solution.py:148
  195.1 5.1 all-to-all-start.4
  211.4 7.8 fusion.17
  219.3 8.7 all-to-all-done.4
  231.8 7.7 fusion.5
  239.5 9.7 fusion.59
  249.2 9.2 all-to-all-done.2
  258.5 5.2 all-to-all-start.6
  263.7 6.2 fusion.43
  274.9 14.6 %all-to-all-done.6 = bf16[2,4,96,1536]{3,2,1,0:T(8,128)(2,1)} async-done(((bf16[2,4,96,1536]{3,2,1,0:T(8,128)(2,1)}), bf16[2,4,96,1536]{3,2,1,0:T(8,128)(2,1)}, u32[]{:S(2)}, u32[]{:S(2)}) %all-to-all-start.6) | async-done | bytes 2359328 | tf_op jit(solution)/shard_map/all_to_all | solution.py:197
  293.6 7.7 fusion.3
  301.4 7.4 fusion.66
  314.6 5.4 fusion.11
  319.9 4.9 all-to-all-start.3
  324.9 9.8 fusion.49
  338.1 5.4 fusion.13
  343.5 6.4 all-to-all-done.3
  349.8 5.4 all-to-all-start.7
  355.2 8.2 fusion.46
  371.0 4.6 multiply_reduce_fusion.1
  375.7 6.4 gather_fusion.3
  385.0 4.6 multiply_reduce_fusion
  398.3 6.9 gather_fusion.7
  405.2 4.8 reshape.390
  410.3 7.2 all-to-all-done.5
  420.5 6.0 gather_fusion.5
  440.6 4.8 convolution_convert_fusion.4
  479.8 30.0 %all-reduce.7 = (bf16[1536]{0:T(1024)(128)(2,1)S(1)}, bf16[1536]{0:T(1024)(128)(2,1)S(1)}) all-reduce(bf16[1536]{0:T(1024)(128)(2,1)S(1)} %get-tuple-element.18, bf16[1536]{0:T(1024)(128)(2,1)S(1)} %get-tuple-element.12), channel_id=2, replica_groups=mesh['dp'=16,'expert'=2] {'dp'}, use_global_device_ids=true, to_apply=%region_28.29.clone | all-reduce | flops 3072 | bytes 12288
  512.4 54.2 %reduce-scatter.15.cloned.1.call-done = bf16[96,256]{1,0:T(8,128)(2,1)} async-done(((bf16[1536,256]{1,0:T(8,128)(2,1)}), bf16[96,256]{1,0:T(8,128)(2,1)}) %reduce-scatter.15.cloned.1.call-update) | async-done | bytes 49168 | tf_op jit(solution)/shard_map/reduce_scatter | solution.py:289
  566.6 59.5 %reduce-scatter.13.cloned.1.call-done = bf16[96,256]{1,0:T(8,128)(2,1)} async-done(((bf16[1536,256]{1,0:T(8,128)(2,1)}), bf16[96,256]{1,0:T(8,128)(2,1)}) %reduce-scatter.13.cloned.1.call-update) | async-done | bytes 49168 | tf_op jit(solution)/shard_map/reduce_scatter | solution.py:286
  626.2 11.3 fusion.77
  637.5 67.4 %reduce-scatter.17.cloned.1.call-done = bf16[96,1536]{1,0:T(8,128)(2,1)} async-done(((bf16[1536,1536]{1,0:T(8,128)(2,1)}), bf16[96,1536]{1,0:T(8,128)(2,1)}) %reduce-scatter.17.cloned.1.call-update) | async-done | bytes 294928 | tf_op jit(solution)/shard_map/reduce_scatter | solution.py:292
  705.0 78.5 %reduce-scatter.11.cloned.1.call-done = bf16[96,1536]{1,0:T(8,128)(2,1)} async-done(((bf16[1536,1536]{1,0:T(8,128)(2,1)}), bf16[96,1536]{1,0:T(8,128)(2,1)}) %reduce-scatter.11.cloned.1.call-update) | async-done | bytes 294928 | tf_op jit(solution)/shard_map/reduce_scatter | solution.py:283
  783.7 13.4 %fusion = bf16[4,768,1536]{1,2,0:T(8,128)(2,1)} fusion(f32[4,768,1536,1]{1,2,3,0:T(8,128)} %fusion.77, bf16[2,4,96,768]{3,2,0,1:T(8,128)(2,1)S(1)} %copy-done.33, bf16[2,4,96,1536]{3,2,1,0:T(8,128)(2,1)} %all-to-all-done.6), kind=kOutput, calls=%fused_computation.11 | convolution fusion | flops 1821376512 | bytes 31850496 | tf_op jit(solution)/shard_map/secf,secd->efd/dot_general | solution.py:201
  797.2 11.3 fusion.98
  808.5 11.0 fusion.2
  819.6 11.2 fusion.95
  830.7 11.4 fusion.1
  856.5 99.9 %reduce-scatter.23.cloned.1.call-done = bf16[4,768,96]{1,2,0:T(8,128)(2,1)} async-done(((bf16[4,768,1536]{1,2,0:T(8,128)(2,1)}), bf16[4,768,96]{1,2,0:T(8,128)(2,1)}) %reduce-scatter.23.cloned.1.call-update) | async-done | bytes 589840 | tf_op jit(solution)/shard_map/reduce_scatter | solution.py:318
  958.5 113.6 %reduce-scatter.19.cloned.1.call-done = bf16[4,96,768]{2,1,0:T(8,128)(2,1)} async-done(((bf16[4,1536,768]{2,1,0:T(8,128)(2,1)}), bf16[4,96,768]{2,1,0:T(8,128)(2,1)}) %reduce-scatter.19.cloned.1.call-update) | async-done | bytes 589840 | tf_op jit(solution)/shard_map/reduce_scatter | solution.py:312
  1074.3 112.9 %reduce-scatter.21.cloned.1.call-done = bf16[4,96,768]{2,1,0:T(8,128)(2,1)} async-done(((bf16[4,1536,768]{2,1,0:T(8,128)(2,1)}), bf16[4,96,768]{2,1,0:T(8,128)(2,1)}) %reduce-scatter.21.cloned.1.call-update) | async-done | bytes 589840 | tf_op jit(solution)/shard_map/reduce_scatter | solution.py:315
  (385 shorter events, 179.1 us)
Async XLA Ops:
  7.2 66.6 %copy-start.5 = (bf16[256,1536]{1,0:T(8,128)(2,1)S(1)}, bf16[256,1536]{1,0:T(8,128)(2,1)}, u32[]{:S(2)}) copy-start(bf16[256,1536]{1,0:T(8,128)(2,1)} %param.14) | copy-start | bytes 2359300
  7.2 66.9 %copy-start.67 = (bf16[96,256]{1,0:T(8,128)(2,1)S(1)}, bf16[96,256]{1,0:T(8,128)(2,1)}, u32[]{:S(2)}) copy-start(bf16[96,256]{1,0:T(8,128)(2,1)} %param.17) | copy-start | bytes 147460
  7.2 136.0 %all-gather.4.cloned.1.call-start = ((), (), s32[]{:S(2)}) async-start(), calls=%async_computation.16 | async-start | bytes 5013504 | tf_op jit(solution)/shard_map/all_gather | solution.py:69
  7.9 144.1 %all-gather.6.cloned.1.call-start = ((), (), s32[]{:S(2)}) async-start(), calls=%async_computation.17 | async-start | bytes 5013504 | tf_op jit(solution)/shard_map/all_gather | solution.py:72
  50.7 92.5 %copy-start.63 = (f32[1536]{0:T(1024)}, f32[1536]{0:T(1024)S(1)}, u32[]{:S(2)}) copy-start(f32[1536]{0:T(1024)S(1)} %convert_element_type.305) | copy-start | bytes 18436
  68.5 88.4 %copy-start.65 = (bf16[1536,8]{0,1:T(8,128)(2,1)}, bf16[1536,8]{0,1:T(8,128)(2,1)S(1)}, u32[]{:S(2)}) copy-start(bf16[1536,8]{0,1:T(8,128)(2,1)S(1)} %reshape.491) | copy-start | bytes 73732
  70.0 29.3 %copy-start.81 = (s32[8,5]{0,1:T(8,128)}, s32[8,5]{0,1:T(8,128)S(1)}, u32[]{:S(2)}) copy-start(s32[8,5]{0,1:T(8,128)S(1)} %reduce-window.15) | copy-start | bytes 484
  71.4 27.9 %copy-start.80 = (s32[8,5]{0,1:T(8,128)}, s32[8,5]{0,1:T(8,128)S(1)}, u32[]{:S(2)}) copy-start(s32[8,5]{0,1:T(8,128)S(1)} %reduce-window.19) | copy-start | bytes 484
  72.2 27.2 %copy-start.55 = (f32[256,64]{0,1:T(8,128)}, f32[256,64]{0,1:T(8,128)S(1)}, u32[]{:S(2)}) copy-start(f32[256,64]{0,1:T(8,128)S(1)} %get-tuple-element.65) | copy-start | bytes 196612
  72.2 75.4 %copy-start.49 = (f32[256,64]{0,1:T(8,128)}, f32[256,64]{0,1:T(8,128)S(1)}, u32[]{:S(2)}) copy-start(f32[256,64]{0,1:T(8,128)S(1)} %get-tuple-element.67) | copy-start | bytes 196612
  72.3 49.2 %copy-start.43 = (f32[256,64]{1,0:T(8,128)}, f32[256,64]{1,0:T(8,128)S(1)}, u32[]{:S(2)}) copy-start(f32[256,64]{1,0:T(8,128)S(1)} %copy.227) | copy-start | bytes 196612
  74.0 25.7 %copy-start.76 = (f32[256]{0:T(256)}, f32[256]{0:T(256)S(1)}, u32[]{:S(2)}) copy-start(f32[256]{0:T(256)S(1)} %fusion.91) | copy-start | bytes 3076
  74.0 25.6 %copy-start.20 = (bf16[256,1536]{1,0:T(8,128)(2,1)S(1)}, bf16[256,1536]{1,0:T(8,128)(2,1)}, u32[]{:S(2)}) copy-start(bf16[256,1536]{1,0:T(8,128)(2,1)} %param.27) | copy-start | bytes 2359300
  74.1 69.1 %copy-start.70 = (f32[256]{0:T(256)}, f32[256]{0:T(256)S(1)}, u32[]{:S(2)}) copy-start(f32[256]{0:T(256)S(1)} %fusion.125) | copy-start | bytes 3076
  109.9 11.5 copy-start.60
  109.9 11.6 copy-start.68
  121.6 27.0 %copy-start.45 = (bf16[256,2,64]{2,0,1:T(8,128)(2,1)}, bf16[256,2,64]{2,0,1:T(8,128)(2,1)S(1)}, u32[]{:S(2)}) copy-start(bf16[256,2,64]{2,0,1:T(8,128)(2,1)S(1)} %get-tuple-element.47) | copy-start | bytes 196612
  121.6 27.0 %copy-start.47 = (bf16[256,2,64]{2,0,1:T(8,128)(2,1)}, bf16[256,2,64]{2,0,1:T(8,128)(2,1)S(1)}, u32[]{:S(2)}) copy-start(bf16[256,2,64]{2,0,1:T(8,128)(2,1)S(1)} %get-tuple-element.48) | copy-start | bytes 196612
  157.4 46.2 %copy-start.16 = (bf16[256,1536]{1,0:T(8,128)(2,1)}, bf16[256,1536]{1,0:T(8,128)(2,1)S(1)}, u32[]{:S(2)}) copy-start(bf16[256,1536]{1,0:T(8,128)(2,1)S(1)} %multiply_convert_fusion.2) | copy-start | bytes 2359300
  161.6 33.5 %all-to-all-start = ((bf16[2,4,96,1536]{3,2,1,0:T(8,128)(2,1)}), bf16[2,4,96,1536]{3,2,1,0:T(8,128)(2,1)}, u32[]{:S(2)}, u32[]{:S(2)}) async-start(bf16[2,4,96,1536]{3,2,1,0:T(8,128)(2,1)} %bitcast.295), calls=%async_computation | async-start | bytes 4718592 | tf_op jit(solution)/shard_map/all_to_all | solution.py:148
  195.1 32.8 %all-to-all-start.4 = ((bf16[2,4,96,1536]{3,2,1,0:T(8,128)(2,1)}), bf16[2,4,96,1536]{3,2,1,0:T(8,128)(2,1)}, u32[]{:S(2)}, u32[]{:S(2)}) async-start(bf16[2,4,96,1536]{3,2,1,0:T(8,128)(2,1)} %bitcast.297), calls=%async_computation.4 | async-start | bytes 4718592 | tf_op jit(solution)/shard_map/all_to_all | solution.py:197
  227.9 30.5 %all-to-all-start.2 = ((bf16[2,4,96,1536]{3,2,1,0:T(8,128)(2,1)}), bf16[2,4,96,1536]{3,2,1,0:T(8,128)(2,1)S(1)}, u32[]{:S(2)}, u32[]{:S(2)}) async-start(bf16[2,4,96,1536]{3,2,1,0:T(8,128)(2,1)} %bitcast.298), calls=%async_computation.2 | async-start | bytes 4718592 | tf_op jit(solution)/shard_map/all_to_all | solution.py:148
  258.4 13.0 %copy-start.2 = (bf16[2,4,96,1536]{3,2,1,0:T(8,128)(2,1)}, bf16[2,4,96,1536]{3,2,1,0:T(8,128)(2,1)S(1)}, u32[]{:S(2)}) copy-start(bf16[2,4,96,1536]{3,2,1,0:T(8,128)(2,1)S(1)} %all-to-all-done.2) | copy-start | bytes 7077892
  258.5 13.0 %slice-start.3 = ((s8[9437184]{0:T(1024)(128)(4,1)}), s8[1048576]{0:T(1024)(128)(4,1)S(1)}, s32[]{:S(2)}) async-start(s8[9437184]{0:T(1024)(128)(4,1)} %bitcast.286), calls=%async_computation.31 | async-start | bytes 2097152
  258.5 31.1 %all-to-all-start.6 = ((bf16[2,4,96,1536]{3,2,1,0:T(8,128)(2,1)}), bf16[2,4,96,1536]{3,2,1,0:T(8,128)(2,1)}, u32[]{:S(2)}, u32[]{:S(2)}) async-start(bf16[2,4,96,1536]{3,2,1,0:T(8,128)(2,1)} %bitcast.296), calls=%async_computation.6 | async-start | bytes 4718592 | tf_op jit(solution)/shard_map/all_to_all | solution.py:197
  289.5 30.4 %all-to-all-start.1 = ((bf16[2,4,96,1536]{3,2,1,0:T(8,128)(2,1)}), bf16[2,4,96,1536]{3,2,1,0:T(8,128)(2,1)S(1)}, u32[]{:S(2)}, u32[]{:S(2)}) async-start(bf16[2,4,96,1536]{3,2,1,0:T(8,128)(2,1)} %copy.241), calls=%async_computation.1 | async-start | bytes 4718592 | tf_op jit(solution)/shard_map/all_to_all | solution.py:157
  293.6 15.2 %slice-start = ((s8[9437184]{0:T(1024)(128)(4,1)}), s8[4194304]{0:T(1024)(128)(4,1)S(1)}, s32[]{:S(2)}) async-start(s8[9437184]{0:T(1024)(128)(4,1)} %bitcast.284), calls=%async_computation.28 | async-start | bytes 8388608
  293.6 15.2 %slice-start.1 = ((s8[9437184]{0:T(1024)(128)(4,1)}), s8[1048576]{0:T(1024)(128)(4,1)S(1)}, s32[]{:S(2)}) async-start(s8[9437184]{0:T(1024)(128)(4,1)} %bitcast.284), calls=%async_computation.29 | async-start | bytes 2097152
  308.7 16.1 %copy-start.18 = (bf16[2,4,96,768]{3,2,0,1:T(8,128)(2,1)}, bf16[2,4,96,768]{3,2,0,1:T(8,128)(2,1)S(1)}, u32[]{:S(2)}) copy-start(bf16[2,4,96,768]{3,2,0,1:T(8,128)(2,1)S(1)} %get-tuple-element.36) | copy-start | bytes 3538948
  319.9 29.9 %all-to-all-start.3 = ((bf16[2,4,96,1536]{3,2,1,0:T(8,128)(2,1)}), bf16[2,4,96,1536]{3,2,1,0:T(8,128)(2,1)}, u32[]{:S(2)}, u32[]{:S(2)}) async-start(bf16[2,4,96,1536]{3,2,1,0:T(8,128)(2,1)} %copy.248), calls=%async_computation.3 | async-start | bytes 4718592 | tf_op jit(solution)/shard_map/all_to_all | solution.py:157
  324.9 13.2 %slice-start.9 = ((s8[9437184]{0:T(1024)(128)(4,1)}), s8[4194304]{0:T(1024)(128)(4,1)S(1)}, s32[]{:S(2)}) async-start(s8[9437184]{0:T(1024)(128)(4,1)} %bitcast.290), calls=%async_computation.37 | async-start | bytes 8388608
  324.9 13.2 %slice-start.10 = ((s8[9437184]{0:T(1024)(128)(4,1)}), s8[4194304]{0:T(1024)(128)(4,1)S(1)}, s32[]{:S(2)}) async-start(s8[9437184]{0:T(1024)(128)(4,1)} %bitcast.290), calls=%async_computation.38 | async-start | bytes 8388608
  324.9 13.1 %slice-start.11 = ((s8[9437184]{0:T(1024)(128)(4,1)}), s8[1048576]{0:T(1024)(128)(4,1)S(1)}, s32[]{:S(2)}) async-start(s8[9437184]{0:T(1024)(128)(4,1)} %bitcast.290), calls=%async_computation.39 | async-start | bytes 2097152
  343.5 11.7 copy-start.30
  349.8 39.9 %all-to-all-start.7 = ((bf16[2,4,96,1536]{3,2,1,0:T(8,128)(2,1)}), bf16[2,4,96,1536]{3,2,1,0:T(8,128)(2,1)}, u32[]{:S(2)}, u32[]{:S(2)}) async-start(bf16[2,4,96,1536]{3,2,1,0:T(8,128)(2,1)} %copy.254), calls=%async_computation.7 | async-start | bytes 4718592 | tf_op jit(solution)/shard_map/all_to_all | solution.py:221
  389.7 27.8 %all-to-all-start.5 = ((bf16[2,4,96,1536]{3,2,1,0:T(8,128)(2,1)}), bf16[2,4,96,1536]{3,2,1,0:T(8,128)(2,1)S(1)}, u32[]{:S(2)}, u32[]{:S(2)}) async-start(bf16[2,4,96,1536]{3,2,1,0:T(8,128)(2,1)} %copy.251), calls=%async_computation.5 | async-start | bytes 4718592 | tf_op jit(solution)/shard_map/all_to_all | solution.py:221
  393.6 117.4 %reduce-scatter.25.cloned.1.call-start = ((), (), s32[]{:S(2)}) async-start(), calls=%async_computation.25 | async-start | bytes 417792
  452.9 113.7 %reduce-scatter.15.cloned.1.call-start = ((), (), s32[]{:S(2)}) async-start(), calls=%async_computation.20 | async-start | bytes 835584 | tf_op jit(solution)/shard_map/reduce_scatter | solution.py:289
  455.5 170.6 %reduce-scatter.13.cloned.1.call-start = ((), (), s32[]{:S(2)}) async-start(), calls=%async_computation.19 | async-start | bytes 835584 | tf_op jit(solution)/shard_map/reduce_scatter | solution.py:286
  462.3 242.7 %reduce-scatter.17.cloned.1.call-start = ((), (), s32[]{:S(2)}) async-start(), calls=%async_computation.21 | async-start | bytes 5013504 | tf_op jit(solution)/shard_map/reduce_scatter | solution.py:292
  466.3 317.1 %reduce-scatter.11.cloned.1.call-start = ((), (), s32[]{:S(2)}) async-start(), calls=%async_computation.18 | async-start | bytes 5013504 | tf_op jit(solution)/shard_map/reduce_scatter | solution.py:283
  472.2 374.1 %all-reduce.14.cloned.1.call-start = ((), (), s32[]{:S(2)}) async-start(), calls=%async_computation.26 | async-start | bytes 202752 | tf_op jit(solution)/shard_map/psum | solution.py:303
  477.9 148.3 %copy-start.31 = (bf16[2,4,96,768]{3,2,0,1:T(8,128)(2,1)S(1)}, bf16[2,4,96,768]{3,2,0,1:T(8,128)(2,1)}, u32[]{:S(2)}) copy-start(bf16[2,4,96,768]{3,2,0,1:T(8,128)(2,1)} %get-tuple-element.35) | copy-start | bytes 3538948
  626.2 157.5 %copy-start.33 = (bf16[2,4,96,768]{3,2,0,1:T(8,128)(2,1)S(1)}, bf16[2,4,96,768]{3,2,0,1:T(8,128)(2,1)}, u32[]{:S(2)}) copy-start(bf16[2,4,96,768]{3,2,0,1:T(8,128)(2,1)} %copy-done.32) | copy-start | bytes 3538948
  626.2 226.6 %all-reduce.16.cloned.1.call-start = ((), (), s32[]{:S(2)}) async-start(), calls=%async_computation.27 | async-start | bytes 1179648 | tf_op jit(solution)/shard_map/psum | solution.py:304
  783.5 172.9 %reduce-scatter.23.cloned.1.call-start = ((), (), s32[]{:S(2)}) async-start(), calls=%async_computation.24 | async-start | bytes 10027008 | tf_op jit(solution)/shard_map/reduce_scatter | solution.py:318
  797.1 275.0 %reduce-scatter.19.cloned.1.call-start = ((), (), s32[]{:S(2)}) async-start(), calls=%async_computation.22 | async-start | bytes 10027008 | tf_op jit(solution)/shard_map/reduce_scatter | solution.py:312
  819.5 367.7 %reduce-scatter.21.cloned.1.call-start = ((), (), s32[]{:S(2)}) async-start(), calls=%async_computation.23 | async-start | bytes 10027008 | tf_op jit(solution)/shard_map/reduce_scatter | solution.py:315
  (69 other events, 232.4 us)
Sparse Core Ops, SparseCore 0:
  10.3 56.5 all-gather.3
  69.2 54.1 all-gather.5
  453.0 54.1 reduce-scatter.24
  511.0 55.5 reduce-scatter.14
  570.6 55.5 reduce-scatter.12
  630.3 74.5 reduce-scatter.16
  708.8 74.5 reduce-scatter.10
  787.3 20.6 all-reduce.13
  810.5 30.4 all-reduce.15
  845.0 111.3 reduce-scatter.22
  961.0 111.0 reduce-scatter.18
  1076.1 111.0 reduce-scatter.20
where the time goes:
time: 1210 us; the launch traced here: 1200 us
  waiting for transfers between devices  655 us (54%)
  matrix products  190 us (16%)
  blocking collectives  128 us (11%)
  local copies, waits for them, and re-layouts  107 us (9%)
  other arithmetic  60.2 us (5%)
  starting transfers between devices  38.5 us (3%)
  between operations  18 us (1%)
    reduce_scatter x1, waiting for transfers between devices, local(): lax.psum_scatter(gate_acc.astype(jnp.bfloat16), 'dp', scatter_dimension=1...  114 us
    reduce_scatter x1, waiting for transfers between devices, local(): lax.psum_scatter(up_acc.astype(jnp.bfloat16), 'dp', scatter_dimension=1,...  113 us
    reduce_scatter x1, waiting for transfers between devices, local(): lax.psum_scatter(down_acc.astype(jnp.bfloat16), 'dp', scatter_dimension=2...  99.9 us
    reduce_scatter x1, waiting for transfers between devices, local(): lax.psum_scatter(query_acc.astype(jnp.bfloat16), 'dp', scatter_dimension=...  78.5 us
    reduce_scatter x1, waiting for transfers between devices, local(): lax.psum_scatter(output_acc.astype(jnp.bfloat16), 'dp', scatter_dimension...  67.4 us
    unnamed x2, blocking collectives  66.2 us
    reduce_scatter x1, waiting for transfers between devices, local(): lax.psum_scatter(key_acc.astype(jnp.bfloat16), 'dp', scatter_dimension=0,...  59.5 us
    reduce_scatter x1, waiting for transfers between devices, local(): lax.psum_scatter(value_acc.astype(jnp.bfloat16), 'dp', scatter_dimension=...  54.2 us
  transfers between devices with their start and end apart: 20, of which 13 were waited for; matrix products, arithmetic and copies ran while one was open for 25% of the time, Pallas kernels for 0%

commit v1 on v0

v1 whole, which is shorter than its diff:
```python
import math

import jax
import jax.numpy as jnp
from jax import lax
from jax.sharding import PartitionSpec as P

HQ = 12
HK = 2
HD = 128
MICRO = 2
PLANE = ("y", "c", "x")
GROUP = ("z", "y", "c")


def rms_scale(values, gain_vec):
    inverse = lax.rsqrt(jnp.mean(values * values, axis=-1, keepdims=True) + 1e-06)
    return values * inverse * gain_vec


def angles(length, head_size):
    positions = jnp.arange(length).astype(jnp.float32)
    freq_rates = jnp.exp(
        -(2.0 * jnp.arange(head_size // 2).astype(jnp.float32) / head_size) * math.log(1000000.0)
    )
    angle_tab = positions[:, None] * freq_rates[None, :]
    return (jnp.cos(angle_tab)[:, None, :], jnp.sin(angle_tab)[:, None, :])


def rotary(values, cosine_tab, sine_tab):
    half_dim = values.shape[-1] // 2
    first_half = values[..., :half_dim]
    second_half = values[..., half_dim:]
    return jnp.concatenate(
        [
            first_half * cosine_tab - second_half * sine_tab,
            second_half * cosine_tab + first_half * sine_tab,
        ],
        axis=-1,
    )


def expert_act(gate_pre, up_pre):
    return jax.nn.gelu(gate_pre, approximate=True) * up_pre


def left_product(left_mat, right_mat):
    return lax.dot_general(
        left_mat, right_mat, (((0,), (0,)), ((), ())), preferred_element_type=jnp.float32
    )


def gather(block, axes):
    return lax.all_gather(block, axes, axis=0, tiled=True)


def exchange(block, axes):
    return lax.all_to_all(block, axes, split_axis=0, concat_axis=0, tiled=True)


def scatter_sum(block, axes):
    return lax.psum_scatter(block, axes, scatter_dimension=0, tiled=True)


def by_owner(cols, parts):
    rows, total = cols.shape
    return jnp.moveaxis(cols.reshape(rows, parts, total // parts), 1, 0).reshape(
        parts * rows, total // parts
    )


def local(
    tokens,
    norm1_gain,
    w_query,
    w_key,
    w_value,
    w_out,
    norm2_gain,
    w_router,
    w_gate,
    w_up,
    w_down,
    expert_ids,
    prefix_len,
    out_grad,
):
    bf16, f32 = jnp.bfloat16, jnp.float32
    length, model_width = tokens.shape
    shard_rows = w_query.shape[0]
    local_count, _, hidden_width = w_gate.shape
    owners = lax.axis_size("x")
    depth = lax.axis_size("z")
    plane = lax.axis_size(PLANE)
    experts_all = w_router.shape[1]
    top_count = expert_ids.shape[1]
    block_rows = length // MICRO
    capacity = 3 * block_rows * top_count // (2 * experts_all)
    plane_rows = plane * length
    blocks = plane_rows // block_rows
    group_size = HQ // HK
    score_scale = HD ** (-0.5)
    q_cols, kv_cols = w_query.shape[1], w_key.shape[1]
    own_local = lax.axis_index(("y", "c"))
    own_expert = lax.axis_index("x") * local_count + own_local
    own_place = lax.axis_index(PLANE)

    narrow = jnp.concatenate([w_router, norm1_gain[:, None], norm2_gain[:, None]], axis=1)
    narrow = jnp.pad(narrow, ((0, 0), (0, -narrow.shape[1] % 128)))
    packed = gather(jnp.concatenate([w_query, w_key, w_value, narrow], axis=1), GROUP)
    qkv_cols = q_cols + 2 * kv_cols
    qkv_w = packed[:, :qkv_cols]
    router_w = packed[:, qkv_cols : qkv_cols + experts_all]
    gains = packed[:, qkv_cols + experts_all : qkv_cols + experts_all + 2].T.astype(f32)
    gain_one, gain_two = gains[0], gains[1]
    output_w = gather(w_out, GROUP)

    ids_all = gather(expert_ids, PLANE)
    cot_all = gather(out_grad, PLANE)
    chosen_mask = jnp.any(
        ids_all[:, :, None] == jnp.arange(experts_all, dtype=jnp.int32)[None, None, :], axis=1
    )
    own_mask = jnp.any(ids_all == own_expert, axis=1).reshape(blocks, block_rows)
    place = jnp.cumsum(own_mask.astype(jnp.int32), axis=1) - 1
    dispatch = (
        own_mask[:, None, :]
        & (place[:, None, :] == jnp.arange(capacity, dtype=jnp.int32)[None, :, None])
    ).astype(bf16)

    cosine_tab, sine_tab = angles(length, HD)
    inputs_f = tokens.astype(f32)
    first_in = rms_scale(inputs_f, gain_one).astype(bf16)
    qkv = jnp.dot(first_in, qkv_w, preferred_element_type=f32)
    queries = (
        rotary(qkv[:, :q_cols].reshape(length, HQ, HD), cosine_tab, sine_tab)
        .astype(bf16)
        .reshape(length, HK, group_size, HD)
    )
    keys_rot = rotary(
        qkv[:, q_cols : q_cols + kv_cols].reshape(length, HK, HD), cosine_tab, sine_tab
    ).astype(bf16)
    values_b = qkv[:, q_cols + kv_cols :].astype(bf16).reshape(length, HK, HD)
    positions = jnp.arange(length)
    allowed = (positions[None, :] <= positions[:, None]) | (positions[None, :] < prefix_len[0])

    def masked_scores():
        scores = jnp.einsum("ihrd,jhd->hrij", queries, keys_rot, preferred_element_type=f32)
        return jnp.where(allowed, scores * score_scale, -1e30)

    masked = masked_scores()
    row_peak = jnp.max(masked, axis=-1, keepdims=True)
    log_total = row_peak + jnp.log(jnp.sum(jnp.exp(masked - row_peak), axis=-1, keepdims=True))
    prob_bf = jnp.exp(masked - log_total).astype(bf16)
    attended = jnp.einsum("hrij,jhd->ihrd", prob_bf, values_b, preferred_element_type=f32)
    attended = attended.reshape(length, HQ * HD).astype(bf16)
    resid = inputs_f + jnp.dot(attended, output_w, preferred_element_type=f32)
    second_in = rms_scale(resid, gain_two).astype(bf16)

    second_all = gather(second_in, PLANE)
    logits = jnp.dot(second_all, router_w, preferred_element_type=f32)
    gates_all = jax.nn.softmax(jnp.where(chosen_mask, logits, -jnp.inf), axis=-1)
    own_gates = lax.dynamic_index_in_dim(gates_all, own_expert, 1, keepdims=False)
    own_gates = own_gates.reshape(blocks, block_rows)
    gate_rows = jnp.einsum(
        "bct,bt->bc", dispatch.astype(f32), own_gates, precision=lax.Precision.HIGHEST
    )[:, :, None]
    gate_w = lax.dynamic_index_in_dim(w_gate, own_local, 0, keepdims=False)
    up_w = lax.dynamic_index_in_dim(w_up, own_local, 0, keepdims=False)
    down_w = lax.dynamic_index_in_dim(w_down, own_local, 0, keepdims=False)

    def to_rows(array):
        return jnp.einsum(
            "bct,btd->bcd",
            dispatch,
            array.reshape(blocks, block_rows, model_width),
            preferred_element_type=f32,
        ).astype(bf16)

    def to_tokens(rows):
        return (
            jnp.einsum("bct,bcd->btd", dispatch, rows.astype(bf16), preferred_element_type=f32)
            .astype(bf16)
            .reshape(plane_rows, model_width)
        )

    rows_in = to_rows(second_all)
    rows_cot = to_rows(cot_all)
    gate_pre = jnp.einsum("bcd,df->bcf", rows_in, gate_w, preferred_element_type=f32)
    up_pre = jnp.einsum("bcd,df->bcf", rows_in, up_w, preferred_element_type=f32)
    hidden, act_pull = jax.vjp(expert_act, gate_pre, up_pre)
    gated = (gate_rows * hidden).astype(bf16)
    down_part = jnp.einsum("bcd,bcf->df", rows_cot, gated, preferred_element_type=f32)
    down_sum = scatter_sum(down_part.astype(bf16), "z")
    cot_hidden = jnp.einsum("bcd,fd->bcf", rows_cot, down_w, preferred_element_type=f32)
    gate_signal_rows = jnp.sum(hidden * cot_hidden, axis=-1)
    gate_pgrad, up_pgrad = act_pull(gate_rows * cot_hidden)
    gate_pgrad = gate_pgrad.astype(bf16)
    up_pgrad = up_pgrad.astype(bf16)
    gate_part = jnp.einsum("bcd,bcf->df", rows_in, gate_pgrad, preferred_element_type=f32)
    gate_sum = scatter_sum(gate_part.astype(bf16), "z")
    up_part = jnp.einsum("bcd,bcf->df", rows_in, up_pgrad, preferred_element_type=f32)
    up_sum = scatter_sum(up_part.astype(bf16), "z")
    rows_grad = jnp.einsum("bcf,df->bcd", gate_pgrad, gate_w, preferred_element_type=f32)
    rows_grad = rows_grad + jnp.einsum("bcf,df->bcd", up_pgrad, up_w, preferred_element_type=f32)
    second_back = scatter_sum(to_tokens(rows_grad), PLANE).astype(f32)
    gate_signal = jnp.einsum(
        "bct,bc->bt", dispatch.astype(f32), gate_signal_rows, precision=lax.Precision.HIGHEST
    )
    gate_signal = exchange(gate_signal.reshape(plane, length), PLANE)
    gate_signal = jnp.transpose(
        gate_signal.reshape(local_count, owners, length), (2, 1, 0)
    ).reshape(length, experts_all)
    expert_rows = jnp.einsum("bcf,fd->bcd", gated, down_w, preferred_element_type=f32)
    mixture = scatter_sum(to_tokens(expert_rows), PLANE).astype(f32)
    block_out = (resid + mixture).astype(bf16)

    cotangent = out_grad.astype(f32)
    gate_probs = lax.dynamic_slice_in_dim(gates_all, own_place * length, length, 0)
    logit_grad = (
        gate_probs
        * (gate_signal - jnp.sum(gate_probs * gate_signal, axis=-1, keepdims=True))
    ).astype(bf16)
    router_acc = left_product(second_in, logit_grad)
    second_grad = second_back + jnp.dot(logit_grad, router_w.T, preferred_element_type=f32)
    _, norm_two_pull = jax.vjp(rms_scale, resid, gain_two)
    resid_norm_grad, gain_two_grad = norm_two_pull(second_grad)
    resid_grad = cotangent + resid_norm_grad
    branch_grad = resid_grad.astype(bf16)

    attended_all = gather(attended, PLANE)
    branch_cols = exchange(by_owner(branch_grad, plane), PLANE)
    output_part = left_product(attended_all, branch_cols)
    attended_grad = jnp.dot(branch_grad, output_w.T, preferred_element_type=f32).astype(bf16)
    attended_grad = attended_grad.reshape(length, HK, group_size, HD)
    masked = masked_scores()
    prob_full = jnp.exp(masked - log_total)
    prob_bf = prob_full.astype(bf16)
    prob_grad = jnp.einsum("ihrd,jhd->hrij", attended_grad, values_b, preferred_element_type=f32)
    row_inner = jnp.sum(prob_full * prob_grad, axis=-1, keepdims=True)
    score_grad = (prob_full * (prob_grad - row_inner)).astype(bf16)
    query_rot_grad = (
        jnp.einsum("hrij,jhd->ihrd", score_grad, keys_rot, preferred_element_type=f32)
        * score_scale
    )
    query_back = rotary(query_rot_grad.reshape(length, HQ, HD), cosine_tab, -sine_tab)
    query_back = query_back.astype(bf16).reshape(length, HQ * HD)
    key_rot_grad = (
        jnp.einsum("hrij,ihrd->jhd", score_grad, queries, preferred_element_type=f32)
        * score_scale
    )
    key_back = rotary(key_rot_grad, cosine_tab, -sine_tab).astype(bf16).reshape(length, HK * HD)
    value_back = jnp.einsum("hrij,ihrd->jhd", prob_bf, attended_grad, preferred_element_type=f32)
    value_back = value_back.astype(bf16).reshape(length, HK * HD)
    qkv_back = jnp.concatenate([query_back, key_back, value_back], axis=1)
    first_all = gather(first_in, PLANE)
    qkv_part = left_product(first_all, exchange(by_owner(qkv_back, plane), PLANE))
    first_grad = lax.dot_general(
        qkv_back, qkv_w, (((1,), (1,)), ((), ())), preferred_element_type=f32
    )
    _, norm_one_pull = jax.vjp(rms_scale, inputs_f, gain_one)
    input_norm_grad, gain_one_grad = norm_one_pull(first_grad)
    tokens_grad = (resid_grad + input_norm_grad).astype(bf16)

    narrow_part = jnp.concatenate(
        [router_acc, gain_one_grad[:, None], gain_two_grad[:, None]], axis=1
    ).astype(bf16)
    narrow_cols = narrow_part.shape[1]
    narrow_sum = lax.psum(scatter_sum(narrow_part, GROUP), "x").astype(f32)
    dense_part = jnp.concatenate([qkv_part, output_part], axis=1).astype(bf16)
    dense_sum = scatter_sum(dense_part, "z")
    dense_cols = dense_sum.shape[1]
    dense_sum = gather(dense_sum, PLANE).reshape(plane, local_count, shard_rows, dense_cols)
    dense_sum = lax.dynamic_index_in_dim(dense_sum, own_local, 1, keepdims=False).astype(f32)
    dense_sum = jnp.moveaxis(dense_sum, 0, 1)
    qkv_width = qkv_cols // plane
    qkv_sum = dense_sum[:, :, :qkv_width].reshape(shard_rows, qkv_cols)
    output_sum = dense_sum[:, :, qkv_width:].reshape(shard_rows, model_width)

    def placed(total):
        total = exchange(total, ("y", "c"))
        return total.reshape(local_count, shard_rows, hidden_width).astype(f32)

    return (
        block_out,
        tokens_grad,
        narrow_sum[:, experts_all],
        qkv_sum[:, :q_cols],
        qkv_sum[:, q_cols : q_cols + kv_cols],
        qkv_sum[:, q_cols + kv_cols :],
        output_sum,
        narrow_sum[:, experts_all + 1],
        narrow_sum[:, :experts_all],
        placed(gate_sum),
        placed(up_sum),
        jnp.swapaxes(placed(down_sum), 1, 2),
    )


def solution(mesh):
    groups, owners = mesh.shape["dp"], mesh.shape["expert"]
    grid = jax.sharding.Mesh(
        mesh.devices.reshape(groups // 4, 2, 2, owners), ("z", "y", "c", "x")
    )
    rows = P(("z", "y", "c", "x"), None)
    shard, shard_rows = P(GROUP), P(GROUP, None)
    expert = P("x", None, None)
    return jax.shard_map(
        local,
        mesh=grid,
        in_specs=(
            rows,
            shard,
            shard_rows,
            shard_rows,
            shard_rows,
            shard_rows,
            shard,
            shard_rows,
            expert,
            expert,
            expert,
            rows,
            P(("z", "y", "c", "x")),
            rows,
        ),
        out_specs=(
            rows,
            rows,
            shard,
            shard_rows,
            shard_rows,
            shard_rows,
            shard_rows,
            shard,
            shard_rows,
            P("x", GROUP, None),
            P("x", GROUP, None),
            P("x", None, GROUP),
        ),
        check_vma=False,
    )
```

time: 1210 us -> 805 us (0.67)
  waiting for transfers between devices: 655 us -> 529 us
  blocking collectives: 128 us -> 18.2 us
  local copies, waits for them, and re-layouts: 107 us -> 38.7 us
  matrix products: 190 us -> 138 us
  other arithmetic: 60.2 us -> 31.6 us
  starting transfers between devices: 38.5 us -> 24.1 us
    reduce_scatter x7 -> x6, waiting for transfers between devices: 586 us -> 219 us  [scatter_sum(): return lax.psum_scatter(block, axes, scatter_dimension=0, tiled=True)]
    all_gather x2 -> x7, waiting for transfers between devices: 0.04 us -> 228 us  [gather(): return lax.all_gather(block, axes, axis=0, tiled=True)]
    unnamed x2 -> x0, blocking collectives: 66.2 us -> none
    unnamed x13 -> x15, waiting for transfers between devices: 1.54 us -> 58.3 us
    dot_general x30 -> x21, matrix products: 173 us -> 123 us  [the longest x2 22.6 us: to_tokens(): jnp.einsum('bct,bcd->btd', dispatch, rows.astype(bf16), preferred_element...]
    all_gather x3 -> x1, blocking collectives: 61.6 us -> 13.3 us  [gather(): return lax.all_gather(block, axes, axis=0, tiled=True)]
    all_to_all x8 -> x6, waiting for transfers between devices: 66.9 us -> 24 us  [exchange(): return lax.all_to_all(block, axes, split_axis=0, concat_axis=0, tiled=True)]
    gather x8 -> x0, local copies, waits for them, and re-layouts: 37.5 us -> none  [the longest x2 12.9 us: local(): back_grad[slot_ids].reshape(block_rows, top_count, model_width)]
  transfers between devices with their start and end apart: 20 -> 20, of which waited for: 13 -> 16; matrix products, arithmetic and copies ran while one was open for 25% -> 18% of each run, Pallas kernels for 0% -> 0%
where the time goes in v1:
time: 805 us; the launch traced here: 796 us
  waiting for transfers between devices  529 us (66%)
  matrix products  138 us (17%)
  local copies, waits for them, and re-layouts  38.7 us (5%)
  other arithmetic  31.6 us (4%)
  starting transfers between devices  24.1 us (3%)
  blocking collectives  18.2 us (2%)
  between operations  15.9 us (2%)
    all_gather x7, waiting for transfers between devices, gather(): return lax.all_gather(block, axes, axis=0, tiled=True)  228 us
    reduce_scatter x6, waiting for transfers between devices, scatter_sum(): return lax.psum_scatter(block, axes, scatter_dimension=0, tiled=True)  219 us
    unnamed x15, waiting for transfers between devices  58.3 us
    all_to_all x6, waiting for transfers between devices, exchange(): return lax.all_to_all(block, axes, split_axis=0, concat_axis=0, tiled=True)  24 us
    all_to_all x6, starting transfers between devices, exchange(): return lax.all_to_all(block, axes, split_axis=0, concat_axis=0, tiled=True)  23.1 us
    dot_general x2, matrix products, to_tokens(): jnp.einsum('bct,bcd->btd', dispatch, rows.astype(bf16), preferred_element...  22.6 us
  transfers between devices with their start and end apart: 20, of which 16 were waited for; matrix products, arithmetic and copies ran while one was open for 18% of the time, Pallas kernels for 0%

profile of v1, /device:TPU:0, one launch (start us, length us, event | category | flops | bytes accessed | tf_op | source)
XLA Modules:
  0.0 796.0 jit_solution(1645215317779685473)
XLA Ops:
  15.7 62.1 %all-gather.8.cloned.1.call-done = bf16[1536,2176]{1,0:T(8,128)(2,1)} async-done(((bf16[96,2176]{1,0:T(8,128)(2,1)}), bf16[1536,2176]{1,0:T(8,128)(2,1)}) %all-gather.8.cloned.1.call-update) | async-done | bytes 6684688 | tf_op jit(solution)/shard_map/all_gather | solution.py:54
  80.6 4.6 fusion.2
  89.7 2.4 fusion.106
  94.2 37.7 %all-gather.10.cloned.1.call-done = bf16[1536,1536]{1,0:T(8,128)(2,1)} async-done(((bf16[96,1536]{1,0:T(8,128)(2,1)}), bf16[1536,1536]{1,0:T(8,128)(2,1)}) %all-gather.10.cloned.1.call-update) | async-done | bytes 4718608 | tf_op jit(solution)/shard_map/all_gather | solution.py:54
  131.8 4.3 multiply_reduce_fusion.3
  138.5 13.3 %all_gather.26 = s32[2048,4]{0,1:T(4,128)S(1)} all-gather(s32[256,4]{0,1:T(4,128)} %param.25), channel_id=1, replica_groups=mesh['z'=4,'y'=2,'c'=2,'x'=2] {'y','c','x'}, dimensions={0}, use_global_device_ids=true | all-gather | bytes 36864 | tf_op jit(solution)/shard_map/all_gather | solution.py:54
  157.9 20.0 %all-gather.14.cloned.1.call-done = bf16[2048,1536]{1,0:T(8,128)(2,1)} async-done(((bf16[256,1536]{1,0:T(8,128)(2,1)}), bf16[2048,1536]{1,0:T(8,128)(2,1)}) %all-gather.14.cloned.1.call-update) | async-done | bytes 6291472 | tf_op jit(solution)/shard_map/all_gather | solution.py:54
  177.9 4.2 convolution_convert_fusion.2
  184.2 7.6 fusion.18
  191.8 33.9 %all-gather.12.cloned.1.call-done = bf16[2048,1536]{1,0:T(8,128)(2,1)} async-done(((bf16[256,1536]{1,0:T(8,128)(2,1)}), bf16[2048,1536]{1,0:T(8,128)(2,1)}) %all-gather.12.cloned.1.call-update) | async-done | bytes 6291472 | tf_op jit(solution)/shard_map/all_gather | solution.py:54
  225.8 4.8 fusion.107
  232.9 6.5 fusion.24
  239.5 11.8 %fusion.10 = (bf16[16,96,768]{2,1,0:T(8,128)(2,1)S(1)}, f32[16,96]{1,0:T(8,128)}, bf16[16,96,768]{2,1,0:T(8,128)(2,1)}, f32[16,96,768]{2,1,0:T(8,128)}) fusion(f32[16,96,768]{2,1,0:T(8,128)S(1)} %fusion.24, f32[16,96,768]{2,1,0:T(8,128)} %fusion.18, f32[16,96]{1,0:T(8,128)S(1)} %bitcast.213, bf16[16,96,1536]{2,1,0:T(8,128)(2,1)S(1)} %convolution_convert_fusion.3, ...), kind=kOutput, calls=%fused_computation.15 | convolution fusion | flops 3656907264 | bytes 25966596 | tf_op jit(solution)/shard_map/bcd,df->bcf/dot_general | solution.py:188
  251.3 6.5 fusion.26
  257.8 11.0 %convolution_convert_fusion = bf16[16,128,1536]{2,1,0:T(8,128)(2,1)} fusion(f32[16,96,1536]{2,1,0:T(8,128)} %fusion.26, bf16[16,96,768]{2,1,0:T(8,128)(2,1)} %get-tuple-element.20, bf16[4,1536,768]{2,1,0:T(8,128)(2,1)} %param.23, s32[]{:T(128)S(6)} %select_n.28, s32[16,128]{1,0:T(8,128)} %broadcast_add_fusion, pred[16,128]{1,0:T(8,128)(4,1)} %bitcast.203), kind=kOutput, calls=%fused_computation.7 | convolution fusion | flops 4236115968 | bytes 20457476 | tf_op jit(solution)/shard_map/bct,bcd->btd/dot_general | solution.py:181
  272.0 3.9 all-to-all-start
  277.6 3.0 all-to-all-done
  287.9 42.8 %reduce-scatter.14.cloned.1.call-done = bf16[256,1536]{1,0:T(8,128)(2,1)} async-done(((bf16[2048,1536]{1,0:T(8,128)(2,1)}), bf16[256,1536]{1,0:T(8,128)(2,1)}) %reduce-scatter.14.cloned.1.call-update) | async-done | bytes 786448 | tf_op jit(solution)/shard_map/reduce_scatter | solution.py:62
  330.8 3.2 multiply_reduce_fusion.1
  336.5 2.3 copy.184
  338.8 5.4 convolution_convert_fusion.5
  344.2 2.3 copy.172
  353.7 4.2 all-to-all-start.2
  362.6 15.8 %all-to-all-done.2 = bf16[8,256,192]{1,2,0:T(8,128)(2,1)} async-done(((bf16[8,256,192]{1,2,0:T(8,128)(2,1)}), bf16[8,256,192]{1,2,0:T(8,128)(2,1)}, u32[]{:S(2)}, u32[]{:S(2)}) %all-to-all-start.2) | async-done | bytes 786464 | tf_op jit(solution)/shard_map/all_to_all | solution.py:58
  378.5 3.6 all-to-all-start.1
  383.5 4.9 all-gather.18.cloned.1.call-done
  388.4 5.0 convolution_convert_fusion.6
  393.4 42.7 %all-gather.16.cloned.1.call-done = bf16[2048,1536]{1,0:T(8,128)(2,1)} async-done(((bf16[256,1536]{1,0:T(8,128)(2,1)}), bf16[2048,1536]{1,0:T(8,128)(2,1)}) %all-gather.16.cloned.1.call-update) | async-done | bytes 6291472 | tf_op jit(solution)/shard_map/all_gather | solution.py:54
  436.1 4.6 convolution_convert_fusion.4
  442.5 8.6 %bitcast_convert_fusion.2 = bf16[1536,768]{1,0:T(8,128)(2,1)} fusion(bf16[16,96,1536]{2,1,0:T(8,128)(2,1)} %copy-done.15, bf16[16,96,768]{2,1,0:T(8,128)(2,1)} %copy-done.59), kind=kOutput, calls=%fused_computation.18 | convolution fusion | flops 3625058304 | bytes 9437184 | tf_op jit(solution)/shard_map/bcd,bcf->df/dot_general | solution.py:199
  451.2 7.6 bitcast_convert_fusion.1
  459.1 10.8 %bitcast_convert_fusion = bf16[1536,768]{1,0:T(8,128)(2,1)} fusion(bf16[16,96,1536]{2,1,0:T(8,128)(2,1)} %copy-done.14, f32[16,96]{1,0:T(8,128)S(1)} %bitcast.214, f32[16,96,768]{2,1,0:T(8,128)} %copy-done.58, f32[16,96,768]{2,1,0:T(8,128)} %get-tuple-element.46), kind=kOutput, calls=%fused_computation.16 | convolution fusion | flops 3638034432 | bytes 16521216 | tf_op jit(solution)/shard_map/bcd,bcf->df/dot_general | solution.py:192
  470.1 11.6 %convolution_convert_fusion.1 = bf16[16,128,1536]{2,1,0:T(8,128)(2,1)} fusion(bf16[4,768,1536]{2,1,0:T(8,128)(2,1)} %param.24, s32[]{:T(128)S(6)} %select_n.28, f32[16,96]{1,0:T(8,128)S(1)} %bitcast.215, s32[16,128]{1,0:T(8,128)S(1)} %copy-done.38, pred[16,128]{1,0:T(8,128)(4,1)S(1)} %bitcast.207, f32[16,96,768]{2,1,0:T(8,128)} %copy-done.58, ...), kind=kOutput, calls=%fused_computation.8 | convolution fusion | flops 4246732800 | bytes 18104324 | tf_op jit(solution)/shard_map/bct,bcd->btd/dot_general | solution.py:181
  483.3 6.4 fusion.42
  491.3 36.0 %reduce-scatter.16.cloned.1.call-done = bf16[384,768]{1,0:T(8,128)(2,1)} async-done(((bf16[1536,768]{1,0:T(8,128)(2,1)}), bf16[384,768]{1,0:T(8,128)(2,1)}) %reduce-scatter.16.cloned.1.call-update) | async-done | bytes 589840 | tf_op jit(solution)/shard_map/reduce_scatter | solution.py:62
  527.3 3.5 all-to-all-start.3
  530.8 46.3 %reduce-scatter.18.cloned.1.call-done = bf16[384,768]{1,0:T(8,128)(2,1)} async-done(((bf16[1536,768]{1,0:T(8,128)(2,1)}), bf16[384,768]{1,0:T(8,128)(2,1)}) %reduce-scatter.18.cloned.1.call-update) | async-done | bytes 589840 | tf_op jit(solution)/shard_map/reduce_scatter | solution.py:62
  577.2 3.5 all-to-all-start.4
  580.7 46.5 %reduce-scatter.20.cloned.1.call-done = bf16[384,768]{1,0:T(8,128)(2,1)} async-done(((bf16[1536,768]{1,0:T(8,128)(2,1)}), bf16[384,768]{1,0:T(8,128)(2,1)}) %reduce-scatter.20.cloned.1.call-update) | async-done | bytes 589840 | tf_op jit(solution)/shard_map/reduce_scatter | solution.py:62
  628.0 4.4 all-to-all-start.5
  634.6 2.2 convert_element_type.252
  636.9 5.2 all-to-all-done.5
  642.0 2.2 convert_bitcast_fusion.1
  644.3 47.7 %reduce-scatter.12.cloned.1.call-done = bf16[256,1536]{1,0:T(8,128)(2,1)} async-done(((bf16[2048,1536]{1,0:T(8,128)(2,1)}), bf16[256,1536]{1,0:T(8,128)(2,1)}) %reduce-scatter.12.cloned.1.call-update) | async-done | bytes 786448 | tf_op jit(solution)/shard_map/reduce_scatter | solution.py:62
  692.0 4.0 fusion.45
  696.1 55.0 %reduce-scatter.22.cloned.1.call-done = bf16[96,10]{1,0:T(8,128)(2,1)} async-done(((bf16[1536,10]{1,0:T(8,128)(2,1)}), bf16[96,10]{1,0:T(8,128)(2,1)}) %reduce-scatter.22.cloned.1.call-update) | async-done | bytes 1936
  751.9 4.9 psum.7
  757.9 26.4 %all-gather.20.cloned.1.call-done = bf16[3072,448]{1,0:T(8,128)(2,1)} async-done(((bf16[384,448]{1,0:T(8,128)(2,1)}), bf16[3072,448]{1,0:T(8,128)(2,1)}) %all-gather.20.cloned.1.call-update) | async-done | bytes 2752528 | tf_op jit(solution)/shard_map/all_gather | solution.py:54
  (243 shorter events, 72.4 us)
Async XLA Ops:
  7.2 7.5 copy-start.7
  7.2 70.6 %all-gather.8.cloned.1.call-start = ((), (), s32[]{:S(2)}) async-start(), calls=%async_computation.13 | async-start | bytes 7102464 | tf_op jit(solution)/shard_map/all_gather | solution.py:54
  10.0 121.9 %all-gather.10.cloned.1.call-start = ((), (), s32[]{:S(2)}) async-start(), calls=%async_computation.14 | async-start | bytes 5013504 | tf_op jit(solution)/shard_map/all_gather | solution.py:54
  10.7 167.2 %all-gather.14.cloned.1.call-start = ((), (), s32[]{:S(2)}) async-start(), calls=%async_computation.17 | async-start | bytes 7077888 | tf_op jit(solution)/shard_map/all_gather | solution.py:54
  11.5 214.3 %all-gather.12.cloned.1.call-start = ((), (), s32[]{:S(2)}) async-start(), calls=%async_computation.15 | async-start | bytes 7077888 | tf_op jit(solution)/shard_map/all_gather | solution.py:54
  12.5 74.2 %copy-start.23 = (f32[256,64]{0,1:T(8,128)}, f32[256,64]{0,1:T(8,128)S(1)}, u32[]{:S(2)}) copy-start(f32[256,64]{0,1:T(8,128)S(1)} %get-tuple-element.39) | copy-start | bytes 196612
  14.9 65.1 %copy-start.47 = (f32[256]{0:T(256)}, f32[256]{0:T(256)S(1)}, u32[]{:S(2)}) copy-start(f32[256]{0:T(256)S(1)} %fusion.46) | copy-start | bytes 3076
  14.9 65.4 %copy-start.53 = (f32[256]{0:T(256)}, f32[256]{0:T(256)S(1)}, u32[]{:S(2)}) copy-start(f32[256]{0:T(256)S(1)} %fusion.95) | copy-start | bytes 3076
  80.3 4.9 copy-start.16
  131.8 5.5 copy-start.31
  138.4 192.3 %reduce-scatter.14.cloned.1.call-start = ((), (), s32[]{:S(2)}) async-start(), calls=%async_computation.18 | async-start | bytes 7077888 | tf_op jit(solution)/shard_map/reduce_scatter | solution.py:62
  225.8 4.9 copy-start.41
  230.7 8.7 %slice-start = ((s8[9437184]{0:T(1024)(128)(4,1)}), s8[1048576]{0:T(1024)(128)(4,1)S(1)}, s32[]{:S(2)}) async-start(s8[9437184]{0:T(1024)(128)(4,1)} %bitcast.211), calls=%async_computation.27 | async-start | bytes 2097152
  232.1 7.3 copy-start.15
  232.9 6.6 copy-start.55
  232.9 6.6 slice-start.1
  232.9 6.6 slice-start.2
  239.4 11.9 %copy-start.58 = (f32[16,96,768]{2,1,0:T(8,128)}, f32[16,96,768]{2,1,0:T(8,128)S(1)}, u32[]{:S(2)}) copy-start(f32[16,96,768]{2,1,0:T(8,128)S(1)} %fusion.24) | copy-start | bytes 14155780
  251.3 6.5 copy-start.59
  268.8 119.5 %all-gather.18.cloned.1.call-start = ((), (), s32[]{:S(2)}) async-start(), calls=%async_computation.20 | async-start | bytes 7077888 | tf_op jit(solution)/shard_map/all_gather | solution.py:54
  269.4 166.7 %all-gather.16.cloned.1.call-start = ((), (), s32[]{:S(2)}) async-start(), calls=%async_computation.19 | async-start | bytes 7077888 | tf_op jit(solution)/shard_map/all_gather | solution.py:54
  272.0 8.6 %all-to-all-start = ((f32[8,1,256]{2,1,0:T(1,128)}), f32[8,1,256]{2,1,0:T(1,128)}, u32[]{:S(2)}, u32[]{:S(2)}) async-start(f32[8,1,256]{2,1,0:T(1,128)} %bitcast.208), calls=%async_computation.2 | async-start | bytes 16384 | tf_op jit(solution)/shard_map/all_to_all | solution.py:58
  351.1 8.9 %copy-start.24 = (f32[256,64]{0,1:T(8,128)S(1)}, f32[256,64]{0,1:T(8,128)}, u32[]{:S(2)}) copy-start(f32[256,64]{0,1:T(8,128)} %copy-done.23) | copy-start | bytes 196612
  351.1 8.9 %copy-start.25 = (f32[256,64]{0,1:T(8,128)S(1)}, f32[256,64]{0,1:T(8,128)}, u32[]{:S(2)}) copy-start(f32[256,64]{0,1:T(8,128)} %get-tuple-element.37) | copy-start | bytes 196612
  353.7 24.7 %all-to-all-start.2 = ((bf16[8,256,192]{1,2,0:T(8,128)(2,1)}), bf16[8,256,192]{1,2,0:T(8,128)(2,1)}, u32[]{:S(2)}, u32[]{:S(2)}) async-start(bf16[8,256,192]{1,2,0:T(8,128)(2,1)} %bitcast.184), calls=%async_computation.4 | async-start | bytes 1572864 | tf_op jit(solution)/shard_map/all_to_all | solution.py:58
  378.5 57.7 %all-to-all-start.1 = ((bf16[8,256,256]{2,1,0:T(8,128)(2,1)}), bf16[8,256,256]{2,1,0:T(8,128)(2,1)S(1)}, u32[]{:S(2)}, u32[]{:S(2)}) async-start(bf16[8,256,256]{2,1,0:T(8,128)(2,1)} %bitcast.52), calls=%async_computation.3 | async-start | bytes 2097152 | tf_op jit(solution)/shard_map/all_to_all | solution.py:58
  382.0 108.8 %reduce-scatter.24.cloned.1.call-start = ((), (), s32[]{:S(2)}) async-start(), calls=%async_computation.26 | async-start | bytes 1966080 | tf_op jit(solution)/shard_map/reduce_scatter | solution.py:62
  442.4 8.7 %copy-start.57 = (bf16[16,96,768]{2,1,0:T(8,128)(2,1)S(1)}, bf16[16,96,768]{2,1,0:T(8,128)(2,1)}, u32[]{:S(2)}) copy-start(bf16[16,96,768]{2,1,0:T(8,128)(2,1)} %get-tuple-element.20) | copy-start | bytes 7077892
  442.4 84.9 %reduce-scatter.16.cloned.1.call-start = ((), (), s32[]{:S(2)}) async-start(), calls=%async_computation.22 | async-start | bytes 2949120 | tf_op jit(solution)/shard_map/reduce_scatter | solution.py:62
  451.1 8.0 %copy-start.56 = (f32[16,1,96]{2,1,0:T(1,128)S(1)}, f32[16,1,96]{2,1,0:T(1,128)}, u32[]{:S(2)}) copy-start(f32[16,1,96]{2,1,0:T(1,128)} %copy-done.55) | copy-start | bytes 18436
  451.1 126.1 %reduce-scatter.18.cloned.1.call-start = ((), (), s32[]{:S(2)}) async-start(), calls=%async_computation.23 | async-start | bytes 2949120 | tf_op jit(solution)/shard_map/reduce_scatter | solution.py:62
  458.8 168.3 %reduce-scatter.20.cloned.1.call-start = ((), (), s32[]{:S(2)}) async-start(), calls=%async_computation.24 | async-start | bytes 2949120 | tf_op jit(solution)/shard_map/reduce_scatter | solution.py:62
  459.1 10.9 %copy-start.38 = (s32[16,128]{1,0:T(8,128)S(1)}, s32[16,128]{1,0:T(8,128)}, u32[]{:S(2)}) copy-start(s32[16,128]{1,0:T(8,128)} %broadcast_add_fusion) | copy-start | bytes 24580
  459.1 10.9 %copy-start.42 = (pred[2048]{0:T(1024)(128)(4,1)S(1)}, pred[2048]{0:T(1024)(128)(4,1)}, u32[]{:S(2)}) copy-start(pred[2048]{0:T(1024)(128)(4,1)} %copy-done.40) | copy-start | bytes 6148
  470.0 222.0 %reduce-scatter.12.cloned.1.call-start = ((), (), s32[]{:S(2)}) async-start(), calls=%async_computation.16 | async-start | bytes 7077888 | tf_op jit(solution)/shard_map/reduce_scatter | solution.py:62
  481.7 269.3 %reduce-scatter.22.cloned.1.call-start = ((), (), s32[]{:S(2)}) async-start(), calls=%async_computation.25 | async-start | bytes 417792
  483.3 6.4 copy-start.46
  490.8 293.6 %all-gather.20.cloned.1.call-start = ((), (), s32[]{:S(2)}) async-start(), calls=%async_computation.21 | async-start | bytes 3538944 | tf_op jit(solution)/shard_map/all_gather | solution.py:54
  527.3 49.8 %all-to-all-start.3 = ((bf16[4,96,768]{2,1,0:T(8,128)(2,1)}), bf16[4,96,768]{2,1,0:T(8,128)(2,1)S(1)}, u32[]{:S(2)}, u32[]{:S(2)}) async-start(bf16[4,96,768]{2,1,0:T(8,128)(2,1)} %bitcast.195), calls=%async_computation.6 | async-start | bytes 1179648 | tf_op jit(solution)/shard_map/all_to_all | solution.py:58
  577.2 50.0 %copy-start.19 = (bf16[4,96,768]{2,1,0:T(8,128)(2,1)}, bf16[4,96,768]{2,1,0:T(8,128)(2,1)S(1)}, u32[]{:S(2)}) copy-start(bf16[4,96,768]{2,1,0:T(8,128)(2,1)S(1)} %all-to-all-done.3) | copy-start | bytes 1769476
  577.2 50.0 %all-to-all-start.4 = ((bf16[4,96,768]{2,1,0:T(8,128)(2,1)}), bf16[4,96,768]{2,1,0:T(8,128)(2,1)S(1)}, u32[]{:S(2)}, u32[]{:S(2)}) async-start(bf16[4,96,768]{2,1,0:T(8,128)(2,1)} %bitcast.194), calls=%async_computation.8 | async-start | bytes 1179648 | tf_op jit(solution)/shard_map/all_to_all | solution.py:58
  628.0 16.3 %copy-start.48 = (f32[256]{0:T(256)S(1)}, f32[256]{0:T(256)}, u32[]{:S(2)}) copy-start(f32[256]{0:T(256)} %copy-done.47) | copy-start | bytes 3076
  628.0 64.0 %copy-start.3 = (f32[256,1536]{1,0:T(8,128)S(1)}, f32[256,1536]{1,0:T(8,128)}, u32[]{:S(2)}) copy-start(f32[256,1536]{1,0:T(8,128)} %copy-done.1) | copy-start | bytes 4718596
  628.0 64.0 %copy-start.5 = (f32[256,1536]{1,0:T(8,128)S(1)}, f32[256,1536]{1,0:T(8,128)}, u32[]{:S(2)}) copy-start(f32[256,1536]{1,0:T(8,128)} %copy-done.4) | copy-start | bytes 4718596
  628.0 64.1 %copy-start.33 = (f32[1536]{0:T(1024)S(1)}, f32[1536]{0:T(1024)}, u32[]{:S(2)}) copy-start(f32[1536]{0:T(1024)} %get-tuple-element.16) | copy-start | bytes 18436
  628.0 64.0 %copy-start.45 = (f32[256]{0:T(256)S(1)}, f32[256]{0:T(256)}, u32[]{:S(2)}) copy-start(f32[256]{0:T(256)} %copy-done.43) | copy-start | bytes 3076
  628.0 64.0 %copy-start.52 = (f32[256]{0:T(256)S(1)}, f32[256]{0:T(256)}, u32[]{:S(2)}) copy-start(f32[256]{0:T(256)} %copy-done.51) | copy-start | bytes 3076
  628.0 14.0 %all-to-all-start.5 = ((bf16[4,96,768]{2,1,0:T(8,128)(2,1)}), bf16[4,96,768]{2,1,0:T(8,128)(2,1)}, u32[]{:S(2)}, u32[]{:S(2)}) async-start(bf16[4,96,768]{2,1,0:T(8,128)(2,1)} %bitcast.193), calls=%async_computation.10 | async-start | bytes 1179648 | tf_op jit(solution)/shard_map/all_to_all | solution.py:58
  (35 other events, 69.3 us)
Sparse Core Ops, SparseCore 0:
  10.9 66.8 all-gather.7
  80.0 51.7 all-gather.9
  133.7 44.1 all-gather.13
  180.2 45.5 all-gather.11
  269.0 61.7 reduce-scatter.13
  333.2 55.1 all-gather.17
  390.4 45.6 all-gather.15
  442.6 35.2 reduce-scatter.23
  480.3 47.0 reduce-scatter.15
  529.6 47.5 reduce-scatter.17
  579.6 47.5 reduce-scatter.19
  630.7 61.2 reduce-scatter.11
  695.5 55.5 reduce-scatter.21
  753.0 31.3 all-gather.19

commit v2 on v1

--- a/solution.py
+++ b/solution.py
@@ -9,7 +9,7 @@
 HK = 2
 HD = 128
 MICRO = 2
-PLANE = ("y", "c", "x")
+PLANE = ("c", "y", "x")
 GROUP = ("z", "y", "c")
 
 
@@ -62,11 +62,70 @@
     return lax.psum_scatter(block, axes, scatter_dimension=0, tiled=True)
 
 
-def by_owner(cols, parts):
+def swap(block, axis):
+    return lax.ppermute(block, axis, [(0, 1), (1, 0)])
+
+
+def by_pairs():
+    return lax.axis_size("x") == 2
+
+
+def plane_gather(block):
+    if not by_pairs():
+        return gather(block, PLANE)
+    half = block.shape[0] // 2
+    over_c = swap(block, "c")
+    over_y = swap(block, "y")
+    over_x = swap(block, "x")
+    over_both = [swap(over_y[:half], "x"), swap(over_x[half:], "y")]
+    others = [over_x, over_y] + over_both
+    pieces = [block] + others + [over_c] + [swap(piece, "c") for piece in others]
+    return jnp.concatenate(pieces, axis=0)
+
+
+def late_gather(block, after):
+    if not by_pairs():
+        block, after = lax.optimization_barrier((block, after))
+    return plane_gather(block)
+
+
+def add(left, right):
+    return (left.astype(jnp.float32) + right.astype(jnp.float32)).astype(left.dtype)
+
+
+def plane_sum(shares):
+    if not by_pairs():
+        return scatter_sum(shares[0].reshape(-1, shares[0].shape[-1]), PLANE)
+    shares = add(shares[0], swap(shares[1], "c"))
+    shares = shares.reshape((2, 2) + shares.shape[1:])
+    half = shares.shape[2] // 2
+    upper = add(shares[:, 0, :half], swap(shares[:, 1, :half], "x"))
+    lower = add(shares[0, :, half:], swap(shares[1, :, half:], "y"))
+    upper = add(upper[0], swap(upper[1], "y"))
+    lower = add(lower[0], swap(lower[1], "x"))
+    return jnp.concatenate([upper, lower], axis=0)
+
+
+def by_distance(array):
+    if not by_pairs():
+        return array
+    shape = array.shape
+    array = array.reshape((2, 2, 2) + shape[1:])
+    for dim, axis in enumerate(PLANE):
+        array = jnp.where(lax.axis_index(axis) == 1, jnp.flip(array, dim), array)
+    return array.reshape(shape)
+
+
+def own_block(array, rows):
+    place = 0 if by_pairs() else lax.axis_index(PLANE)
+    return lax.dynamic_slice_in_dim(array, place * rows, rows, 0)
+
+
+def by_source(cols):
     rows, total = cols.shape
-    return jnp.moveaxis(cols.reshape(rows, parts, total // parts), 1, 0).reshape(
-        parts * rows, total // parts
-    )
+    parts = 4 * lax.axis_size("x")
+    pieces = jnp.moveaxis(cols.reshape(rows, parts, total // parts), 1, 0)
+    return by_distance(exchange(pieces, PLANE)).reshape(parts * rows, total // parts)
 
 
 def local(
@@ -103,7 +162,6 @@
     q_cols, kv_cols = w_query.shape[1], w_key.shape[1]
     own_local = lax.axis_index(("y", "c"))
     own_expert = lax.axis_index("x") * local_count + own_local
-    own_place = lax.axis_index(PLANE)
 
     narrow = jnp.concatenate([w_router, norm1_gain[:, None], norm2_gain[:, None]], axis=1)
     narrow = jnp.pad(narrow, ((0, 0), (0, -narrow.shape[1] % 128)))
@@ -115,8 +173,8 @@
     gain_one, gain_two = gains[0], gains[1]
     output_w = gather(w_out, GROUP)
 
-    ids_all = gather(expert_ids, PLANE)
-    cot_all = gather(out_grad, PLANE)
+    ids_all = plane_gather(expert_ids)
+    cot_all = plane_gather(out_grad)
     chosen_mask = jnp.any(
         ids_all[:, :, None] == jnp.arange(experts_all, dtype=jnp.int32)[None, None, :], axis=1
     )
@@ -156,7 +214,7 @@
     resid = inputs_f + jnp.dot(attended, output_w, preferred_element_type=f32)
     second_in = rms_scale(resid, gain_two).astype(bf16)
 
-    second_all = gather(second_in, PLANE)
+    second_all = plane_gather(second_in)
     logits = jnp.dot(second_all, router_w, preferred_element_type=f32)
     gates_all = jax.nn.softmax(jnp.where(chosen_mask, logits, -jnp.inf), axis=-1)
     own_gates = lax.dynamic_index_in_dim(gates_all, own_expert, 1, keepdims=False)
@@ -177,11 +235,14 @@
         ).astype(bf16)
 
     def to_tokens(rows):
-        return (
-            jnp.einsum("bct,bcd->btd", dispatch, rows.astype(bf16), preferred_element_type=f32)
-            .astype(bf16)
-            .reshape(plane_rows, model_width)
-        )
+        def side(part):
+            tokens_part = jnp.einsum(
+                "bct,bcd->btd", dispatch[part], rows[part].astype(bf16), preferred_element_type=f32
+            )
+            return tokens_part.astype(bf16).reshape(-1, length, model_width)
+
+        step = blocks // 2 if by_pairs() else blocks
+        return [side(slice(at, at + step)) for at in range(0, blocks, step)]
 
     rows_in = to_rows(second_all)
     rows_cot = to_rows(cot_all)
@@ -202,20 +263,20 @@
     up_sum = scatter_sum(up_part.astype(bf16), "z")
     rows_grad = jnp.einsum("bcf,df->bcd", gate_pgrad, gate_w, preferred_element_type=f32)
     rows_grad = rows_grad + jnp.einsum("bcf,df->bcd", up_pgrad, up_w, preferred_element_type=f32)
-    second_back = scatter_sum(to_tokens(rows_grad), PLANE).astype(f32)
+    second_back = plane_sum(to_tokens(rows_grad)).astype(f32)
     gate_signal = jnp.einsum(
         "bct,bc->bt", dispatch.astype(f32), gate_signal_rows, precision=lax.Precision.HIGHEST
     )
-    gate_signal = exchange(gate_signal.reshape(plane, length), PLANE)
+    gate_signal = exchange(by_distance(gate_signal.reshape(plane, length)), PLANE)
     gate_signal = jnp.transpose(
-        gate_signal.reshape(local_count, owners, length), (2, 1, 0)
+        gate_signal.reshape(2, 2, owners, length), (3, 2, 1, 0)
     ).reshape(length, experts_all)
     expert_rows = jnp.einsum("bcf,fd->bcd", gated, down_w, preferred_element_type=f32)
-    mixture = scatter_sum(to_tokens(expert_rows), PLANE).astype(f32)
+    mixture = plane_sum(to_tokens(expert_rows)).astype(f32)
     block_out = (resid + mixture).astype(bf16)
 
     cotangent = out_grad.astype(f32)
-    gate_probs = lax.dynamic_slice_in_dim(gates_all, own_place * length, length, 0)
+    gate_probs = own_block(gates_all, length)
     logit_grad = (
         gate_probs
         * (gate_signal - jnp.sum(gate_probs * gate_signal, axis=-1, keepdims=True))
@@ -227,8 +288,8 @@
     resid_grad = cotangent + resid_norm_grad
     branch_grad = resid_grad.astype(bf16)
 
-    attended_all = gather(attended, PLANE)
-    branch_cols = exchange(by_owner(branch_grad, plane), PLANE)
+    attended_all = late_gather(attended, branch_grad)
+    branch_cols = by_source(branch_grad)
     output_part = left_product(attended_all, branch_cols)
     attended_grad = jnp.dot(branch_grad, output_w.T, preferred_element_type=f32).astype(bf16)
     attended_grad = attended_grad.reshape(length, HK, group_size, HD)
@@ -252,8 +313,8 @@
     value_back = jnp.einsum("hrij,ihrd->jhd", prob_bf, attended_grad, preferred_element_type=f32)
     value_back = value_back.astype(bf16).reshape(length, HK * HD)
     qkv_back = jnp.concatenate([query_back, key_back, value_back], axis=1)
-    first_all = gather(first_in, PLANE)
-    qkv_part = left_product(first_all, exchange(by_owner(qkv_back, plane), PLANE))
+    first_all = late_gather(first_in, output_part)
+    qkv_part = left_product(first_all, by_source(qkv_back))
     first_grad = lax.dot_general(
         qkv_back, qkv_w, (((1,), (1,)), ((), ())), preferred_element_type=f32
     )
@@ -263,18 +324,46 @@
 
     narrow_part = jnp.concatenate(
         [router_acc, gain_one_grad[:, None], gain_two_grad[:, None]], axis=1
+    )
+    narrow_cols = -(-narrow_part.shape[1] // owners) * owners
+    narrow_part = jnp.pad(narrow_part, ((0, 0), (0, narrow_cols - narrow_part.shape[1])))
+    narrow_part = jnp.transpose(
+        narrow_part.reshape(depth, 2, 2, shard_rows, owners, narrow_cols // owners),
+        (2, 1, 4, 0, 3, 5),
+    ).reshape(plane, depth, shard_rows * narrow_cols // owners)
+    narrow_part = jnp.sum(exchange(narrow_part, PLANE), axis=0)
+    qkv_width = qkv_cols // plane
+    dense_cols = qkv_width + model_width // plane
+    narrow_len = narrow_part.shape[1]
+    narrow_rows = -(-narrow_len // dense_cols)
+    narrow_part = jnp.pad(narrow_part, ((0, 0), (0, narrow_rows * dense_cols - narrow_len)))
+    pad_rows = -(local_count * shard_rows + narrow_rows) % 8
+    dense_part = jnp.concatenate(
+        [
+            jnp.concatenate([qkv_part, output_part], axis=1).reshape(
+                depth, local_count * shard_rows, dense_cols
+            ),
+            narrow_part.reshape(depth, narrow_rows, dense_cols),
+            jnp.zeros((depth, pad_rows, dense_cols), f32),
+        ],
+        axis=1,
     ).astype(bf16)
-    narrow_cols = narrow_part.shape[1]
-    narrow_sum = lax.psum(scatter_sum(narrow_part, GROUP), "x").astype(f32)
-    dense_part = jnp.concatenate([qkv_part, output_part], axis=1).astype(bf16)
-    dense_sum = scatter_sum(dense_part, "z")
-    dense_cols = dense_sum.shape[1]
-    dense_sum = gather(dense_sum, PLANE).reshape(plane, local_count, shard_rows, dense_cols)
-    dense_sum = lax.dynamic_index_in_dim(dense_sum, own_local, 1, keepdims=False).astype(f32)
-    dense_sum = jnp.moveaxis(dense_sum, 0, 1)
-    qkv_width = qkv_cols // plane
-    qkv_sum = dense_sum[:, :, :qkv_width].reshape(shard_rows, qkv_cols)
-    output_sum = dense_sum[:, :, qkv_width:].reshape(shard_rows, model_width)
+    dense_sum = scatter_sum(dense_part.reshape(-1, dense_cols), "z")
+    wide_sum = dense_sum[: local_count * shard_rows].reshape(2, 2, 1, shard_rows, dense_cols)
+    wide_sum = jnp.broadcast_to(
+        jnp.swapaxes(wide_sum, 0, 1), (2, 2, owners, shard_rows, dense_cols)
+    ).reshape(plane, shard_rows, dense_cols)
+    narrow_sum = dense_sum[local_count * shard_rows :][:narrow_rows]
+    narrow_sum = jnp.broadcast_to(narrow_sum[None], (plane, narrow_rows, dense_cols))
+    dense_sum = exchange(jnp.concatenate([wide_sum, narrow_sum], axis=1), PLANE)
+    wide_sum = jnp.moveaxis(dense_sum[:, :shard_rows].astype(f32), 0, 1)
+    qkv_sum = wide_sum[:, :, :qkv_width].reshape(shard_rows, qkv_cols)
+    output_sum = wide_sum[:, :, qkv_width:].reshape(shard_rows, model_width)
+    narrow_sum = dense_sum[:, shard_rows:].reshape(2, 2, owners, narrow_rows * dense_cols)
+    narrow_sum = narrow_sum[lax.axis_index("c"), lax.axis_index("y"), :, :narrow_len]
+    narrow_sum = jnp.moveaxis(
+        narrow_sum.reshape(owners, shard_rows, narrow_cols // owners), 0, 1
+    ).reshape(shard_rows, narrow_cols).astype(f32)
 
     def placed(total):
         total = exchange(total, ("y", "c"))

time: 805 us -> 559 us (0.69)
  waiting for transfers between devices: 529 us -> 177 us
  local copies, waits for them, and re-layouts: 38.7 us -> 91.8 us
  starting transfers between devices: 24.1 us -> 72 us
  other arithmetic: 31.6 us -> 52.9 us
  blocking collectives: 18.2 us -> 0 us
    reduce_scatter x6 -> x4, waiting for transfers between devices: 219 us -> 0.03 us  [scatter_sum(): return lax.psum_scatter(block, axes, scatter_dimension=0, tiled=True)]
    all_gather x7 -> x2, waiting for transfers between devices: 228 us -> 47.7 us  [gather(): return lax.all_gather(block, axes, axis=0, tiled=True)]
    ppermute x0 -> x55, waiting for transfers between devices: none -> 91.1 us  [swap(): return lax.ppermute(block, axis, [(0, 1), (1, 0)])]
    unnamed x15 -> x6, waiting for transfers between devices: 58.3 us -> 0.1 us
    ppermute x0 -> x55, starting transfers between devices: none -> 39.8 us  [swap(): return lax.ppermute(block, axis, [(0, 1), (1, 0)])]
    unnamed x131 -> x179, local copies, waits for them, and re-layouts: 13.3 us -> 45.1 us
    all_to_all x6 -> x8, waiting for transfers between devices: 24 us -> 38.6 us  [exchange(): return lax.all_to_all(block, axes, split_axis=0, concat_axis=0, tiled=True)]
    convert_element_type x3 -> x9, other arithmetic: 1.33 us -> 14.8 us  [the longest x8 14.8 us: add(): (left.astype(jnp.float32) + right.astype(jnp.float32)).astype(left.dtype)]
  transfers between devices with their start and end apart: 20 -> 69, of which waited for: 16 -> 25; matrix products, arithmetic and copies ran while one was open for 18% -> 47% of each run, Pallas kernels for 0% -> 0%
where the time goes in v2:
time: 559 us; the launch traced here: 548 us
  waiting for transfers between devices  177 us (32%)
  matrix products  137 us (25%)
  local copies, waits for them, and re-layouts  91.8 us (16%)
  starting transfers between devices  72 us (13%)
  other arithmetic  52.9 us (9%)
  between operations  16.7 us (3%)
    ppermute x55, waiting for transfers between devices, swap(): return lax.ppermute(block, axis, [(0, 1), (1, 0)])  91.1 us
    all_gather x2, waiting for transfers between devices, gather(): return lax.all_gather(block, axes, axis=0, tiled=True)  47.7 us
    unnamed x179, local copies, waits for them, and re-layouts  45.1 us
    ppermute x55, starting transfers between devices, swap(): return lax.ppermute(block, axis, [(0, 1), (1, 0)])  39.8 us
    all_to_all x8, waiting for transfers between devices, exchange(): return lax.all_to_all(block, axes, split_axis=0, concat_axis=0, tiled=True)  38.6 us
    all_to_all x8, starting transfers between devices, exchange(): return lax.all_to_all(block, axes, split_axis=0, concat_axis=0, tiled=True)  31.5 us
    dot_general x4, matrix products, side(): jnp.einsum('bct,bcd->btd', dispatch[part], rows[part].astype(bf16), prefe...  16 us
    convert_element_type x8, other arithmetic, add(): (left.astype(jnp.float32) + right.astype(jnp.float32)).astype(left.dtype)  14.8 us
  transfers between devices with their start and end apart: 69, of which 25 were waited for; matrix products, arithmetic and copies ran while one was open for 47% of the time, Pallas kernels for 0%

profile of v2, /device:TPU:0, one launch (start us, length us, event | category | flops | bytes accessed | tf_op | source)
XLA Modules:
  0.0 547.8 jit_solution(11846366754741121603)
XLA Ops:
  10.0 3.0 collective-permute-start.1
  24.7 10.2 %collective-permute-done.2 = s32[128,4]{0,1:T(4,128)S(1)} collective-permute-done((s32[128,4]{0,1:T(4,128)S(1)}, s32[128,4]{0,1:T(4,128)S(1)}, u32[]{:S(2)}, u32[]{:S(2)}) %collective-permute-start.2) | collective-permute-done | bytes 2080 | tf_op jit(solution)/shard_map/ppermute | solution.py:66
  47.0 7.3 %collective-permute-done.25 = bf16[128,1536]{1,0:T(8,128)(2,1)S(1)} collective-permute-done((bf16[128,1536]{1,0:T(8,128)(2,1)S(1)}, bf16[128,1536]{1,0:T(8,128)(2,1)S(1)}, u32[]{:S(2)}, u32[]{:S(2)}) %collective-permute-start.25) | collective-permute-done | bytes 393248 | tf_op jit(solution)/shard_map/ppermute | solution.py:66
  54.3 7.2 %collective-permute-done.26 = bf16[128,1536]{1,0:T(8,128)(2,1)S(1)} collective-permute-done((bf16[128,1536]{1,0:T(8,128)(2,1)S(1)}, bf16[128,1536]{1,0:T(8,128)(2,1)S(1)}, u32[]{:S(2)}, u32[]{:S(2)}) %collective-permute-start.26) | collective-permute-done | bytes 393248 | tf_op jit(solution)/shard_map/ppermute | solution.py:66
  67.5 6.4 %convolution_convert_fusion.1 = bf16[16,96,1536]{2,1,0:T(8,128)(2,1)} fusion(bf16[16,128,1536]{2,1,0:T(8,128)(2,1)} %bitcast.264, s32[16,128]{1,0:T(8,128)S(1)} %broadcast_add_fusion, pred[16,128]{1,0:T(8,128)(4,1)S(1)} %bitcast.303), kind=kOutput, calls=%fused_computation.25 | convolution fusion | flops 606732288 | bytes 11020288 | tf_op jit(solution)/shard_map/bct,btd->bcd/dot_general | solution.py:230
  73.9 13.3 %all-gather.3.cloned.1.call-done = bf16[1536,2176]{1,0:T(8,128)(2,1)} async-done(((bf16[96,2176]{1,0:T(8,128)(2,1)}), bf16[1536,2176]{1,0:T(8,128)(2,1)}) %all-gather.3.cloned.1.call-update) | async-done | bytes 6684688 | tf_op jit(solution)/shard_map/all_gather | solution.py:54
  90.5 4.8 fusion.4
  107.1 34.5 %all-gather.5.cloned.1.call-done = bf16[1536,1536]{1,0:T(8,128)(2,1)} async-done(((bf16[96,1536]{1,0:T(8,128)(2,1)}), bf16[1536,1536]{1,0:T(8,128)(2,1)}) %all-gather.5.cloned.1.call-update) | async-done | bytes 4718608 | tf_op jit(solution)/shard_map/all_gather | solution.py:54
  141.6 3.8 multiply_reduce_fusion.3
  147.8 6.6 %fusion.21 = f32[16,96,768]{2,1,0:T(8,128)S(1)} fusion(bf16[16,96,1536]{2,1,0:T(8,128)(2,1)} %convolution_convert_fusion.1, bf16[4,768,1536]{2,1,0:T(8,128)(2,1)} %param.24, s32[]{:T(128)S(6)} %select_n.89), kind=kOutput, calls=%fused_computation.56 | convolution fusion | flops 3623878656 | bytes 11796484 | tf_op jit(solution)/shard_map/bcd,fd->bcf/dot_general | solution.py:255
  155.9 10.2 %collective-permute-done.10 = bf16[256,1536]{1,0:T(8,128)(2,1)S(1)} collective-permute-done((bf16[256,1536]{1,0:T(8,128)(2,1)S(1)}, bf16[256,1536]{1,0:T(8,128)(2,1)S(1)}, u32[]{:S(2)}, u32[]{:S(2)}) %collective-permute-start.10) | collective-permute-done | bytes 786464 | tf_op jit(solution)/shard_map/ppermute | solution.py:66
  168.5 7.6 %collective-permute-done.11 = bf16[128,1536]{1,0:T(8,128)(2,1)S(1)} collective-permute-done((bf16[128,1536]{1,0:T(8,128)(2,1)S(1)}, bf16[128,1536]{1,0:T(8,128)(2,1)S(1)}, u32[]{:S(2)}, u32[]{:S(2)}) %collective-permute-start.11) | collective-permute-done | bytes 393248 | tf_op jit(solution)/shard_map/ppermute | solution.py:66
  176.1 14.7 %collective-permute-done.12 = bf16[128,1536]{1,0:T(8,128)(2,1)S(1)} collective-permute-done((bf16[128,1536]{1,0:T(8,128)(2,1)S(1)}, bf16[128,1536]{1,0:T(8,128)(2,1)S(1)}, u32[]{:S(2)}, u32[]{:S(2)}) %collective-permute-start.12) | collective-permute-done | bytes 393248 | tf_op jit(solution)/shard_map/ppermute | solution.py:66
  200.3 6.5 %fusion.25 = f32[16,96,768]{2,1,0:T(8,128)S(1)} fusion(bf16[16,96,1536]{2,1,0:T(8,128)(2,1)S(1)} %convolution_convert_fusion.2, bf16[4,1536,768]{2,1,0:T(8,128)(2,1)} %param.23, s32[]{:T(128)S(6)} %select_n.89), kind=kOutput, calls=%fused_computation.60 | convolution fusion | flops 3623878656 | bytes 11796484 | tf_op jit(solution)/shard_map/bcd,df->bcf/dot_general | solution.py:250
  206.8 12.5 %fusion.12 = (bf16[16,96,768]{2,1,0:T(8,128)(2,1)}, f32[16,96]{1,0:T(8,128)S(1)}, bf16[16,96,768]{2,1,0:T(8,128)(2,1)}, f32[16,96,768]{2,1,0:T(8,128)S(1)}) fusion(f32[16,96,768]{2,1,0:T(8,128)S(1)} %fusion.25, f32[16,96,768]{2,1,0:T(8,128)S(1)} %fusion.21, f32[16,96]{1,0:T(8,128)S(1)} %bitcast.314, ...), kind=kOutput, calls=%fused_computation.17 | convolution fusion | flops 3656907264 | bytes 25964548 | tf_op jit(solution)/shard_map/bcd,df->bcf/dot_general | solution.py:249
  221.5 5.7 %bitcast_convert_fusion = bf16[1536,768]{1,0:T(8,128)(2,1)} fusion(bf16[16,96,1536]{2,1,0:T(8,128)(2,1)S(1)} %bitcast.277, f32[16,96]{1,0:T(8,128)S(1)} %bitcast.315, f32[16,96,768]{2,1,0:T(8,128)S(1)} %fusion.25, f32[16,96,768]{2,1,0:T(8,128)S(1)} %get-tuple-element.54), kind=kOutput, calls=%fused_computation.18 | convolution fusion | flops 3638034432 | bytes 16521216 | tf_op jit(solution)/shard_map/bcd,bcf->df/dot_general | solution.py:253
  251.6 5.0 collective-permute-done.49
  260.5 8.4 %bitcast_convert_fusion.2 = bf16[1536,768]{1,0:T(8,128)(2,1)} fusion(bf16[16,96,1536]{2,1,0:T(8,128)(2,1)} %copy-done.13, bf16[16,96,768]{2,1,0:T(8,128)(2,1)} %get-tuple-element.22), kind=kOutput, calls=%fused_computation.20 | convolution fusion | flops 3625058304 | bytes 9437184 | tf_op jit(solution)/shard_map/bcd,bcf->df/dot_general | solution.py:260
  269.6 3.3 all-to-all-start
  273.4 6.4 %fusion.27 = f32[16,96,1536]{2,1,0:T(8,128)S(1)} fusion(bf16[16,96,768]{2,1,0:T(8,128)(2,1)} %get-tuple-element.22, bf16[4,1536,768]{2,1,0:T(8,128)(2,1)} %param.22, s32[]{:T(128)S(6)} %select_n.89), kind=kOutput, calls=%fused_computation.62 | convolution fusion | flops 3623878656 | bytes 14155780 | tf_op jit(solution)/shard_map/bcf,df->bcd/dot_general | solution.py:264
  279.8 12.1 %convolution_convert_fusion = bf16[16,96,1536]{2,1,0:T(8,128)(2,1)} fusion(bf16[4,768,1536]{2,1,0:T(8,128)(2,1)} %param.24, s32[]{:T(128)S(6)} %select_n.89, f32[16,96]{1,0:T(8,128)S(1)} %bitcast.316, f32[16,96,768]{2,1,0:T(8,128)} %copy-done.56, f32[16,96,768]{2,1,0:T(8,128)} %copy-done.57), kind=kOutput, calls=%fused_computation.24 | convolution fusion | flops 3639214080 | bytes 16521220 | tf_op jit(solution)/shard_map/bcf,fd->bcd/dot_general | solution.py:274
  291.9 7.3 %add_convert_fusion = bf16[16,96,1536]{2,1,0:T(8,128)(2,1)} fusion(f32[16,96,1536]{2,1,0:T(8,128)S(1)} %fusion.27, bf16[16,96,768]{2,1,0:T(8,128)(2,1)S(1)} %copy-done.58, bf16[4,1536,768]{2,1,0:T(8,128)(2,1)} %param.23, s32[]{:T(128)S(6)} %select_n.89), kind=kOutput, calls=%fused_computation | convolution fusion | flops 3628597248 | bytes 18874372 | tf_op jit(solution)/shard_map/bcf,df->bcd/dot_general | solution.py:265
  299.3 5.4 bitcast_convert_fusion.1
  304.7 4.4 convolution_convert_fusion.5
  309.1 4.4 convolution_convert_fusion.3
  316.1 4.5 convolution_convert_fusion.6
  335.0 3.9 fusion
  342.5 4.4 fusion.1
  346.9 11.9 %collective-permute-done.33 = bf16[2,128,1536]{2,1,0:T(8,128)(2,1)S(1)} collective-permute-done((bf16[2,128,1536]{2,1,0:T(8,128)(2,1)S(1)}, bf16[2,128,1536]{2,1,0:T(8,128)(2,1)S(1)}, u32[]{:S(2)}, u32[]{:S(2)}) %collective-permute-start.33) | collective-permute-done | bytes 786464 | tf_op jit(solution)/shard_map/ppermute | solution.py:66
  363.0 8.3 %collective-permute-done.36 = bf16[128,1536]{1,0:T(8,128)(2,1)S(1)} collective-permute-done((bf16[128,1536]{1,0:T(8,128)(2,1)S(1)}, bf16[128,1536]{1,0:T(8,128)(2,1)S(1)}, u32[]{:S(2)}, u32[]{:S(2)}) %collective-permute-start.36) | collective-permute-done | bytes 393248 | tf_op jit(solution)/shard_map/ppermute | solution.py:66
  387.9 7.0 %fusion.41 = (f32[1536]{0:T(1024)S(1)}, f32[256]{0:T(256)}, f32[256,1536]{1,0:T(8,128)}) fusion(bf16[256,1536]{1,0:T(8,128)(2,1)} %param.14, f32[256]{0:T(256)S(1)} %copy-done.54, f32[1536]{0:T(1024)S(1)} %copy-done.46, bf16[1536,2176]{1,0:T(8,128)(2,1)} %all-gather.3.cloned.1.call-done, bf16[256,256]{0,1:T(8,128)(2,1)S(1)} %bitcast.297, ...), kind=kOutput, calls=%fused_computation.78 | convolution fusion | flops 1616509184 | bytes 9713664 | tf_op jit(solution)/shard_map/dot_general | solution.py:318
  401.1 3.7 all-to-all-start.3
  410.0 4.2 all-to-all-start.2
  419.4 15.4 %all-to-all-done.2 = bf16[8,256,192]{1,2,0:T(8,128)(2,1)} async-done(((bf16[8,256,192]{1,2,0:T(8,128)(2,1)}), bf16[8,256,192]{1,2,0:T(8,128)(2,1)}, u32[]{:S(2)}, u32[]{:S(2)}) %all-to-all-start.2) | async-done | bytes 786464 | tf_op jit(solution)/shard_map/all_to_all | solution.py:58
  434.8 4.2 all-to-all-start.1
  442.7 3.4 reshape_reshape.11
  446.0 6.0 %convolution_convert_fusion.9 = bf16[1536,192]{0,1:T(8,128)(2,1)} fusion(bf16[2048,1536]{0,1:T(8,128)(2,1)} %constant_dynamic-update-slice_fusion.40, bf16[2048,192]{0,1:T(8,128)(2,1)} %reshape_reshape.11), kind=kOutput, calls=%fused_computation.48 | convolution fusion | flops 1208254464 | bytes 7667712 | tf_op jit(solution)/shard_map/dot_general | solution.py:48
  458.5 4.7 convolution_convert_fusion.7
  467.0 2.9 maximum_maximum_fusion
  474.6 3.5 all-to-all-start.7
  481.9 6.2 %all-to-all-done.7 = bf16[4,96,768]{2,1,0:T(8,128)(2,1)S(1)} async-done(((bf16[4,96,768]{2,1,0:T(8,128)(2,1)}), bf16[4,96,768]{2,1,0:T(8,128)(2,1)S(1)}, u32[]{:S(2)}, u32[]{:S(2)}) %all-to-all-start.7) | async-done | bytes 589856 | tf_op jit(solution)/shard_map/all_to_all | solution.py:58
  488.9 4.2 all-to-all-start.5
  494.5 8.2 %all-to-all-done.5 = bf16[4,96,768]{2,1,0:T(8,128)(2,1)} async-done(((bf16[4,96,768]{2,1,0:T(8,128)(2,1)}), bf16[4,96,768]{2,1,0:T(8,128)(2,1)}, u32[]{:S(2)}, u32[]{:S(2)}) %all-to-all-start.5) | async-done | bytes 589856 | tf_op jit(solution)/shard_map/all_to_all | solution.py:58
  502.7 4.2 all-to-all-start.6
  513.0 3.5 all-to-all-done.6
  516.5 4.2 all-to-all-start.4
  520.7 4.0 fusion.44
  530.2 3.3 all-to-all-done.4
  (452 shorter events, 194.4 us)
Async XLA Ops:
  7.2 80.0 %all-gather.3.cloned.1.call-start = ((), (), s32[]{:S(2)}) async-start(), calls=%async_computation.12 | async-start | bytes 7102464 | tf_op jit(solution)/shard_map/all_gather | solution.py:54
  9.9 131.7 %all-gather.5.cloned.1.call-start = ((), (), s32[]{:S(2)}) async-start(), calls=%async_computation.13 | async-start | bytes 5013504 | tf_op jit(solution)/shard_map/all_gather | solution.py:54
  10.0 12.7 %collective-permute-start.1 = (s32[256,4]{0,1:T(4,128)}, s32[256,4]{0,1:T(4,128)S(1)}, u32[]{:S(2)}, u32[]{:S(2)}) collective-permute-start(s32[256,4]{0,1:T(4,128)} %param.25), channel_id=1, source_target_pairs={{0,4},{4,0},{1,5},{5,1},{2,6},{6,2},{3,7},{7,3},{8,12},{12,8},{9,1... | collective-permute-start | bytes 12296 | tf_op jit(solution)/shard_map/ppermute | solution.py:66
  14.5 24.7 %collective-permute-start.4 = (s32[256,4]{0,1:T(4,128)}, s32[256,4]{0,1:T(4,128)S(1)}, u32[]{:S(2)}, u32[]{:S(2)}) collective-permute-start(s32[256,4]{0,1:T(4,128)} %param.25), channel_id=1, source_target_pairs={{0,2},{2,0},{1,3},{3,1},{4,6},{6,4},{5,7},{7,5},{8,10},{10,8},{9,1... | collective-permute-start | bytes 12296 | tf_op jit(solution)/shard_map/ppermute | solution.py:66
  14.5 28.5 %collective-permute-start.24 = (bf16[256,1536]{1,0:T(8,128)(2,1)}, bf16[256,1536]{1,0:T(8,128)(2,1)S(1)}, u32[]{:S(2)}, u32[]{:S(2)}) collective-permute-start(bf16[256,1536]{1,0:T(8,128)(2,1)} %param.27), channel_id=1, source_target_pairs={{0,4},{4,0},{1,5},{5,1},{2,6},{6,2},{3,7},{7,3},{8,12},{12,8},{9,1... | collective-permute-start | bytes 2359304 | tf_op jit(solution)/shard_map/ppermute | solution.py:66
  15.0 28.7 %collective-permute-start.23 = (bf16[256,1536]{1,0:T(8,128)(2,1)}, bf16[256,1536]{1,0:T(8,128)(2,1)S(1)}, u32[]{:S(2)}, u32[]{:S(2)}) collective-permute-start(bf16[256,1536]{1,0:T(8,128)(2,1)} %param.27), channel_id=1, source_target_pairs={{0,1},{1,0},{2,3},{3,2},{4,5},{5,4},{6,7},{7,6},{8,9},{9,8},{10,11... | collective-permute-start | bytes 2359304 | tf_op jit(solution)/shard_map/ppermute | solution.py:66
  15.1 459.5 %reduce-scatter.11.cloned.1.call-start = ((), (), s32[]{:S(2)}) async-start(), calls=%async_computation.17 | async-start | bytes 2949120 | tf_op jit(solution)/shard_map/reduce_scatter | solution.py:62
  22.7 40.4 %collective-permute-start.27 = (bf16[256,1536]{1,0:T(8,128)(2,1)}, bf16[256,1536]{1,0:T(8,128)(2,1)S(1)}, u32[]{:S(2)}, u32[]{:S(2)}) collective-permute-start(bf16[256,1536]{1,0:T(8,128)(2,1)} %param.27), channel_id=1, source_target_pairs={{0,2},{2,0},{1,3},{3,1},{4,6},{6,4},{5,7},{7,5},{8,10},{10,8},{9,1... | collective-permute-start | bytes 2359304 | tf_op jit(solution)/shard_map/ppermute | solution.py:66
  43.7 17.8 %collective-permute-start.26 = (bf16[128,1536]{1,0:T(8,128)(2,1)S(1)}, bf16[128,1536]{1,0:T(8,128)(2,1)S(1)}, u32[]{:S(2)}, u32[]{:S(2)}) collective-permute-start(bf16[128,1536]{1,0:T(8,128)(2,1)S(1)} %slice.276), channel_id=1, source_target_pairs={{0,4},{4,0},{1,5},{5,1},{2,6},{6,2},{3,7},{7,3},{8,12},{12,8},{9,1... | collective-permute-start | bytes 1179656 | tf_op jit(solution)/shard_map/ppermute | solution.py:66
  44.6 20.4 %collective-permute-start.29 = (bf16[256,1536]{1,0:T(8,128)(2,1)S(1)}, bf16[256,1536]{1,0:T(8,128)(2,1)S(1)}, u32[]{:S(2)}, u32[]{:S(2)}) collective-permute-start(bf16[256,1536]{1,0:T(8,128)(2,1)S(1)} %collective-permute-done.24), channel_id=1, source_target_pairs={{0,2},{2,0},{1,3},{3,1},{4,6},{6,4},{5,7},{7,5},{8,10},{10,8},{9,1... | collective-permute-start | bytes 2359304 | tf_op jit(solution)/shard_map/ppermute | solution.py:66
  44.6 19.4 %collective-permute-start.28 = (bf16[256,1536]{1,0:T(8,128)(2,1)S(1)}, bf16[256,1536]{1,0:T(8,128)(2,1)S(1)}, u32[]{:S(2)}, u32[]{:S(2)}) collective-permute-start(bf16[256,1536]{1,0:T(8,128)(2,1)S(1)} %collective-permute-done.23), channel_id=1, source_target_pairs={{0,2},{2,0},{1,3},{3,1},{4,6},{6,4},{5,7},{7,5},{8,10},{10,8},{9,1... | collective-permute-start | bytes 2359304 | tf_op jit(solution)/shard_map/ppermute | solution.py:66
  145.7 20.4 %collective-permute-start.10 = (bf16[256,1536]{1,0:T(8,128)(2,1)S(1)}, bf16[256,1536]{1,0:T(8,128)(2,1)S(1)}, u32[]{:S(2)}, u32[]{:S(2)}) collective-permute-start(bf16[256,1536]{1,0:T(8,128)(2,1)S(1)} %get-tuple-element.21), channel_id=1, source_target_pairs={{0,4},{4,0},{1,5},{5,1},{2,6},{6,2},{3,7},{7,3},{8,12},{12,8},{9,1... | collective-permute-start | bytes 2359304 | tf_op jit(solution)/shard_map/ppermute | solution.py:66
  146.3 21.4 %collective-permute-start.9 = (bf16[256,1536]{1,0:T(8,128)(2,1)S(1)}, bf16[256,1536]{1,0:T(8,128)(2,1)S(1)}, u32[]{:S(2)}, u32[]{:S(2)}) collective-permute-start(bf16[256,1536]{1,0:T(8,128)(2,1)S(1)} %get-tuple-element.21), channel_id=1, source_target_pairs={{0,1},{1,0},{2,3},{3,2},{4,5},{5,4},{6,7},{7,6},{8,9},{9,8},{10,11... | collective-permute-start | bytes 2359304 | tf_op jit(solution)/shard_map/ppermute | solution.py:66
  154.4 75.3 %collective-permute-start.38 = (bf16[256,1536]{1,0:T(8,128)(2,1)}, bf16[256,1536]{1,0:T(8,128)(2,1)}, u32[]{:S(2)}, u32[]{:S(2)}) collective-permute-start(bf16[256,1536]{1,0:T(8,128)(2,1)} %get-tuple-element.19), channel_id=1, source_target_pairs={{0,4},{4,0},{1,5},{5,1},{2,6},{6,2},{3,7},{7,3},{8,12},{12,8},{9,1... | collective-permute-start | bytes 2359304 | tf_op jit(solution)/shard_map/ppermute | solution.py:66
  155.9 36.3 %collective-permute-start.13 = (bf16[256,1536]{1,0:T(8,128)(2,1)S(1)}, bf16[256,1536]{1,0:T(8,128)(2,1)S(1)}, u32[]{:S(2)}, u32[]{:S(2)}) collective-permute-start(bf16[256,1536]{1,0:T(8,128)(2,1)S(1)} %get-tuple-element.21), channel_id=1, source_target_pairs={{0,2},{2,0},{1,3},{3,1},{4,6},{6,4},{5,7},{7,5},{8,10},{10,8},{9,1... | collective-permute-start | bytes 2359304 | tf_op jit(solution)/shard_map/ppermute | solution.py:66
  167.7 23.0 %collective-permute-start.12 = (bf16[128,1536]{1,0:T(8,128)(2,1)S(1)}, bf16[128,1536]{1,0:T(8,128)(2,1)S(1)}, u32[]{:S(2)}, u32[]{:S(2)}) collective-permute-start(bf16[128,1536]{1,0:T(8,128)(2,1)S(1)} %slice.263), channel_id=1, source_target_pairs={{0,4},{4,0},{1,5},{5,1},{2,6},{6,2},{3,7},{7,3},{8,12},{12,8},{9,1... | collective-permute-start | bytes 1179656 | tf_op jit(solution)/shard_map/ppermute | solution.py:66
  168.3 24.6 %collective-permute-start.14 = (bf16[256,1536]{1,0:T(8,128)(2,1)S(1)}, bf16[256,1536]{1,0:T(8,128)(2,1)S(1)}, u32[]{:S(2)}, u32[]{:S(2)}) collective-permute-start(bf16[256,1536]{1,0:T(8,128)(2,1)S(1)} %collective-permute-done.9), channel_id=1, source_target_pairs={{0,2},{2,0},{1,3},{3,1},{4,6},{6,4},{5,7},{7,5},{8,10},{10,8},{9,1... | collective-permute-start | bytes 2359304 | tf_op jit(solution)/shard_map/ppermute | solution.py:66
  176.0 17.1 %collective-permute-start.15 = (bf16[256,1536]{1,0:T(8,128)(2,1)S(1)}, bf16[256,1536]{1,0:T(8,128)(2,1)S(1)}, u32[]{:S(2)}, u32[]{:S(2)}) collective-permute-start(bf16[256,1536]{1,0:T(8,128)(2,1)S(1)} %collective-permute-done.10), channel_id=1, source_target_pairs={{0,2},{2,0},{1,3},{3,1},{4,6},{6,4},{5,7},{7,5},{8,10},{10,8},{9,1... | collective-permute-start | bytes 2359304 | tf_op jit(solution)/shard_map/ppermute | solution.py:66
  190.7 40.4 %collective-permute-start.37 = (bf16[256,1536]{1,0:T(8,128)(2,1)}, bf16[256,1536]{1,0:T(8,128)(2,1)}, u32[]{:S(2)}, u32[]{:S(2)}) collective-permute-start(bf16[256,1536]{1,0:T(8,128)(2,1)} %get-tuple-element.19), channel_id=1, source_target_pairs={{0,1},{1,0},{2,3},{3,2},{4,5},{5,4},{6,7},{7,6},{8,9},{9,8},{10,11... | collective-permute-start | bytes 2359304 | tf_op jit(solution)/shard_map/ppermute | solution.py:66
  192.2 41.5 %collective-permute-start.47 = (bf16[256,1536]{0,1:T(8,128)(2,1)S(1)}, bf16[256,1536]{0,1:T(8,128)(2,1)}, u32[]{:S(2)}, u32[]{:S(2)}) collective-permute-start(bf16[256,1536]{0,1:T(8,128)(2,1)S(1)} %bitcast.260), channel_id=1, source_target_pairs={{0,4},{4,0},{1,5},{5,1},{2,6},{6,2},{3,7},{7,3},{8,12},{12,8},{9,1... | collective-permute-start | bytes 2359304 | tf_op jit(solution)/shard_map/ppermute | solution.py:66
  194.7 41.6 %collective-permute-start.46 = (bf16[256,1536]{0,1:T(8,128)(2,1)S(1)}, bf16[256,1536]{0,1:T(8,128)(2,1)}, u32[]{:S(2)}, u32[]{:S(2)}) collective-permute-start(bf16[256,1536]{0,1:T(8,128)(2,1)S(1)} %bitcast.261), channel_id=1, source_target_pairs={{0,1},{1,0},{2,3},{3,2},{4,5},{5,4},{6,7},{7,6},{8,9},{9,8},{10,11... | collective-permute-start | bytes 2359304 | tf_op jit(solution)/shard_map/ppermute | solution.py:66
  227.1 254.8 %reduce-scatter.7.cloned.1.call-start = ((), (), s32[]{:S(2)}) async-start(), calls=%async_computation.15 | async-start | bytes 2949120 | tf_op jit(solution)/shard_map/reduce_scatter | solution.py:62
  228.6 28.9 %collective-permute-start.41 = (bf16[256,1536]{1,0:T(8,128)(2,1)}, bf16[256,1536]{1,0:T(8,128)(2,1)S(1)}, u32[]{:S(2)}, u32[]{:S(2)}) collective-permute-start(bf16[256,1536]{1,0:T(8,128)(2,1)} %get-tuple-element.19), channel_id=1, source_target_pairs={{0,2},{2,0},{1,3},{3,1},{4,6},{6,4},{5,7},{7,5},{8,10},{10,8},{9,1... | collective-permute-start | bytes 2359304 | tf_op jit(solution)/shard_map/ppermute | solution.py:66
  229.7 29.2 %collective-permute-start.50 = (bf16[256,1536]{0,1:T(8,128)(2,1)S(1)}, bf16[256,1536]{0,1:T(8,128)(2,1)S(1)}, u32[]{:S(2)}, u32[]{:S(2)}) collective-permute-start(bf16[256,1536]{0,1:T(8,128)(2,1)S(1)} %bitcast.263), channel_id=1, source_target_pairs={{0,2},{2,0},{1,3},{3,1},{4,6},{6,4},{5,7},{7,5},{8,10},{10,8},{9,1... | collective-permute-start | bytes 2359304 | tf_op jit(solution)/shard_map/ppermute | solution.py:66
  231.1 15.2 %collective-permute-start.39 = (bf16[128,1536]{1,0:T(8,128)(2,1)S(1)}, bf16[128,1536]{1,0:T(8,128)(2,1)}, u32[]{:S(2)}, u32[]{:S(2)}) collective-permute-start(bf16[128,1536]{1,0:T(8,128)(2,1)S(1)} %slice.291), channel_id=1, source_target_pairs={{0,1},{1,0},{2,3},{3,2},{4,5},{5,4},{6,7},{7,6},{8,9},{9,8},{10,11... | collective-permute-start | bytes 1179656 | tf_op jit(solution)/shard_map/ppermute | solution.py:66
  233.7 14.9 %collective-permute-start.40 = (bf16[128,1536]{1,0:T(8,128)(2,1)S(1)}, bf16[128,1536]{1,0:T(8,128)(2,1)S(1)}, u32[]{:S(2)}, u32[]{:S(2)}) collective-permute-start(bf16[128,1536]{1,0:T(8,128)(2,1)S(1)} %slice.292), channel_id=1, source_target_pairs={{0,4},{4,0},{1,5},{5,1},{2,6},{6,2},{3,7},{7,3},{8,12},{12,8},{9,1... | collective-permute-start | bytes 1179656 | tf_op jit(solution)/shard_map/ppermute | solution.py:66
  236.4 14.4 %collective-permute-start.48 = (bf16[128,1536]{0,1:T(8,128)(2,1)S(1)}, bf16[128,1536]{0,1:T(8,128)(2,1)S(1)}, u32[]{:S(2)}, u32[]{:S(2)}) collective-permute-start(bf16[128,1536]{0,1:T(8,128)(2,1)S(1)} %slice.293), channel_id=1, source_target_pairs={{0,1},{1,0},{2,3},{3,2},{4,5},{5,4},{6,7},{7,6},{8,9},{9,8},{10,11... | collective-permute-start | bytes 1179656 | tf_op jit(solution)/shard_map/ppermute | solution.py:66
  248.7 71.9 %collective-permute-start.43 = (bf16[256,1536]{1,0:T(8,128)(2,1)}, bf16[256,1536]{1,0:T(8,128)(2,1)}, u32[]{:S(2)}, u32[]{:S(2)}) collective-permute-start(bf16[256,1536]{1,0:T(8,128)(2,1)} %collective-permute-done.38), channel_id=1, source_target_pairs={{0,2},{2,0},{1,3},{3,1},{4,6},{6,4},{5,7},{7,5},{8,10},{10,8},{9,1... | collective-permute-start | bytes 2359304 | tf_op jit(solution)/shard_map/ppermute | solution.py:66
  250.7 62.8 %collective-permute-start.42 = (bf16[256,1536]{1,0:T(8,128)(2,1)}, bf16[256,1536]{1,0:T(8,128)(2,1)}, u32[]{:S(2)}, u32[]{:S(2)}) collective-permute-start(bf16[256,1536]{1,0:T(8,128)(2,1)} %collective-permute-done.37), channel_id=1, source_target_pairs={{0,2},{2,0},{1,3},{3,1},{4,6},{6,4},{5,7},{7,5},{8,10},{10,8},{9,1... | collective-permute-start | bytes 2359304 | tf_op jit(solution)/shard_map/ppermute | solution.py:66
  256.6 71.5 %collective-permute-start.52 = (bf16[256,1536]{0,1:T(8,128)(2,1)}, bf16[256,1536]{0,1:T(8,128)(2,1)}, u32[]{:S(2)}, u32[]{:S(2)}) collective-permute-start(bf16[256,1536]{0,1:T(8,128)(2,1)} %collective-permute-done.47), channel_id=1, source_target_pairs={{0,2},{2,0},{1,3},{3,1},{4,6},{6,4},{5,7},{7,5},{8,10},{10,8},{9,1... | collective-permute-start | bytes 2359304 | tf_op jit(solution)/shard_map/ppermute | solution.py:66
  257.5 68.2 %collective-permute-start.51 = (bf16[256,1536]{0,1:T(8,128)(2,1)}, bf16[256,1536]{0,1:T(8,128)(2,1)}, u32[]{:S(2)}, u32[]{:S(2)}) collective-permute-start(bf16[256,1536]{0,1:T(8,128)(2,1)} %collective-permute-done.46), channel_id=1, source_target_pairs={{0,2},{2,0},{1,3},{3,1},{4,6},{6,4},{5,7},{7,5},{8,10},{10,8},{9,1... | collective-permute-start | bytes 2359304 | tf_op jit(solution)/shard_map/ppermute | solution.py:66
  258.9 71.5 %collective-permute-start.44 = (bf16[128,1536]{1,0:T(8,128)(2,1)}, bf16[128,1536]{1,0:T(8,128)(2,1)}, u32[]{:S(2)}, u32[]{:S(2)}) collective-permute-start(bf16[128,1536]{1,0:T(8,128)(2,1)} %collective-permute-done.39), channel_id=1, source_target_pairs={{0,2},{2,0},{1,3},{3,1},{4,6},{6,4},{5,7},{7,5},{8,10},{10,8},{9,1... | collective-permute-start | bytes 1179656 | tf_op jit(solution)/shard_map/ppermute | solution.py:66
  269.6 65.3 %all-to-all-start = ((f32[8,1,256]{2,1,0:T(1,128)}), f32[8,1,256]{2,1,0:T(1,128)S(1)}, u32[]{:S(2)}, u32[]{:S(2)}) async-start(f32[8,1,256]{2,1,0:T(1,128)} %all_to_all.36), calls=%async_computation | async-start | bytes 16384 | tf_op jit(solution)/shard_map/all_to_all | solution.py:58
  272.9 221.6 %reduce-scatter.9.cloned.1.call-start = ((), (), s32[]{:S(2)}) async-start(), calls=%async_computation.16 | async-start | bytes 2949120 | tf_op jit(solution)/shard_map/reduce_scatter | solution.py:62
  313.5 21.5 %collective-permute-start.32 = (bf16[4,256,1536]{2,1,0:T(8,128)(2,1)}, bf16[4,256,1536]{2,1,0:T(8,128)(2,1)}, u32[]{:S(2)}, u32[]{:S(2)}) collective-permute-start(bf16[4,256,1536]{2,1,0:T(8,128)(2,1)} %bitcast.39), channel_id=1, source_target_pairs={{0,2},{2,0},{1,3},{3,1},{4,6},{6,4},{5,7},{7,5},{8,10},{10,8},{9,1... | collective-permute-start | bytes 9437192 | tf_op jit(solution)/shard_map/ppermute | solution.py:66
  339.0 19.8 %collective-permute-start.33 = (bf16[2,128,1536]{2,1,0:T(8,128)(2,1)S(1)}, bf16[2,128,1536]{2,1,0:T(8,128)(2,1)S(1)}, u32[]{:S(2)}, u32[]{:S(2)}) collective-permute-start(bf16[2,128,1536]{2,1,0:T(8,128)(2,1)S(1)} %slice_bitcast_fusion.3), channel_id=1, source_target_pairs={{0,1},{1,0},{2,3},{3,2},{4,5},{5,4},{6,7},{7,6},{8,9},{9,8},{10,11... | collective-permute-start | bytes 2359304 | tf_op jit(solution)/shard_map/ppermute | solution.py:66
  340.7 19.7 %collective-permute-start.35 = (bf16[2,128,1536]{2,1,0:T(8,128)(2,1)S(1)}, bf16[2,128,1536]{2,1,0:T(8,128)(2,1)S(1)}, u32[]{:S(2)}, u32[]{:S(2)}) collective-permute-start(bf16[2,128,1536]{2,1,0:T(8,128)(2,1)S(1)} %slice_bitcast_fusion.1), channel_id=1, source_target_pairs={{0,4},{4,0},{1,5},{5,1},{2,6},{6,2},{3,7},{7,3},{8,12},{12,8},{9,1... | collective-permute-start | bytes 2359304 | tf_op jit(solution)/shard_map/ppermute | solution.py:66
  405.7 64.2 %collective-permute-start.19 = (bf16[2,128,1536]{2,1,0:T(8,128)(2,1)}, bf16[2,128,1536]{2,1,0:T(8,128)(2,1)}, u32[]{:S(2)}, u32[]{:S(2)}) collective-permute-start(bf16[2,128,1536]{2,1,0:T(8,128)(2,1)} %slice_bitcast_fusion.7), channel_id=1, source_target_pairs={{0,1},{1,0},{2,3},{3,2},{4,5},{5,4},{6,7},{7,6},{8,9},{9,8},{10,11... | collective-permute-start | bytes 2359304 | tf_op jit(solution)/shard_map/ppermute | solution.py:66
  410.0 24.8 %all-to-all-start.2 = ((bf16[8,256,192]{1,2,0:T(8,128)(2,1)}), bf16[8,256,192]{1,2,0:T(8,128)(2,1)}, u32[]{:S(2)}, u32[]{:S(2)}) async-start(bf16[8,256,192]{1,2,0:T(8,128)(2,1)} %bitcast.282), calls=%async_computation.2 | async-start | bytes 1572864 | tf_op jit(solution)/shard_map/all_to_all | solution.py:58
  415.2 54.8 %collective-permute-start.21 = (bf16[2,128,1536]{2,1,0:T(8,128)(2,1)}, bf16[2,128,1536]{2,1,0:T(8,128)(2,1)}, u32[]{:S(2)}, u32[]{:S(2)}) collective-permute-start(bf16[2,128,1536]{2,1,0:T(8,128)(2,1)} %slice_bitcast_fusion.5), channel_id=1, source_target_pairs={{0,4},{4,0},{1,5},{5,1},{2,6},{6,2},{3,7},{7,3},{8,12},{12,8},{9,1... | collective-permute-start | bytes 2359304 | tf_op jit(solution)/shard_map/ppermute | solution.py:66
  434.8 19.1 %all-to-all-start.1 = ((bf16[8,256,256]{1,2,0:T(8,128)(2,1)}), bf16[8,256,256]{1,2,0:T(8,128)(2,1)}, u32[]{:S(2)}, u32[]{:S(2)}) async-start(bf16[8,256,256]{1,2,0:T(8,128)(2,1)} %bitcast.281), calls=%async_computation.1 | async-start | bytes 2097152 | tf_op jit(solution)/shard_map/all_to_all | solution.py:58
  439.1 71.0 %reduce-scatter.5.cloned.1.call-start = ((), (), s32[]{:S(2)}) async-start(), calls=%async_computation.14 | async-start | bytes 2007040 | tf_op jit(solution)/shard_map/reduce_scatter | solution.py:62
  473.5 19.7 %collective-permute-start.22 = (bf16[128,1536]{1,0:T(8,128)(2,1)S(1)}, bf16[128,1536]{1,0:T(8,128)(2,1)}, u32[]{:S(2)}, u32[]{:S(2)}) collective-permute-start(bf16[128,1536]{1,0:T(8,128)(2,1)S(1)} %slice_bitcast_fusion.13), channel_id=1, source_target_pairs={{0,1},{1,0},{2,3},{3,2},{4,5},{5,4},{6,7},{7,6},{8,9},{9,8},{10,11... | collective-permute-start | bytes 1179656 | tf_op jit(solution)/shard_map/ppermute | solution.py:66
  474.6 13.5 %all-to-all-start.7 = ((bf16[4,96,768]{2,1,0:T(8,128)(2,1)}), bf16[4,96,768]{2,1,0:T(8,128)(2,1)S(1)}, u32[]{:S(2)}, u32[]{:S(2)}) async-start(bf16[4,96,768]{2,1,0:T(8,128)(2,1)} %bitcast.294), calls=%async_computation.11 | async-start | bytes 1179648 | tf_op jit(solution)/shard_map/all_to_all | solution.py:58
  479.9 27.0 %collective-permute-start.20 = (bf16[128,1536]{1,0:T(8,128)(2,1)}, bf16[128,1536]{1,0:T(8,128)(2,1)}, u32[]{:S(2)}, u32[]{:S(2)}) collective-permute-start(bf16[128,1536]{1,0:T(8,128)(2,1)} %slice_bitcast_fusion.15), channel_id=1, source_target_pairs={{0,4},{4,0},{1,5},{5,1},{2,6},{6,2},{3,7},{7,3},{8,12},{12,8},{9,1... | collective-permute-start | bytes 1179656 | tf_op jit(solution)/shard_map/ppermute | solution.py:66
  488.9 13.8 %all-to-all-start.5 = ((bf16[4,96,768]{2,1,0:T(8,128)(2,1)}), bf16[4,96,768]{2,1,0:T(8,128)(2,1)}, u32[]{:S(2)}, u32[]{:S(2)}) async-start(bf16[4,96,768]{2,1,0:T(8,128)(2,1)} %bitcast.296), calls=%async_computation.7 | async-start | bytes 1179648 | tf_op jit(solution)/shard_map/all_to_all | solution.py:58
  502.7 13.8 %all-to-all-start.6 = ((bf16[4,96,768]{2,1,0:T(8,128)(2,1)}), bf16[4,96,768]{2,1,0:T(8,128)(2,1)}, u32[]{:S(2)}, u32[]{:S(2)}) async-start(bf16[4,96,768]{2,1,0:T(8,128)(2,1)} %bitcast.295), calls=%async_computation.9 | async-start | bytes 1179648 | tf_op jit(solution)/shard_map/all_to_all | solution.py:58
  516.5 17.0 %all-to-all-start.4 = ((bf16[8,98,448]{2,1,0:T(8,128)(2,1)}), bf16[8,98,448]{2,1,0:T(8,128)(2,1)}, u32[]{:S(2)}, u32[]{:S(2)}) async-start(bf16[8,98,448]{2,1,0:T(8,128)(2,1)} %pad_maximum_fusion.2), calls=%async_computation.5 | async-start | bytes 1703936 | tf_op jit(solution)/shard_map/all_to_all | solution.py:58
  (88 other events, 1605.6 us)
Sparse Core Ops, SparseCore 0:
  10.9 76.2 all-gather.2
  89.4 52.1 all-gather.4
  227.2 47.5 reduce-scatter.10
  277.0 47.5 reduce-scatter.6
  326.7 47.5 reduce-scatter.8
  470.0 34.3 reduce-scatter.4

commit v3 on v2

--- a/solution.py
+++ b/solution.py
@@ -84,9 +84,35 @@
 
 
 def late_gather(block, after):
+    block, after = lax.optimization_barrier((block, after))
+    return plane_gather(block)
+
+
+def gather_halves(halves):
+    _, rows, cols = halves.shape
+    depth = lax.axis_size("z")
     if not by_pairs():
-        block, after = lax.optimization_barrier((block, after))
-    return plane_gather(block)
+        total = gather(jnp.moveaxis(halves, 0, 1), GROUP)
+        return jnp.moveaxis(total, 1, 0)
+    z, y, c, x = (lax.axis_index(axis) for axis in ("z", "y", "c", "x"))
+    own = lax.dynamic_index_in_dim(halves, x, 0, keepdims=False)
+    column = jnp.zeros((depth, rows, cols), halves.dtype)
+    for k in range(depth):
+        piece = own
+        if k:
+            piece = lax.ppermute(own, "z", [(i, (i + k) % depth) for i in range(depth)])
+        column = lax.dynamic_update_index_in_dim(column, piece, (z - k) % depth, 0)
+    over_x, over_y = swap(column, "x"), swap(column, "y")
+    cut = depth // 2
+    near, far = swap(over_y[:cut], "x"), swap(over_x[cut:], "y")
+    total = jnp.zeros((2, depth, 2, 2, rows, cols), halves.dtype)
+    pieces = ((column, 0, 0, 0), (over_x, 0, 1, 0), (over_y, 0, 0, 1), (near, 0, 1, 1), (far, cut, 1, 1))
+    for flip in (0, 1):
+        for piece, at, dx, dy in pieces:
+            piece = swap(piece, "c") if flip else piece
+            start = (x ^ dx, at, y ^ dy, c ^ flip, 0, 0)
+            total = lax.dynamic_update_slice(total, piece[None, :, None, None], start)
+    return total.reshape(2, -1, cols)
 
 
 def add(left, right):
@@ -165,13 +191,22 @@
 
     narrow = jnp.concatenate([w_router, norm1_gain[:, None], norm2_gain[:, None]], axis=1)
     narrow = jnp.pad(narrow, ((0, 0), (0, -narrow.shape[1] % 128)))
-    packed = gather(jnp.concatenate([w_query, w_key, w_value, narrow], axis=1), GROUP)
+    narrow = gather(narrow, GROUP)
+    router_w = narrow[:, :experts_all]
+    gains = narrow[:, experts_all : experts_all + 2].T.astype(f32)
+    gain_one, gain_two = gains[0], gains[1]
     qkv_cols = q_cols + 2 * kv_cols
-    qkv_w = packed[:, :qkv_cols]
-    router_w = packed[:, qkv_cols : qkv_cols + experts_all]
-    gains = packed[:, qkv_cols + experts_all : qkv_cols + experts_all + 2].T.astype(f32)
-    gain_one, gain_two = gains[0], gains[1]
-    output_w = gather(w_out, GROUP)
+    q_group = q_cols // HK
+    qkv_w = gather_halves(
+        jnp.concatenate(
+            [
+                jnp.moveaxis(part.reshape(shard_rows, HK, -1), 1, 0)
+                for part in (w_query, w_key, w_value)
+            ],
+            axis=2,
+        )
+    )
+    output_w = gather_halves(jnp.moveaxis(w_out.reshape(shard_rows, 2, -1), 1, 0))
 
     ids_all = plane_gather(expert_ids)
     cot_all = plane_gather(out_grad)
@@ -188,16 +223,14 @@
     cosine_tab, sine_tab = angles(length, HD)
     inputs_f = tokens.astype(f32)
     first_in = rms_scale(inputs_f, gain_one).astype(bf16)
-    qkv = jnp.dot(first_in, qkv_w, preferred_element_type=f32)
+    qkv = jnp.einsum("id,gde->ige", first_in, qkv_w, preferred_element_type=f32)
     queries = (
-        rotary(qkv[:, :q_cols].reshape(length, HQ, HD), cosine_tab, sine_tab)
+        rotary(qkv[:, :, :q_group].reshape(length, HQ, HD), cosine_tab, sine_tab)
         .astype(bf16)
         .reshape(length, HK, group_size, HD)
     )
-    keys_rot = rotary(
-        qkv[:, q_cols : q_cols + kv_cols].reshape(length, HK, HD), cosine_tab, sine_tab
-    ).astype(bf16)
-    values_b = qkv[:, q_cols + kv_cols :].astype(bf16).reshape(length, HK, HD)
+    keys_rot = rotary(qkv[:, :, q_group : q_group + HD], cosine_tab, sine_tab).astype(bf16)
+    values_b = qkv[:, :, q_group + HD :].astype(bf16)
     positions = jnp.arange(length)
     allowed = (positions[None, :] <= positions[:, None]) | (positions[None, :] < prefix_len[0])
 
@@ -211,7 +244,8 @@
     prob_bf = jnp.exp(masked - log_total).astype(bf16)
     attended = jnp.einsum("hrij,jhd->ihrd", prob_bf, values_b, preferred_element_type=f32)
     attended = attended.reshape(length, HQ * HD).astype(bf16)
-    resid = inputs_f + jnp.dot(attended, output_w, preferred_element_type=f32)
+    branch = jnp.einsum("ie,hed->ihd", attended, output_w, preferred_element_type=f32)
+    resid = inputs_f + branch.reshape(length, model_width)
     second_in = rms_scale(resid, gain_two).astype(bf16)
 
     second_all = plane_gather(second_in)
@@ -288,10 +322,12 @@
     resid_grad = cotangent + resid_norm_grad
     branch_grad = resid_grad.astype(bf16)
 
-    attended_all = late_gather(attended, branch_grad)
+    attended_all = late_gather(attended, second_all if by_pairs() else branch_grad)
     branch_cols = by_source(branch_grad)
     output_part = left_product(attended_all, branch_cols)
-    attended_grad = jnp.dot(branch_grad, output_w.T, preferred_element_type=f32).astype(bf16)
+    attended_grad = jnp.einsum(
+        "ihd,hed->ie", branch_grad.reshape(length, 2, -1), output_w, preferred_element_type=f32
+    ).astype(bf16)
     attended_grad = attended_grad.reshape(length, HK, group_size, HD)
     masked = masked_scores()
     prob_full = jnp.exp(masked - log_total)
@@ -304,20 +340,17 @@
         * score_scale
     )
     query_back = rotary(query_rot_grad.reshape(length, HQ, HD), cosine_tab, -sine_tab)
-    query_back = query_back.astype(bf16).reshape(length, HQ * HD)
+    query_back = query_back.astype(bf16).reshape(length, HK, q_group)
     key_rot_grad = (
         jnp.einsum("hrij,ihrd->jhd", score_grad, queries, preferred_element_type=f32)
         * score_scale
     )
-    key_back = rotary(key_rot_grad, cosine_tab, -sine_tab).astype(bf16).reshape(length, HK * HD)
+    key_back = rotary(key_rot_grad, cosine_tab, -sine_tab).astype(bf16)
     value_back = jnp.einsum("hrij,ihrd->jhd", prob_bf, attended_grad, preferred_element_type=f32)
-    value_back = value_back.astype(bf16).reshape(length, HK * HD)
-    qkv_back = jnp.concatenate([query_back, key_back, value_back], axis=1)
-    first_all = late_gather(first_in, output_part)
-    qkv_part = left_product(first_all, by_source(qkv_back))
-    first_grad = lax.dot_general(
-        qkv_back, qkv_w, (((1,), (1,)), ((), ())), preferred_element_type=f32
-    )
+    qkv_back = jnp.concatenate([query_back, key_back, value_back.astype(bf16)], axis=2)
+    first_all = late_gather(first_in, second_all if by_pairs() else output_part)
+    qkv_part = left_product(first_all, by_source(qkv_back.reshape(length, qkv_cols)))
+    first_grad = jnp.einsum("ige,gde->id", qkv_back, qkv_w, preferred_element_type=f32)
     _, norm_one_pull = jax.vjp(rms_scale, inputs_f, gain_one)
     input_norm_grad, gain_one_grad = norm_one_pull(first_grad)
     tokens_grad = (resid_grad + input_norm_grad).astype(bf16)
@@ -357,7 +390,7 @@
     narrow_sum = jnp.broadcast_to(narrow_sum[None], (plane, narrow_rows, dense_cols))
     dense_sum = exchange(jnp.concatenate([wide_sum, narrow_sum], axis=1), PLANE)
     wide_sum = jnp.moveaxis(dense_sum[:, :shard_rows].astype(f32), 0, 1)
-    qkv_sum = wide_sum[:, :, :qkv_width].reshape(shard_rows, qkv_cols)
+    qkv_sum = wide_sum[:, :, :qkv_width].reshape(shard_rows, HK, qkv_cols // HK)
     output_sum = wide_sum[:, :, qkv_width:].reshape(shard_rows, model_width)
     narrow_sum = dense_sum[:, shard_rows:].reshape(2, 2, owners, narrow_rows * dense_cols)
     narrow_sum = narrow_sum[lax.axis_index("c"), lax.axis_index("y"), :, :narrow_len]
@@ -373,9 +406,9 @@
         block_out,
         tokens_grad,
         narrow_sum[:, experts_all],
-        qkv_sum[:, :q_cols],
-        qkv_sum[:, q_cols : q_cols + kv_cols],
-        qkv_sum[:, q_cols + kv_cols :],
+        qkv_sum[:, :, :q_group].reshape(shard_rows, q_cols),
+        qkv_sum[:, :, q_group : q_group + HD].reshape(shard_rows, kv_cols),
+        qkv_sum[:, :, q_group + HD :].reshape(shard_rows, kv_cols),
         output_sum,
         narrow_sum[:, experts_all + 1],
         narrow_sum[:, :experts_all],

time: 559 us -> 610 us (1.091)
  local copies, waits for them, and re-layouts: 91.8 us -> 155 us
  waiting for transfers between devices: 177 us -> 136 us
  blocking collectives: 0 us -> 19.2 us
  starting transfers between devices: 72 us -> 90.8 us
  matrix products: 137 us -> 130 us
    all_gather x2 -> x0, waiting for transfers between devices: 47.7 us -> none  [gather(): return lax.all_gather(block, axes, axis=0, tiled=True)]
    all_gather x0 -> x1, blocking collectives: none -> 19.2 us  [gather(): return lax.all_gather(block, axes, axis=0, tiled=True)]
    dynamic_update_slice x0 -> x27, local copies, waits for them, and re-layouts: none -> 18.9 us  [the longest x20 14.3 us: gather_halves(): total = lax.dynamic_update_slice(total, piece[None, :, None, None], start)]
    ppermute x55 -> x73, starting transfers between devices: 39.8 us -> 51.1 us  [swap(): return lax.ppermute(block, axis, [(0, 1), (1, 0)])]
    unnamed x179 -> x229, local copies, waits for them, and re-layouts: 45.1 us -> 56.2 us
    ppermute x0 -> x6, starting transfers between devices: none -> 7.92 us  [gather_halves(): piece = lax.ppermute(own, 'z', [(i, (i + k) % depth) for i in range(depth)])]
    reshape x3 -> x7, local copies, waits for them, and re-layouts: 0.89 us -> 8.48 us  [the longest x3 4 us: local(): part.reshape(shard_rows, HK, -1)]
    dot_general x0 -> x1, local copies, waits for them, and re-layouts: none -> 6.9 us  [local(): jnp.einsum('ie,hed->ihd', attended, output_w, preferred_element_type=f32)]
  transfers between devices with their start and end apart: 69 -> 91, of which waited for: 25 -> 36; matrix products, arithmetic and copies ran while one was open for 47% -> 45% of each run, Pallas kernels for 0% -> 0%
where the time goes in v3:
time: 610 us; the launch traced here: 599 us
  local copies, waits for them, and re-layouts  155 us (25%)
  waiting for transfers between devices  136 us (22%)
  matrix products  130 us (21%)
  starting transfers between devices  90.8 us (15%)
  other arithmetic  52.3 us (9%)
  blocking collectives  19.2 us (3%)
  between operations  16.5 us (3%)
    ppermute x73, waiting for transfers between devices, swap(): return lax.ppermute(block, axis, [(0, 1), (1, 0)])  96.1 us
    unnamed x229, local copies, waits for them, and re-layouts  56.2 us
    ppermute x73, starting transfers between devices, swap(): return lax.ppermute(block, axis, [(0, 1), (1, 0)])  51.1 us
    all_to_all x8, waiting for transfers between devices, exchange(): return lax.all_to_all(block, axes, split_axis=0, concat_axis=0, tiled=True)  36.9 us
    all_to_all x8, starting transfers between devices, exchange(): return lax.all_to_all(block, axes, split_axis=0, concat_axis=0, tiled=True)  31.7 us
    all_gather x1, blocking collectives, gather(): return lax.all_gather(block, axes, axis=0, tiled=True)  19.2 us
    dynamic_update_slice x20, local copies, waits for them, and re-layouts, gather_halves(): total = lax.dynamic_update_slice(total, piece[None, :, None, None], start)  14.3 us
    dot_general x1, matrix products, local(): jnp.einsum('bcd,df->bcf', rows_in, gate_w, preferred_element_type=f32)  13.5 us
  transfers between devices with their start and end apart: 91, of which 36 were waited for; matrix products, arithmetic and copies ran while one was open for 45% of the time, Pallas kernels for 0%

profile of v3, /device:TPU:0, one launch (start us, length us, event | category | flops | bytes accessed | tf_op | source)
XLA Modules:
  0.0 599.1 jit_solution(4491567290327311994)
XLA Ops:
  7.2 3.0 collective-permute-start.25
  13.8 3.6 collective-permute-start.14
  26.9 19.2 %all_gather.3 = bf16[1536,128]{1,0:T(8,128)(2,1)S(1)} all-gather(bf16[96,128]{1,0:T(8,128)(2,1)S(1)} %pad.9), channel_id=1, replica_groups=mesh['z'=4,'y'=2,'c'=2,'x'=2] {'z','y','c'}, dimensions={0}, use_global_device_ids=true | all-gather | bytes 417792 | tf_op jit(solution)/shard_map/all_gather | solution.py:54
  61.1 3.7 collective-permute-start.2
  88.8 19.3 %collective-permute-done.15 = bf16[4,96,768]{2,1,0:T(8,128)(2,1)S(1)} collective-permute-done((bf16[4,96,768]{2,1,0:T(8,128)(2,1)S(1)}, bf16[4,96,768]{2,1,0:T(8,128)(2,1)S(1)}, u32[]{:S(2)}, u32[]{:S(2)}) %collective-permute-start.15) | collective-permute-done | bytes 589856 | tf_op jit(solution)/shard_map/ppermute | solution.py:66
  118.4 7.6 %collective-permute-done.3 = bf16[4,96,1024]{2,1,0:T(8,128)(2,1)S(1)} collective-permute-done((bf16[4,96,1024]{2,1,0:T(8,128)(2,1)S(1)}, bf16[4,96,1024]{2,1,0:T(8,128)(2,1)S(1)}, u32[]{:S(2)}, u32[]{:S(2)}) %collective-permute-start.3) | collective-permute-done | bytes 786464 | tf_op jit(solution)/shard_map/ppermute | solution.py:66
  138.1 6.9 %collective-permute-done.49 = bf16[128,1536]{1,0:T(8,128)(2,1)S(1)} collective-permute-done((bf16[128,1536]{1,0:T(8,128)(2,1)S(1)}, bf16[128,1536]{1,0:T(8,128)(2,1)S(1)}, u32[]{:S(2)}, u32[]{:S(2)}) %collective-permute-start.49) | collective-permute-done | bytes 393248 | tf_op jit(solution)/shard_map/ppermute | solution.py:66
  154.6 6.9 %copy.461 = bf16[2,768,1536]{2,1,0:T(8,128)(2,1)} copy(bf16[2,768,1536]{1,2,0:T(8,128)(2,1)} %bitcast.65) | data formatting | bytes 9437184 | tf_op jit(solution)/shard_map/ie,hed->ihd/dot_general | solution.py:247
  175.1 6.8 %convolution_convert_fusion.1 = bf16[16,96,1536]{2,1,0:T(8,128)(2,1)} fusion(bf16[16,128,1536]{2,1,0:T(8,128)(2,1)} %bitcast.396, s32[16,128]{1,0:T(8,128)S(1)} %broadcast_add_fusion, pred[16,128]{1,0:T(8,128)(4,1)S(1)} %bitcast.441), kind=kOutput, calls=%fused_computation.21 | convolution fusion | flops 606732288 | bytes 11020288 | tf_op jit(solution)/shard_map/bct,btd->bcd/dot_general | solution.py:264
  186.2 3.1 copy.446
  199.7 4.1 multiply_reduce_fusion.3
  206.5 5.6 fusion.18
  212.1 11.5 %collective-permute-done.34 = bf16[256,1536]{1,0:T(8,128)(2,1)S(1)} collective-permute-done((bf16[256,1536]{1,0:T(8,128)(2,1)S(1)}, bf16[256,1536]{1,0:T(8,128)(2,1)S(1)}, u32[]{:S(2)}, u32[]{:S(2)}) %collective-permute-start.34) | collective-permute-done | bytes 786464 | tf_op jit(solution)/shard_map/ppermute | solution.py:66
  227.0 6.9 %collective-permute-done.35 = bf16[128,1536]{1,0:T(8,128)(2,1)S(1)} collective-permute-done((bf16[128,1536]{1,0:T(8,128)(2,1)S(1)}, bf16[128,1536]{1,0:T(8,128)(2,1)S(1)}, u32[]{:S(2)}, u32[]{:S(2)}) %collective-permute-start.35) | collective-permute-done | bytes 393248 | tf_op jit(solution)/shard_map/ppermute | solution.py:66
  240.8 6.5 %fusion.22 = f32[16,96,768]{2,1,0:T(8,128)S(1)} fusion(bf16[16,96,1536]{2,1,0:T(8,128)(2,1)S(1)} %convolution_convert_fusion.2, bf16[4,1536,768]{2,1,0:T(8,128)(2,1)} %param.23, s32[]{:T(128)S(6)} %select_n.220), kind=kOutput, calls=%fused_computation.58 | convolution fusion | flops 3623878656 | bytes 11796484 | tf_op jit(solution)/shard_map/bcd,df->bcf/dot_general | solution.py:284
  247.3 13.5 %fusion.8 = (bf16[16,96,768]{2,1,0:T(8,128)(2,1)}, f32[16,96]{1,0:T(8,128)}, bf16[16,96,768]{2,1,0:T(8,128)(2,1)}, f32[16,96,768]{2,1,0:T(8,128)S(1)}) fusion(f32[16,96,768]{2,1,0:T(8,128)S(1)} %fusion.22, f32[16,96,768]{2,1,0:T(8,128)S(1)} %fusion.18, f32[16,96]{1,0:T(8,128)S(1)} %bitcast.453, bf16[16,96,1536]{2,1,0:T(8,128)(2,1)S(1)} %convolution_convert_fusion.2, ...), kind=kOutput, calls=%fused_computation.13 | convolution fusion | flops 3656907264 | bytes 25964548 | tf_op jit(solution)/shard_map/bcd,df->bcf/dot_general | solution.py:283
  262.9 5.9 bitcast_convert_fusion
  284.3 3.8 all-to-all-start
  290.5 9.5 %convolution_convert_fusion = bf16[16,96,1536]{2,1,0:T(8,128)(2,1)S(1)} fusion(bf16[4,768,1536]{2,1,0:T(8,128)(2,1)} %param.24, s32[]{:T(128)S(6)} %select_n.220, f32[16,96]{1,0:T(8,128)} %bitcast.455, f32[16,96,768]{2,1,0:T(8,128)} %copy-done.77, f32[16,96,768]{2,1,0:T(8,128)} %copy-done.78), kind=kOutput, calls=%fused_computation.20 | convolution fusion | flops 3639214080 | bytes 16523268 | tf_op jit(solution)/shard_map/bcf,fd->bcd/dot_general | solution.py:308
  303.4 5.4 bitcast_convert_fusion.2
  308.9 4.6 convolution_convert_fusion.6
  313.4 5.7 fusion.24
  319.2 5.8 add_convert_fusion
  330.6 5.7 bitcast_convert_fusion.1
  366.6 3.2 collective-permute-done.64
  375.5 4.3 collective-permute-done.73
  393.5 14.1 %collective-permute-done.57 = bf16[2,128,1536]{2,1,0:T(8,128)(2,1)S(1)} collective-permute-done((bf16[2,128,1536]{2,1,0:T(8,128)(2,1)S(1)}, bf16[2,128,1536]{2,1,0:T(8,128)(2,1)S(1)}, u32[]{:S(2)}, u32[]{:S(2)}) %collective-permute-start.57) | collective-permute-done | bytes 786464 | tf_op jit(solution)/shard_map/ppermute | solution.py:66
  411.4 7.3 %collective-permute-done.60 = bf16[128,1536]{1,0:T(8,128)(2,1)S(1)} collective-permute-done((bf16[128,1536]{1,0:T(8,128)(2,1)S(1)}, bf16[128,1536]{1,0:T(8,128)(2,1)S(1)}, u32[]{:S(2)}, u32[]{:S(2)}) %collective-permute-start.60) | collective-permute-done | bytes 393248 | tf_op jit(solution)/shard_map/ppermute | solution.py:66
  423.1 4.6 fusion.12
  441.8 7.3 %fusion.38 = (f32[1536]{0:T(1024)S(1)}, f32[256]{0:T(256)}, f32[256,1536]{1,0:T(8,128)}) fusion(bf16[256,1536]{1,0:T(8,128)(2,1)S(1)} %copy-done.15, f32[256]{0:T(256)S(1)} %copy-done.72, f32[1536]{0:T(1024)S(1)} %copy-done.56, bf16[256,2,1024]{2,0,1:T(8,128)(2,1)S(1)} %pad_maximum_fusion.1, bf16[2,1536,1024]{2,1,0:T(8,128)(2,1)} %bitcast.389), kind=kOutput, calls=%fused_computation.76 | convolution fusion | flops 1613363456 | bytes 9713664 | tf_op jit(solution)/shard_map/ige,gde->id/dot_general | solution.py:353
  451.2 3.4 all-to-all-start.3
  454.5 3.7 fusion.1
  460.6 4.2 all-to-all-start.2
  472.4 4.6 all-to-all-done.2
  477.0 4.2 all-to-all-start.1
  484.8 3.1 reshape_reshape.15
  488.0 6.0 convolution_convert_fusion.8
  493.9 11.1 %all-to-all-done.1 = bf16[8,256,256]{1,2,0:T(8,128)(2,1)} async-done(((bf16[8,256,256]{1,2,0:T(8,128)(2,1)}), bf16[8,256,256]{1,2,0:T(8,128)(2,1)}, u32[]{:S(2)}, u32[]{:S(2)}) %all-to-all-start.1) | async-done | bytes 1048608 | tf_op jit(solution)/shard_map/all_to_all | solution.py:58
  509.5 4.7 convolution_convert_fusion.7
  525.5 3.5 all-to-all-start.7
  532.7 6.2 %all-to-all-done.7 = bf16[4,96,768]{2,1,0:T(8,128)(2,1)S(1)} async-done(((bf16[4,96,768]{2,1,0:T(8,128)(2,1)}), bf16[4,96,768]{2,1,0:T(8,128)(2,1)S(1)}, u32[]{:S(2)}, u32[]{:S(2)}) %all-to-all-start.7) | async-done | bytes 589856 | tf_op jit(solution)/shard_map/all_to_all | solution.py:58
  539.8 4.2 all-to-all-start.5
  545.4 8.2 %all-to-all-done.5 = bf16[4,96,768]{2,1,0:T(8,128)(2,1)} async-done(((bf16[4,96,768]{2,1,0:T(8,128)(2,1)}), bf16[4,96,768]{2,1,0:T(8,128)(2,1)}, u32[]{:S(2)}, u32[]{:S(2)}) %all-to-all-start.5) | async-done | bytes 589856 | tf_op jit(solution)/shard_map/all_to_all | solution.py:58
  553.5 4.2 all-to-all-start.6
  563.8 3.5 all-to-all-done.6
  567.3 4.2 all-to-all-start.4
  571.6 4.0 fusion.41
  581.0 3.3 all-to-all-done.4
  (587 shorter events, 280.9 us)
Async XLA Ops:
  7.2 518.3 %reduce-scatter.11.cloned.1.call-start = ((), (), s32[]{:S(2)}) async-start(), calls=%async_computation.15 | async-start | bytes 2949120 | tf_op jit(solution)/shard_map/reduce_scatter | solution.py:62
  7.2 46.6 %collective-permute-start.25 = (s32[256,4]{0,1:T(4,128)}, s32[256,4]{0,1:T(4,128)S(1)}, u32[]{:S(2)}, u32[]{:S(2)}) collective-permute-start(s32[256,4]{0,1:T(4,128)} %param.25), channel_id=1, source_target_pairs={{0,4},{4,0},{1,5},{5,1},{2,6},{6,2},{3,7},{7,3},{8,12},{12,8},{9,1... | collective-permute-start | bytes 12296 | tf_op jit(solution)/shard_map/ppermute | solution.py:66
  10.3 43.6 %collective-permute-start.24 = (s32[256,4]{0,1:T(4,128)}, s32[256,4]{0,1:T(4,128)S(1)}, u32[]{:S(2)}, u32[]{:S(2)}) collective-permute-start(s32[256,4]{0,1:T(4,128)} %param.25), channel_id=1, source_target_pairs={{0,1},{1,0},{2,3},{3,2},{4,5},{5,4},{6,7},{7,6},{8,9},{9,8},{10,11... | collective-permute-start | bytes 12296 | tf_op jit(solution)/shard_map/ppermute | solution.py:66
  11.8 53.7 %collective-permute-start.28 = (s32[256,4]{0,1:T(4,128)}, s32[256,4]{0,1:T(4,128)S(1)}, u32[]{:S(2)}, u32[]{:S(2)}) collective-permute-start(s32[256,4]{0,1:T(4,128)} %param.25), channel_id=1, source_target_pairs={{0,2},{2,0},{1,3},{3,1},{4,6},{6,4},{5,7},{7,5},{8,10},{10,8},{9,1... | collective-permute-start | bytes 12296 | tf_op jit(solution)/shard_map/ppermute | solution.py:66
  13.8 62.8 %collective-permute-start.14 = (bf16[96,768]{1,0:T(8,128)(2,1)}, bf16[96,768]{1,0:T(8,128)(2,1)}, u32[]{:S(2)}, u32[]{:S(2)}) collective-permute-start(bf16[96,768]{1,0:T(8,128)(2,1)} %bitcast.381), channel_id=1, source_target_pairs={{0,24},{8,0},{16,8},{24,16},{1,25},{9,1},{17,9},{25,17},{2,26},{10... | collective-permute-start | bytes 442376 | tf_op jit(solution)/shard_map/ppermute | solution.py:103
  17.4 57.3 %collective-permute-start.13 = (bf16[96,768]{1,0:T(8,128)(2,1)}, bf16[96,768]{1,0:T(8,128)(2,1)}, u32[]{:S(2)}, u32[]{:S(2)}) collective-permute-start(bf16[96,768]{1,0:T(8,128)(2,1)} %bitcast.381), channel_id=1, source_target_pairs={{0,16},{8,24},{16,0},{24,8},{1,17},{9,25},{17,1},{25,9},{2,18},{10... | collective-permute-start | bytes 442376 | tf_op jit(solution)/shard_map/ppermute | solution.py:103
  53.8 19.3 %collective-permute-start.12 = (bf16[96,768]{1,0:T(8,128)(2,1)}, bf16[96,768]{1,0:T(8,128)(2,1)}, u32[]{:S(2)}, u32[]{:S(2)}) collective-permute-start(bf16[96,768]{1,0:T(8,128)(2,1)} %bitcast.381), channel_id=1, source_target_pairs={{0,8},{8,16},{16,24},{24,0},{1,9},{9,17},{17,25},{25,1},{2,10},{10... | collective-permute-start | bytes 442376 | tf_op jit(solution)/shard_map/ppermute | solution.py:103
  61.1 24.8 %collective-permute-start.2 = (bf16[96,1024]{1,0:T(8,128)(2,1)}, bf16[96,1024]{1,0:T(8,128)(2,1)}, u32[]{:S(2)}, u32[]{:S(2)}) collective-permute-start(bf16[96,1024]{1,0:T(8,128)(2,1)} %get-tuple-element.43), channel_id=1, source_target_pairs={{0,24},{8,0},{16,8},{24,16},{1,25},{9,1},{17,9},{25,17},{2,26},{10... | collective-permute-start | bytes 589832 | tf_op jit(solution)/shard_map/ppermute | solution.py:103
  70.1 14.3 %collective-permute-start.1 = (bf16[96,1024]{1,0:T(8,128)(2,1)}, bf16[96,1024]{1,0:T(8,128)(2,1)}, u32[]{:S(2)}, u32[]{:S(2)}) collective-permute-start(bf16[96,1024]{1,0:T(8,128)(2,1)} %get-tuple-element.43), channel_id=1, source_target_pairs={{0,16},{8,24},{16,0},{24,8},{1,17},{9,25},{17,1},{25,9},{2,18},{10... | collective-permute-start | bytes 589832 | tf_op jit(solution)/shard_map/ppermute | solution.py:103
  74.7 36.9 %collective-permute-start.48 = (bf16[256,1536]{1,0:T(8,128)(2,1)S(1)}, bf16[256,1536]{1,0:T(8,128)(2,1)}, u32[]{:S(2)}, u32[]{:S(2)}) collective-permute-start(bf16[256,1536]{1,0:T(8,128)(2,1)S(1)} %copy-done.16), channel_id=1, source_target_pairs={{0,4},{4,0},{1,5},{5,1},{2,6},{6,2},{3,7},{7,3},{8,12},{12,8},{9,1... | collective-permute-start | bytes 2359304 | tf_op jit(solution)/shard_map/ppermute | solution.py:66
  76.6 36.0 %collective-permute-start.47 = (bf16[256,1536]{1,0:T(8,128)(2,1)S(1)}, bf16[256,1536]{1,0:T(8,128)(2,1)}, u32[]{:S(2)}, u32[]{:S(2)}) collective-permute-start(bf16[256,1536]{1,0:T(8,128)(2,1)S(1)} %copy-done.16), channel_id=1, source_target_pairs={{0,1},{1,0},{2,3},{3,2},{4,5},{5,4},{6,7},{7,6},{8,9},{9,8},{10,11... | collective-permute-start | bytes 2359304 | tf_op jit(solution)/shard_map/ppermute | solution.py:66
  82.3 64.8 %collective-permute-start.51 = (bf16[256,1536]{1,0:T(8,128)(2,1)S(1)}, bf16[256,1536]{1,0:T(8,128)(2,1)S(1)}, u32[]{:S(2)}, u32[]{:S(2)}) collective-permute-start(bf16[256,1536]{1,0:T(8,128)(2,1)S(1)} %copy-done.16), channel_id=1, source_target_pairs={{0,2},{2,0},{1,3},{3,1},{4,6},{6,4},{5,7},{7,5},{8,10},{10,8},{9,1... | collective-permute-start | bytes 2359304 | tf_op jit(solution)/shard_map/ppermute | solution.py:66
  84.4 23.7 %collective-permute-start.15 = (bf16[4,96,768]{2,1,0:T(8,128)(2,1)S(1)}, bf16[4,96,768]{2,1,0:T(8,128)(2,1)S(1)}, u32[]{:S(2)}, u32[]{:S(2)}) collective-permute-start(bf16[4,96,768]{2,1,0:T(8,128)(2,1)S(1)} %bitcast_dynamic-update-slice_fusion.24), channel_id=1, source_target_pairs={{0,1},{1,0},{2,3},{3,2},{4,5},{5,4},{6,7},{7,6},{8,9},{9,8},{10,11... | collective-permute-start | bytes 1769480 | tf_op jit(solution)/shard_map/ppermute | solution.py:66
  85.9 23.6 %collective-permute-start.16 = (bf16[4,96,768]{2,1,0:T(8,128)(2,1)S(1)}, bf16[4,96,768]{2,1,0:T(8,128)(2,1)S(1)}, u32[]{:S(2)}, u32[]{:S(2)}) collective-permute-start(bf16[4,96,768]{2,1,0:T(8,128)(2,1)S(1)} %bitcast_dynamic-update-slice_fusion.24), channel_id=1, source_target_pairs={{0,4},{4,0},{1,5},{5,1},{2,6},{6,2},{3,7},{7,3},{8,12},{12,8},{9,1... | collective-permute-start | bytes 1769480 | tf_op jit(solution)/shard_map/ppermute | solution.py:66
  108.1 17.9 %collective-permute-start.3 = (bf16[4,96,1024]{2,1,0:T(8,128)(2,1)S(1)}, bf16[4,96,1024]{2,1,0:T(8,128)(2,1)S(1)}, u32[]{:S(2)}, u32[]{:S(2)}) collective-permute-start(bf16[4,96,1024]{2,1,0:T(8,128)(2,1)S(1)} %bitcast_dynamic-update-slice_fusion.20), channel_id=1, source_target_pairs={{0,1},{1,0},{2,3},{3,2},{4,5},{5,4},{6,7},{7,6},{8,9},{9,8},{10,11... | collective-permute-start | bytes 2359304 | tf_op jit(solution)/shard_map/ppermute | solution.py:66
  109.5 17.7 %collective-permute-start.4 = (bf16[4,96,1024]{2,1,0:T(8,128)(2,1)S(1)}, bf16[4,96,1024]{2,1,0:T(8,128)(2,1)S(1)}, u32[]{:S(2)}, u32[]{:S(2)}) collective-permute-start(bf16[4,96,1024]{2,1,0:T(8,128)(2,1)S(1)} %bitcast_dynamic-update-slice_fusion.20), channel_id=1, source_target_pairs={{0,4},{4,0},{1,5},{5,1},{2,6},{6,2},{3,7},{7,3},{8,12},{12,8},{9,1... | collective-permute-start | bytes 2359304 | tf_op jit(solution)/shard_map/ppermute | solution.py:66
  111.5 24.7 %collective-permute-start.19 = (bf16[4,96,768]{2,1,0:T(8,128)(2,1)S(1)}, bf16[4,96,768]{2,1,0:T(8,128)(2,1)S(1)}, u32[]{:S(2)}, u32[]{:S(2)}) collective-permute-start(bf16[4,96,768]{2,1,0:T(8,128)(2,1)S(1)} %bitcast_dynamic-update-slice_fusion.24), channel_id=1, source_target_pairs={{0,2},{2,0},{1,3},{3,1},{4,6},{6,4},{5,7},{7,5},{8,10},{10,8},{9,1... | collective-permute-start | bytes 1769480 | tf_op jit(solution)/shard_map/ppermute | solution.py:66
  112.7 53.6 %collective-permute-start.7 = (bf16[4,96,1024]{2,1,0:T(8,128)(2,1)S(1)}, bf16[4,96,1024]{2,1,0:T(8,128)(2,1)}, u32[]{:S(2)}, u32[]{:S(2)}) collective-permute-start(bf16[4,96,1024]{2,1,0:T(8,128)(2,1)S(1)} %bitcast_dynamic-update-slice_fusion.20), channel_id=1, source_target_pairs={{0,2},{2,0},{1,3},{3,1},{4,6},{6,4},{5,7},{7,5},{8,10},{10,8},{9,1... | collective-permute-start | bytes 2359304 | tf_op jit(solution)/shard_map/ppermute | solution.py:66
  132.7 16.7 %collective-permute-start.21 = (bf16[4,96,768]{2,1,0:T(8,128)(2,1)S(1)}, bf16[4,96,768]{2,1,0:T(8,128)(2,1)S(1)}, u32[]{:S(2)}, u32[]{:S(2)}) collective-permute-start(bf16[4,96,768]{2,1,0:T(8,128)(2,1)S(1)} %collective-permute-done.16), channel_id=1, source_target_pairs={{0,2},{2,0},{1,3},{3,1},{4,6},{6,4},{5,7},{7,5},{8,10},{10,8},{9,1... | collective-permute-start | bytes 1769480 | tf_op jit(solution)/shard_map/ppermute | solution.py:66
  146.0 24.9 %collective-permute-start.53 = (bf16[256,1536]{1,0:T(8,128)(2,1)}, bf16[256,1536]{1,0:T(8,128)(2,1)}, u32[]{:S(2)}, u32[]{:S(2)}) collective-permute-start(bf16[256,1536]{1,0:T(8,128)(2,1)} %collective-permute-done.48), channel_id=1, source_target_pairs={{0,2},{2,0},{1,3},{3,1},{4,6},{6,4},{5,7},{7,5},{8,10},{10,8},{9,1... | collective-permute-start | bytes 2359304 | tf_op jit(solution)/shard_map/ppermute | solution.py:66
  147.1 21.3 %collective-permute-start.52 = (bf16[256,1536]{1,0:T(8,128)(2,1)}, bf16[256,1536]{1,0:T(8,128)(2,1)}, u32[]{:S(2)}, u32[]{:S(2)}) collective-permute-start(bf16[256,1536]{1,0:T(8,128)(2,1)} %collective-permute-done.47), channel_id=1, source_target_pairs={{0,2},{2,0},{1,3},{3,1},{4,6},{6,4},{5,7},{7,5},{8,10},{10,8},{9,1... | collective-permute-start | bytes 2359304 | tf_op jit(solution)/shard_map/ppermute | solution.py:66
  162.1 19.9 %collective-permute-start.9 = (bf16[4,96,1024]{2,1,0:T(8,128)(2,1)S(1)}, bf16[4,96,1024]{2,1,0:T(8,128)(2,1)S(1)}, u32[]{:S(2)}, u32[]{:S(2)}) collective-permute-start(bf16[4,96,1024]{2,1,0:T(8,128)(2,1)S(1)} %copy-done.31), channel_id=1, source_target_pairs={{0,2},{2,0},{1,3},{3,1},{4,6},{6,4},{5,7},{7,5},{8,10},{10,8},{9,1... | collective-permute-start | bytes 2359304 | tf_op jit(solution)/shard_map/ppermute | solution.py:66
  164.0 18.0 %collective-permute-start.8 = (bf16[4,96,1024]{2,1,0:T(8,128)(2,1)S(1)}, bf16[4,96,1024]{2,1,0:T(8,128)(2,1)S(1)}, u32[]{:S(2)}, u32[]{:S(2)}) collective-permute-start(bf16[4,96,1024]{2,1,0:T(8,128)(2,1)S(1)} %copy-done.29), channel_id=1, source_target_pairs={{0,2},{2,0},{1,3},{3,1},{4,6},{6,4},{5,7},{7,5},{8,10},{10,8},{9,1... | collective-permute-start | bytes 2359304 | tf_op jit(solution)/shard_map/ppermute | solution.py:66
  204.1 19.5 %collective-permute-start.34 = (bf16[256,1536]{1,0:T(8,128)(2,1)S(1)}, bf16[256,1536]{1,0:T(8,128)(2,1)S(1)}, u32[]{:S(2)}, u32[]{:S(2)}) collective-permute-start(bf16[256,1536]{1,0:T(8,128)(2,1)S(1)} %get-tuple-element.23), channel_id=1, source_target_pairs={{0,4},{4,0},{1,5},{5,1},{2,6},{6,2},{3,7},{7,3},{8,12},{12,8},{9,1... | collective-permute-start | bytes 2359304 | tf_op jit(solution)/shard_map/ppermute | solution.py:66
  205.2 19.8 %collective-permute-start.33 = (bf16[256,1536]{1,0:T(8,128)(2,1)S(1)}, bf16[256,1536]{1,0:T(8,128)(2,1)S(1)}, u32[]{:S(2)}, u32[]{:S(2)}) collective-permute-start(bf16[256,1536]{1,0:T(8,128)(2,1)S(1)} %get-tuple-element.23), channel_id=1, source_target_pairs={{0,1},{1,0},{2,3},{3,2},{4,5},{5,4},{6,7},{7,6},{8,9},{9,8},{10,11... | collective-permute-start | bytes 2359304 | tf_op jit(solution)/shard_map/ppermute | solution.py:66
  212.1 23.0 %collective-permute-start.37 = (bf16[256,1536]{1,0:T(8,128)(2,1)S(1)}, bf16[256,1536]{1,0:T(8,128)(2,1)S(1)}, u32[]{:S(2)}, u32[]{:S(2)}) collective-permute-start(bf16[256,1536]{1,0:T(8,128)(2,1)S(1)} %get-tuple-element.23), channel_id=1, source_target_pairs={{0,2},{2,0},{1,3},{3,1},{4,6},{6,4},{5,7},{7,5},{8,10},{10,8},{9,1... | collective-permute-start | bytes 2359304 | tf_op jit(solution)/shard_map/ppermute | solution.py:66
  271.1 101.0 %collective-permute-start.65 = (bf16[256,1536]{1,0:T(8,128)(2,1)}, bf16[256,1536]{1,0:T(8,128)(2,1)}, u32[]{:S(2)}, u32[]{:S(2)}) collective-permute-start(bf16[256,1536]{1,0:T(8,128)(2,1)} %copy-done.10), channel_id=1, source_target_pairs={{0,2},{2,0},{1,3},{3,1},{4,6},{6,4},{5,7},{7,5},{8,10},{10,8},{9,1... | collective-permute-start | bytes 2359304 | tf_op jit(solution)/shard_map/ppermute | solution.py:66
  271.2 75.8 %collective-permute-start.62 = (bf16[256,1536]{1,0:T(8,128)(2,1)}, bf16[256,1536]{1,0:T(8,128)(2,1)}, u32[]{:S(2)}, u32[]{:S(2)}) collective-permute-start(bf16[256,1536]{1,0:T(8,128)(2,1)} %copy-done.10), channel_id=1, source_target_pairs={{0,4},{4,0},{1,5},{5,1},{2,6},{6,2},{3,7},{7,3},{8,12},{12,8},{9,1... | collective-permute-start | bytes 2359304 | tf_op jit(solution)/shard_map/ppermute | solution.py:66
  272.1 76.2 %collective-permute-start.61 = (bf16[256,1536]{1,0:T(8,128)(2,1)}, bf16[256,1536]{1,0:T(8,128)(2,1)}, u32[]{:S(2)}, u32[]{:S(2)}) collective-permute-start(bf16[256,1536]{1,0:T(8,128)(2,1)} %copy-done.10), channel_id=1, source_target_pairs={{0,1},{1,0},{2,3},{3,2},{4,5},{5,4},{6,7},{7,6},{8,9},{9,8},{10,11... | collective-permute-start | bytes 2359304 | tf_op jit(solution)/shard_map/ppermute | solution.py:66
  273.0 85.7 %collective-permute-start.71 = (bf16[256,1536]{0,1:T(8,128)(2,1)}, bf16[256,1536]{0,1:T(8,128)(2,1)}, u32[]{:S(2)}, u32[]{:S(2)}) collective-permute-start(bf16[256,1536]{0,1:T(8,128)(2,1)} %bitcast.417), channel_id=1, source_target_pairs={{0,4},{4,0},{1,5},{5,1},{2,6},{6,2},{3,7},{7,3},{8,12},{12,8},{9,1... | collective-permute-start | bytes 2359304 | tf_op jit(solution)/shard_map/ppermute | solution.py:66
  274.0 78.8 %collective-permute-start.70 = (bf16[256,1536]{0,1:T(8,128)(2,1)}, bf16[256,1536]{0,1:T(8,128)(2,1)}, u32[]{:S(2)}, u32[]{:S(2)}) collective-permute-start(bf16[256,1536]{0,1:T(8,128)(2,1)} %bitcast.418), channel_id=1, source_target_pairs={{0,1},{1,0},{2,3},{3,2},{4,5},{5,4},{6,7},{7,6},{8,9},{9,8},{10,11... | collective-permute-start | bytes 2359304 | tf_op jit(solution)/shard_map/ppermute | solution.py:66
  284.3 54.0 %all-to-all-start = ((f32[8,1,256]{2,1,0:T(1,128)}), f32[8,1,256]{2,1,0:T(1,128)}, u32[]{:S(2)}, u32[]{:S(2)}) async-start(f32[8,1,256]{2,1,0:T(1,128)} %all_to_all.36), calls=%async_computation | async-start | bytes 16384 | tf_op jit(solution)/shard_map/all_to_all | solution.py:58
  288.2 244.5 %reduce-scatter.7.cloned.1.call-start = ((), (), s32[]{:S(2)}) async-start(), calls=%async_computation.13 | async-start | bytes 2949120 | tf_op jit(solution)/shard_map/reduce_scatter | solution.py:62
  308.8 236.5 %reduce-scatter.9.cloned.1.call-start = ((), (), s32[]{:S(2)}) async-start(), calls=%async_computation.14 | async-start | bytes 2949120 | tf_op jit(solution)/shard_map/reduce_scatter | solution.py:62
  347.0 33.6 %collective-permute-start.74 = (bf16[256,1536]{0,1:T(8,128)(2,1)}, bf16[256,1536]{0,1:T(8,128)(2,1)S(1)}, u32[]{:S(2)}, u32[]{:S(2)}) collective-permute-start(bf16[256,1536]{0,1:T(8,128)(2,1)} %bitcast.420), channel_id=1, source_target_pairs={{0,2},{2,0},{1,3},{3,1},{4,6},{6,4},{5,7},{7,5},{8,10},{10,8},{9,1... | collective-permute-start | bytes 2359304 | tf_op jit(solution)/shard_map/ppermute | solution.py:66
  348.4 38.7 %collective-permute-start.56 = (bf16[4,256,1536]{2,1,0:T(8,128)(2,1)}, bf16[4,256,1536]{2,1,0:T(8,128)(2,1)S(1)}, u32[]{:S(2)}, u32[]{:S(2)}) collective-permute-start(bf16[4,256,1536]{2,1,0:T(8,128)(2,1)} %bitcast.452), channel_id=1, source_target_pairs={{0,2},{2,0},{1,3},{3,1},{4,6},{6,4},{5,7},{7,5},{8,10},{10,8},{9,1... | collective-permute-start | bytes 9437192 | tf_op jit(solution)/shard_map/ppermute | solution.py:66
  382.2 72.4 %collective-permute-start.42 = (bf16[4,256,1536]{2,1,0:T(8,128)(2,1)}, bf16[4,256,1536]{2,1,0:T(8,128)(2,1)}, u32[]{:S(2)}, u32[]{:S(2)}) collective-permute-start(bf16[4,256,1536]{2,1,0:T(8,128)(2,1)} %bitcast.81), channel_id=1, source_target_pairs={{0,2},{2,0},{1,3},{3,1},{4,6},{6,4},{5,7},{7,5},{8,10},{10,8},{9,1... | collective-permute-start | bytes 9437192 | tf_op jit(solution)/shard_map/ppermute | solution.py:66
  388.1 19.5 %collective-permute-start.57 = (bf16[2,128,1536]{2,1,0:T(8,128)(2,1)S(1)}, bf16[2,128,1536]{2,1,0:T(8,128)(2,1)S(1)}, u32[]{:S(2)}, u32[]{:S(2)}) collective-permute-start(bf16[2,128,1536]{2,1,0:T(8,128)(2,1)S(1)} %slice_bitcast_fusion.2), channel_id=1, source_target_pairs={{0,1},{1,0},{2,3},{3,2},{4,5},{5,4},{6,7},{7,6},{8,9},{9,8},{10,11... | collective-permute-start | bytes 2359304 | tf_op jit(solution)/shard_map/ppermute | solution.py:66
  388.6 19.4 %collective-permute-start.59 = (bf16[2,128,1536]{2,1,0:T(8,128)(2,1)S(1)}, bf16[2,128,1536]{2,1,0:T(8,128)(2,1)S(1)}, u32[]{:S(2)}, u32[]{:S(2)}) collective-permute-start(bf16[2,128,1536]{2,1,0:T(8,128)(2,1)S(1)} %slice_bitcast_fusion), channel_id=1, source_target_pairs={{0,4},{4,0},{1,5},{5,1},{2,6},{6,2},{3,7},{7,3},{8,12},{12,8},{9,1... | collective-permute-start | bytes 2359304 | tf_op jit(solution)/shard_map/ppermute | solution.py:66
  460.6 16.4 %all-to-all-start.2 = ((bf16[8,256,192]{1,2,0:T(8,128)(2,1)}), bf16[8,256,192]{1,2,0:T(8,128)(2,1)}, u32[]{:S(2)}, u32[]{:S(2)}) async-start(bf16[8,256,192]{1,2,0:T(8,128)(2,1)} %bitcast.421), calls=%async_computation.2 | async-start | bytes 1572864 | tf_op jit(solution)/shard_map/all_to_all | solution.py:58
  465.7 55.2 %collective-permute-start.43 = (bf16[2,128,1536]{2,1,0:T(8,128)(2,1)}, bf16[2,128,1536]{2,1,0:T(8,128)(2,1)}, u32[]{:S(2)}, u32[]{:S(2)}) collective-permute-start(bf16[2,128,1536]{2,1,0:T(8,128)(2,1)} %slice_bitcast_fusion.6), channel_id=1, source_target_pairs={{0,1},{1,0},{2,3},{3,2},{4,5},{5,4},{6,7},{7,6},{8,9},{9,8},{10,11... | collective-permute-start | bytes 2359304 | tf_op jit(solution)/shard_map/ppermute | solution.py:66
  468.6 52.3 %collective-permute-start.45 = (bf16[2,128,1536]{2,1,0:T(8,128)(2,1)}, bf16[2,128,1536]{2,1,0:T(8,128)(2,1)}, u32[]{:S(2)}, u32[]{:S(2)}) collective-permute-start(bf16[2,128,1536]{2,1,0:T(8,128)(2,1)} %slice_bitcast_fusion.4), channel_id=1, source_target_pairs={{0,4},{4,0},{1,5},{5,1},{2,6},{6,2},{3,7},{7,3},{8,12},{12,8},{9,1... | collective-permute-start | bytes 2359304 | tf_op jit(solution)/shard_map/ppermute | solution.py:66
  477.0 28.0 %all-to-all-start.1 = ((bf16[8,256,256]{1,2,0:T(8,128)(2,1)}), bf16[8,256,256]{1,2,0:T(8,128)(2,1)}, u32[]{:S(2)}, u32[]{:S(2)}) async-start(bf16[8,256,256]{1,2,0:T(8,128)(2,1)} %bitcast.415), calls=%async_computation.1 | async-start | bytes 2097152 | tf_op jit(solution)/shard_map/all_to_all | solution.py:58
  481.2 79.7 %reduce-scatter.5.cloned.1.call-start = ((), (), s32[]{:S(2)}) async-start(), calls=%async_computation.12 | async-start | bytes 2007040 | tf_op jit(solution)/shard_map/reduce_scatter | solution.py:62
  524.5 19.5 %collective-permute-start.46 = (bf16[128,1536]{1,0:T(8,128)(2,1)S(1)}, bf16[128,1536]{1,0:T(8,128)(2,1)}, u32[]{:S(2)}, u32[]{:S(2)}) collective-permute-start(bf16[128,1536]{1,0:T(8,128)(2,1)S(1)} %slice_bitcast_fusion.12), channel_id=1, source_target_pairs={{0,1},{1,0},{2,3},{3,2},{4,5},{5,4},{6,7},{7,6},{8,9},{9,8},{10,11... | collective-permute-start | bytes 1179656 | tf_op jit(solution)/shard_map/ppermute | solution.py:66
  530.7 27.0 %collective-permute-start.44 = (bf16[128,1536]{1,0:T(8,128)(2,1)}, bf16[128,1536]{1,0:T(8,128)(2,1)}, u32[]{:S(2)}, u32[]{:S(2)}) collective-permute-start(bf16[128,1536]{1,0:T(8,128)(2,1)} %slice_bitcast_fusion.14), channel_id=1, source_target_pairs={{0,4},{4,0},{1,5},{5,1},{2,6},{6,2},{3,7},{7,3},{8,12},{12,8},{9,1... | collective-permute-start | bytes 1179656 | tf_op jit(solution)/shard_map/ppermute | solution.py:66
  539.8 13.8 %all-to-all-start.5 = ((bf16[4,96,768]{2,1,0:T(8,128)(2,1)}), bf16[4,96,768]{2,1,0:T(8,128)(2,1)}, u32[]{:S(2)}, u32[]{:S(2)}) async-start(bf16[4,96,768]{2,1,0:T(8,128)(2,1)} %bitcast.433), calls=%async_computation.7 | async-start | bytes 1179648 | tf_op jit(solution)/shard_map/all_to_all | solution.py:58
  567.3 17.0 %all-to-all-start.4 = ((bf16[8,98,448]{2,1,0:T(8,128)(2,1)}), bf16[8,98,448]{2,1,0:T(8,128)(2,1)}, u32[]{:S(2)}, u32[]{:S(2)}) async-start(bf16[8,98,448]{2,1,0:T(8,128)(2,1)} %pad_maximum_fusion.2), calls=%async_computation.5 | async-start | bytes 1703936 | tf_op jit(solution)/shard_map/all_to_all | solution.py:58
  (134 other events, 1505.3 us)
Sparse Core Ops, SparseCore 0:
  268.9 48.3 reduce-scatter.10
  319.6 47.5 reduce-scatter.6
  369.6 47.5 reduce-scatter.8
  521.0 35.8 reduce-scatter.4

commit v4 on v3

--- a/solution.py
+++ b/solution.py
@@ -9,7 +9,7 @@
 HK = 2
 HD = 128
 MICRO = 2
-PLANE = ("c", "y", "x")
+PLANE = ("y", "c", "x")
 GROUP = ("z", "y", "c")
 
 
@@ -70,49 +70,112 @@
     return lax.axis_size("x") == 2
 
 
-def plane_gather(block):
+def plane_sides(block):
+    return swap(block, "x"), swap(block, "y")
+
+
+def plane_pieces(block, sides=None, before_corner=()):
+    half = block.shape[0] // 2
+    over_x, over_y = sides or plane_sides(block)
+    corner = lax.optimization_barrier((over_y[:half], over_x[half:]) + before_corner)
+    others = [over_x, over_y, swap(corner[0], "x"), swap(corner[1], "y")]
+    return [block] + others + [swap(block, "c")] + [swap(piece, "c") for piece in others]
+
+
+def plane_gather(block, sides=None, before_corner=()):
     if not by_pairs():
         return gather(block, PLANE)
-    half = block.shape[0] // 2
-    over_c = swap(block, "c")
-    over_y = swap(block, "y")
-    over_x = swap(block, "x")
-    over_both = [swap(over_y[:half], "x"), swap(over_x[half:], "y")]
-    others = [over_x, over_y] + over_both
-    pieces = [block] + others + [over_c] + [swap(piece, "c") for piece in others]
-    return jnp.concatenate(pieces, axis=0)
-
-
-def late_gather(block, after):
-    block, after = lax.optimization_barrier((block, after))
-    return plane_gather(block)
-
-
-def gather_halves(halves):
-    _, rows, cols = halves.shape
+    return jnp.concatenate(plane_pieces(block, sides, before_corner), axis=0)
+
+
+def gather_two(left, right):
+    rows = left.shape[0]
+    pieces = plane_pieces(jnp.concatenate([left, right], axis=0))
+    corners = (3, 4, 8, 9)
+    lefts = [piece[:rows] for n, piece in enumerate(pieces) if n not in corners[1::2]]
+    rights = [piece[-rows:] for n, piece in enumerate(pieces) if n not in corners[::2]]
+    return jnp.concatenate(lefts, axis=0), jnp.concatenate(rights, axis=0)
+
+
+def small_gather(block):
+    if not by_pairs():
+        return gather(block, PLANE)
+    for axis in ("x", "y", "c"):
+        block = jnp.concatenate([block, swap(block, axis)], axis=0)
+    return block
+
+
+def small_group_gather(block, *before_plane):
+    if not by_pairs():
+        return gather(block, GROUP)
+    total = along_z(block)[:, None, None]
+    total = after(total, *before_plane)
+    for dim, axis in ((1, "y"), (2, "c")):
+        other = swap(total, axis)
+        last = lax.axis_index(axis) == 1
+        pair = [jnp.where(last, other, total), jnp.where(last, total, other)]
+        total = jnp.concatenate(pair, axis=dim)
+    return total.reshape(-1, block.shape[1])
+
+
+def after(block, *others):
+    return lax.optimization_barrier((block,) + others)[0]
+
+
+def along_z(block):
     depth = lax.axis_size("z")
-    if not by_pairs():
-        total = gather(jnp.moveaxis(halves, 0, 1), GROUP)
-        return jnp.moveaxis(total, 1, 0)
-    z, y, c, x = (lax.axis_index(axis) for axis in ("z", "y", "c", "x"))
-    own = lax.dynamic_index_in_dim(halves, x, 0, keepdims=False)
-    column = jnp.zeros((depth, rows, cols), halves.dtype)
-    for k in range(depth):
-        piece = own
-        if k:
-            piece = lax.ppermute(own, "z", [(i, (i + k) % depth) for i in range(depth)])
-        column = lax.dynamic_update_index_in_dim(column, piece, (z - k) % depth, 0)
-    over_x, over_y = swap(column, "x"), swap(column, "y")
-    cut = depth // 2
+    order = jnp.stack(([block] + shifts(block))[::-1] * 2)
+    return lax.dynamic_slice_in_dim(order, (depth - 1 - lax.axis_index("z")) % depth, depth, 0)
+
+
+def column_of(halves):
+    own = lax.dynamic_index_in_dim(halves, lax.axis_index("x"), 0, keepdims=False)
+    return along_z(own).reshape(-1, halves.shape[2])
+
+
+def shifts(block):
+    depth = lax.axis_size("z")
+    return [
+        lax.ppermute(block, "z", [(i, (i + k) % depth) for i in range(depth)])
+        for k in range(1, depth)
+    ]
+
+
+def weight_sides(column):
+    cut = column.shape[0] // 2
+    over_x, over_y = plane_sides(column)
     near, far = swap(over_y[:cut], "x"), swap(over_x[cut:], "y")
-    total = jnp.zeros((2, depth, 2, 2, rows, cols), halves.dtype)
-    pieces = ((column, 0, 0, 0), (over_x, 0, 1, 0), (over_y, 0, 0, 1), (near, 0, 1, 1), (far, cut, 1, 1))
+    return [(column, 0, 0, 0), (over_x, 0, 1, 0), (over_y, 0, 0, 1), (near, 0, 1, 1), (far, cut, 1, 1)]
+
+
+def whole_weight(sides):
+    rows, cols = sides[0][0].shape
+    y, c, x = (lax.axis_index(axis) for axis in ("y", "c", "x"))
+    total = jnp.zeros((2, 2, 2, rows, cols), sides[0][0].dtype)
     for flip in (0, 1):
-        for piece, at, dx, dy in pieces:
+        for piece, first, dx, dy in sides:
             piece = swap(piece, "c") if flip else piece
-            start = (x ^ dx, at, y ^ dy, c ^ flip, 0, 0)
-            total = lax.dynamic_update_slice(total, piece[None, :, None, None], start)
+            start = (x ^ dx, y ^ dy, c ^ flip, first, 0)
+            total = lax.dynamic_update_slice(total, piece[None, None, None], start)
     return total.reshape(2, -1, cols)
+
+
+def by_row_order(array):
+    if not by_pairs():
+        return array
+    depth = lax.axis_size("z")
+    return jnp.swapaxes(array.reshape(array.shape[0], depth, 4, -1), 1, 2).reshape(array.shape)
+
+
+def from_row_order(array):
+    if not by_pairs():
+        return array
+    depth = lax.axis_size("z")
+    return jnp.swapaxes(array.reshape(array.shape[0], 4, depth, -1), 1, 2).reshape(array.shape)
+
+
+def all_rows(halves):
+    return jnp.moveaxis(gather(jnp.moveaxis(halves, 0, 1), GROUP), 1, 0)
 
 
 def add(left, right):
@@ -132,14 +195,24 @@
     return jnp.concatenate([upper, lower], axis=0)
 
 
-def by_distance(array):
+def flips(array):
+    for dim, axis in enumerate(("c", "y", "x")):
+        array = jnp.where(lax.axis_index(axis) == 1, jnp.flip(array, dim), array)
+    return array
+
+
+def to_distance(array):
     if not by_pairs():
         return array
     shape = array.shape
-    array = array.reshape((2, 2, 2) + shape[1:])
-    for dim, axis in enumerate(PLANE):
-        array = jnp.where(lax.axis_index(axis) == 1, jnp.flip(array, dim), array)
-    return array.reshape(shape)
+    return flips(jnp.swapaxes(array.reshape((2, 2, 2) + shape[1:]), 0, 1)).reshape(shape)
+
+
+def to_place(array):
+    if not by_pairs():
+        return array
+    shape = array.shape
+    return jnp.swapaxes(flips(array.reshape((2, 2, 2) + shape[1:])), 0, 1).reshape(shape)
 
 
 def own_block(array, rows):
@@ -151,7 +224,7 @@
     rows, total = cols.shape
     parts = 4 * lax.axis_size("x")
     pieces = jnp.moveaxis(cols.reshape(rows, parts, total // parts), 1, 0)
-    return by_distance(exchange(pieces, PLANE)).reshape(parts * rows, total // parts)
+    return to_distance(exchange(pieces, PLANE)).reshape(parts * rows, total // parts)
 
 
 def local(
@@ -189,27 +262,40 @@
     own_local = lax.axis_index(("y", "c"))
     own_expert = lax.axis_index("x") * local_count + own_local
 
+    qkv_cols = q_cols + 2 * kv_cols
+    q_group = q_cols // HK
+    qkv_halves = jnp.concatenate(
+        [
+            jnp.moveaxis(part.reshape(shard_rows, HK, -1), 1, 0)
+            for part in (w_query, w_key, w_value)
+        ],
+        axis=2,
+    )
+    out_halves = jnp.moveaxis(w_out.reshape(shard_rows, 2, -1), 1, 0)
     narrow = jnp.concatenate([w_router, norm1_gain[:, None], norm2_gain[:, None]], axis=1)
-    narrow = jnp.pad(narrow, ((0, 0), (0, -narrow.shape[1] % 128)))
-    narrow = gather(narrow, GROUP)
+    if by_pairs():
+        cot_sides = plane_sides(out_grad)
+        qkv_column = after(column_of(qkv_halves), *cot_sides)
+        out_column = column_of(after(out_halves, qkv_column))
+        qkv_sides = weight_sides(qkv_column)
+        corners = tuple(piece[0] for piece in qkv_sides[3:])
+        narrow = small_group_gather(narrow, *corners)
+        out_sides = weight_sides(after(out_column, narrow))
+        qkv_w = whole_weight(qkv_sides)
+        output_w = whole_weight(out_sides)
+        corners = tuple(piece[0] for piece in out_sides[3:])
+        ids_all = small_gather(after(expert_ids, *corners))
+        cot_all = plane_gather(out_grad, cot_sides, corners)
+    else:
+        narrow = small_group_gather(narrow)
+        ids_all = small_gather(expert_ids)
+        cot_all = plane_gather(out_grad)
+        qkv_w = all_rows(qkv_halves)
+        output_w = all_rows(out_halves)
     router_w = narrow[:, :experts_all]
     gains = narrow[:, experts_all : experts_all + 2].T.astype(f32)
     gain_one, gain_two = gains[0], gains[1]
-    qkv_cols = q_cols + 2 * kv_cols
-    q_group = q_cols // HK
-    qkv_w = gather_halves(
-        jnp.concatenate(
-            [
-                jnp.moveaxis(part.reshape(shard_rows, HK, -1), 1, 0)
-                for part in (w_query, w_key, w_value)
-            ],
-            axis=2,
-        )
-    )
-    output_w = gather_halves(jnp.moveaxis(w_out.reshape(shard_rows, 2, -1), 1, 0))
-
-    ids_all = plane_gather(expert_ids)
-    cot_all = plane_gather(out_grad)
+
     chosen_mask = jnp.any(
         ids_all[:, :, None] == jnp.arange(experts_all, dtype=jnp.int32)[None, None, :], axis=1
     )
@@ -221,7 +307,8 @@
     ).astype(bf16)
 
     cosine_tab, sine_tab = angles(length, HD)
-    inputs_f = tokens.astype(f32)
+    inputs_f = by_row_order(tokens).astype(f32)
+    gain_one = by_row_order(gain_one[None])
     first_in = rms_scale(inputs_f, gain_one).astype(bf16)
     qkv = jnp.einsum("id,gde->ige", first_in, qkv_w, preferred_element_type=f32)
     queries = (
@@ -233,19 +320,14 @@
     values_b = qkv[:, :, q_group + HD :].astype(bf16)
     positions = jnp.arange(length)
     allowed = (positions[None, :] <= positions[:, None]) | (positions[None, :] < prefix_len[0])
-
-    def masked_scores():
-        scores = jnp.einsum("ihrd,jhd->hrij", queries, keys_rot, preferred_element_type=f32)
-        return jnp.where(allowed, scores * score_scale, -1e30)
-
-    masked = masked_scores()
-    row_peak = jnp.max(masked, axis=-1, keepdims=True)
-    log_total = row_peak + jnp.log(jnp.sum(jnp.exp(masked - row_peak), axis=-1, keepdims=True))
-    prob_bf = jnp.exp(masked - log_total).astype(bf16)
-    attended = jnp.einsum("hrij,jhd->ihrd", prob_bf, values_b, preferred_element_type=f32)
+    scores = jnp.einsum("ihrd,jhd->hrij", queries, keys_rot, preferred_element_type=f32)
+    masked = jnp.where(allowed, scores * score_scale, -1e30)
+    probs = jax.nn.softmax(masked, axis=-1).astype(bf16)
+    attended = jnp.einsum("hrij,jhd->ihrd", probs, values_b, preferred_element_type=f32)
     attended = attended.reshape(length, HQ * HD).astype(bf16)
-    branch = jnp.einsum("ie,hed->ihd", attended, output_w, preferred_element_type=f32)
-    resid = inputs_f + branch.reshape(length, model_width)
+    attended_in = by_row_order(attended)
+    branch = [jnp.dot(attended_in, output_w[half], preferred_element_type=f32) for half in (0, 1)]
+    resid = tokens.astype(f32) + jnp.concatenate(branch, axis=1)
     second_in = rms_scale(resid, gain_two).astype(bf16)
 
     second_all = plane_gather(second_in)
@@ -301,9 +383,9 @@
     gate_signal = jnp.einsum(
         "bct,bc->bt", dispatch.astype(f32), gate_signal_rows, precision=lax.Precision.HIGHEST
     )
-    gate_signal = exchange(by_distance(gate_signal.reshape(plane, length)), PLANE)
+    gate_signal = exchange(to_place(gate_signal.reshape(plane, length)), PLANE)
     gate_signal = jnp.transpose(
-        gate_signal.reshape(2, 2, owners, length), (3, 2, 1, 0)
+        gate_signal.reshape(2, 2, owners, length), (3, 2, 0, 1)
     ).reshape(length, experts_all)
     expert_rows = jnp.einsum("bcf,fd->bcd", gated, down_w, preferred_element_type=f32)
     mixture = plane_sum(to_tokens(expert_rows)).astype(f32)
@@ -322,16 +404,24 @@
     resid_grad = cotangent + resid_norm_grad
     branch_grad = resid_grad.astype(bf16)
 
-    attended_all = late_gather(attended, second_all if by_pairs() else branch_grad)
+    if by_pairs():
+        attended_all, first_all = gather_two(
+            *lax.optimization_barrier((attended, from_row_order(first_in), second_all))[:2]
+        )
+    else:
+        attended_all = plane_gather(after(attended, branch_grad))
     branch_cols = by_source(branch_grad)
     output_part = left_product(attended_all, branch_cols)
-    attended_grad = jnp.einsum(
-        "ihd,hed->ie", branch_grad.reshape(length, 2, -1), output_w, preferred_element_type=f32
-    ).astype(bf16)
+    attended_grad = sum(
+        lax.dot_general(
+            part, output_w[half], (((1,), (1,)), ((), ())), preferred_element_type=f32
+        )
+        for half, part in enumerate(jnp.split(branch_grad, 2, axis=1))
+    )
+    attended_grad = from_row_order(attended_grad.astype(bf16))
     attended_grad = attended_grad.reshape(length, HK, group_size, HD)
-    masked = masked_scores()
-    prob_full = jnp.exp(masked - log_total)
-    prob_bf = prob_full.astype(bf16)
+    prob_bf = probs
+    prob_full = prob_bf.astype(f32)
     prob_grad = jnp.einsum("ihrd,jhd->hrij", attended_grad, values_b, preferred_element_type=f32)
     row_inner = jnp.sum(prob_full * prob_grad, axis=-1, keepdims=True)
     score_grad = (prob_full * (prob_grad - row_inner)).astype(bf16)
@@ -348,12 +438,14 @@
     key_back = rotary(key_rot_grad, cosine_tab, -sine_tab).astype(bf16)
     value_back = jnp.einsum("hrij,ihrd->jhd", prob_bf, attended_grad, preferred_element_type=f32)
     qkv_back = jnp.concatenate([query_back, key_back, value_back.astype(bf16)], axis=2)
-    first_all = late_gather(first_in, second_all if by_pairs() else output_part)
+    if not by_pairs():
+        first_all = plane_gather(after(first_in, output_part))
     qkv_part = left_product(first_all, by_source(qkv_back.reshape(length, qkv_cols)))
     first_grad = jnp.einsum("ige,gde->id", qkv_back, qkv_w, preferred_element_type=f32)
     _, norm_one_pull = jax.vjp(rms_scale, inputs_f, gain_one)
     input_norm_grad, gain_one_grad = norm_one_pull(first_grad)
-    tokens_grad = (resid_grad + input_norm_grad).astype(bf16)
+    gain_one_grad = from_row_order(gain_one_grad)[0]
+    tokens_grad = (resid_grad + from_row_order(input_norm_grad)).astype(bf16)
 
     narrow_part = jnp.concatenate(
         [router_acc, gain_one_grad[:, None], gain_two_grad[:, None]], axis=1
@@ -362,7 +454,7 @@
     narrow_part = jnp.pad(narrow_part, ((0, 0), (0, narrow_cols - narrow_part.shape[1])))
     narrow_part = jnp.transpose(
         narrow_part.reshape(depth, 2, 2, shard_rows, owners, narrow_cols // owners),
-        (2, 1, 4, 0, 3, 5),
+        (1, 2, 4, 0, 3, 5),
     ).reshape(plane, depth, shard_rows * narrow_cols // owners)
     narrow_part = jnp.sum(exchange(narrow_part, PLANE), axis=0)
     qkv_width = qkv_cols // plane
@@ -370,7 +462,7 @@
     narrow_len = narrow_part.shape[1]
     narrow_rows = -(-narrow_len // dense_cols)
     narrow_part = jnp.pad(narrow_part, ((0, 0), (0, narrow_rows * dense_cols - narrow_len)))
-    pad_rows = -(local_count * shard_rows + narrow_rows) % 8
+    pad_rows = -(local_count * shard_rows + narrow_rows) % 16
     dense_part = jnp.concatenate(
         [
             jnp.concatenate([qkv_part, output_part], axis=1).reshape(
@@ -383,17 +475,21 @@
     ).astype(bf16)
     dense_sum = scatter_sum(dense_part.reshape(-1, dense_cols), "z")
     wide_sum = dense_sum[: local_count * shard_rows].reshape(2, 2, 1, shard_rows, dense_cols)
-    wide_sum = jnp.broadcast_to(
-        jnp.swapaxes(wide_sum, 0, 1), (2, 2, owners, shard_rows, dense_cols)
-    ).reshape(plane, shard_rows, dense_cols)
+    wide_sum = jnp.broadcast_to(wide_sum, (2, 2, owners, shard_rows, dense_cols)).reshape(
+        plane, shard_rows, dense_cols
+    )
     narrow_sum = dense_sum[local_count * shard_rows :][:narrow_rows]
     narrow_sum = jnp.broadcast_to(narrow_sum[None], (plane, narrow_rows, dense_cols))
-    dense_sum = exchange(jnp.concatenate([wide_sum, narrow_sum], axis=1), PLANE)
+    pad_rows = -(shard_rows + narrow_rows) % 16
+    padding = jnp.zeros((plane, pad_rows, dense_cols), bf16)
+    dense_sum = exchange(jnp.concatenate([wide_sum, narrow_sum, padding], axis=1), PLANE)
     wide_sum = jnp.moveaxis(dense_sum[:, :shard_rows].astype(f32), 0, 1)
     qkv_sum = wide_sum[:, :, :qkv_width].reshape(shard_rows, HK, qkv_cols // HK)
     output_sum = wide_sum[:, :, qkv_width:].reshape(shard_rows, model_width)
-    narrow_sum = dense_sum[:, shard_rows:].reshape(2, 2, owners, narrow_rows * dense_cols)
-    narrow_sum = narrow_sum[lax.axis_index("c"), lax.axis_index("y"), :, :narrow_len]
+    narrow_sum = dense_sum[:, shard_rows : shard_rows + narrow_rows].reshape(
+        2, 2, owners, narrow_rows * dense_cols
+    )
+    narrow_sum = narrow_sum[lax.axis_index("y"), lax.axis_index("c"), :, :narrow_len]
     narrow_sum = jnp.moveaxis(
         narrow_sum.reshape(owners, shard_rows, narrow_cols // owners), 0, 1
     ).reshape(shard_rows, narrow_cols).astype(f32)

time: 610 us -> 596 us (0.977)
  local copies, waits for them, and re-layouts: 155 us -> 188 us
  waiting for transfers between devices: 136 us -> 112 us
  blocking collectives: 19.2 us -> 0 us
    ppermute x73 -> x60, waiting for transfers between devices: 96.1 us -> 71.4 us  [swap(): return lax.ppermute(block, axis, [(0, 1), (1, 0)])]
    all_gather x1 -> x0, blocking collectives: 19.2 us -> none  [gather(): return lax.all_gather(block, axes, axis=0, tiled=True)]
    another operation x5 -> x14, local copies, waits for them, and re-layouts: 7.06 us -> 23.8 us  [the longest x8 20.6 us: along_z(): order = jnp.stack(([block] + shifts(block))[::-1] * 2)]
    ppermute x73 -> x60, starting transfers between devices: 51.1 us -> 39.1 us  [swap(): return lax.ppermute(block, axis, [(0, 1), (1, 0)])]
    dynamic_update_slice x27 -> x20, local copies, waits for them, and re-layouts: 18.9 us -> 28.6 us  [whole_weight(): total = lax.dynamic_update_slice(total, piece[None, None, None], start)]
    ppermute x6 -> x9, starting transfers between devices: 7.92 us -> 15.6 us  [shifts(): lax.ppermute(block, 'z', [(i, (i + k) % depth) for i in range(depth)])]
    dot_general x4 -> x5, matrix products: 12.9 us -> 5.72 us  [the longest x2 2.49 us: local(): lax.dot_general(part, output_w[half], (((1,), (1,)), ((), ())), preferred...]
    dot_general x1 -> x0, local copies, waits for them, and re-layouts: 6.9 us -> none  [local(): jnp.einsum('ie,hed->ihd', attended, output_w, preferred_element_type=f32)]
  transfers between devices with their start and end apart: 91 -> 81, of which waited for: 36 -> 21; matrix products, arithmetic and copies ran while one was open for 45% -> 54% of each run, Pallas kernels for 0% -> 0%
where the time goes in v4:
time: 596 us; the launch traced here: 585 us
  local copies, waits for them, and re-layouts  188 us (32%)
  matrix products  130 us (22%)
  waiting for transfers between devices  112 us (19%)
  starting transfers between devices  86.2 us (14%)
  other arithmetic  52 us (9%)
  between operations  16.8 us (3%)
    ppermute x60, waiting for transfers between devices, swap(): return lax.ppermute(block, axis, [(0, 1), (1, 0)])  71.4 us
    unnamed x225, local copies, waits for them, and re-layouts  52.2 us
    all_to_all x8, waiting for transfers between devices, exchange(): return lax.all_to_all(block, axes, split_axis=0, concat_axis=0, tiled=True)  40.5 us
    ppermute x60, starting transfers between devices, swap(): return lax.ppermute(block, axis, [(0, 1), (1, 0)])  39.1 us
    all_to_all x8, starting transfers between devices, exchange(): return lax.all_to_all(block, axes, split_axis=0, concat_axis=0, tiled=True)  30.8 us
    dynamic_update_slice x20, local copies, waits for them, and re-layouts, whole_weight(): total = lax.dynamic_update_slice(total, piece[None, None, None], start)  28.6 us
    another operation x8, local copies, waits for them, and re-layouts, along_z(): order = jnp.stack(([block] + shifts(block))[::-1] * 2)  20.6 us
    ppermute x9, starting transfers between devices, shifts(): lax.ppermute(block, 'z', [(i, (i + k) % depth) for i in range(depth)])  15.6 us
  transfers between devices with their start and end apart: 81, of which 21 were waited for; matrix products, arithmetic and copies ran while one was open for 54% of the time, Pallas kernels for 0%

profile of v4, /device:TPU:0, one launch (start us, length us, event | category | flops | bytes accessed | tf_op | source)
XLA Modules:
  0.0 584.9 jit_solution(11528138361818223483)
XLA Ops:
  8.0 3.0 collective-permute-start.2
  30.7 3.1 copy.471
  44.0 8.6 %stack.61 = bf16[8,96,1024]{2,0,1:T(8,128)(2,1)} concatenate(bf16[1,96,1024]{2,0,1:T(2,128)(2,1)} %copy.426, bf16[1,96,1024]{2,0,1:T(2,128)(2,1)S(1)} %copy.427, bf16[1,96,1024]{2,0,1:T(2,128)(2,1)S(1)} %copy.428, bf16[1,96,1024]{2,0,1:T(2,128)(2,1)S(1)} %dynamic-slice_maximum_fusion, bf16[1,96,1024]{2,0,1:T(2,128)(2,1)} %copy.426, bf16[1,96,1024]{2,0,1:T(2,128)(2,1)S(1)} %copy.427, ...), dimensions={0} | concatenate | bytes 3145728 | tf_op jit(solution)/shard_map/stack | solution.py:127
  69.4 3.4 broadcast_in_dim.140
  79.0 7.0 %stack.65 = bf16[8,96,768]{2,0,1:T(8,128)(2,1)} concatenate(bf16[1,96,768]{2,0,1:T(2,128)(2,1)} %copy.444, bf16[1,96,768]{2,0,1:T(2,128)(2,1)S(1)} %copy.445, bf16[1,96,768]{2,0,1:T(2,128)(2,1)S(1)} %copy.446, bf16[1,96,768]{2,0,1:T(2,128)(2,1)S(1)} %constant_dynamic-slice_fusion.2, bf16[1,96,768]{2,0,1:T(2,128)(2,1)} %copy.444, bf16[1,96,768]{2,0,1:T(2,128)(2,1)S(1)} %copy.445, ...), dimensions={0} | concatenate | bytes 2359296 | tf_op jit(solution)/shard_map/stack | solution.py:127
  96.9 4.2 collective-permute-done.11
  126.9 4.6 fusion.114
  140.4 4.1 fusion.112
  202.7 4.2 convolution_convert_fusion.1
  206.9 8.9 %fusion.18 = f32[16,96,768]{2,1,0:T(8,128)} fusion(bf16[16,96,1536]{2,1,0:T(8,128)(2,1)S(1)} %convolution_convert_fusion.1, bf16[4,768,1536]{2,1,0:T(8,128)(2,1)} %param.24, s32[]{:T(128)S(6)} %select_n.214), kind=kOutput, calls=%fused_computation.50 | convolution fusion | flops 3623878656 | bytes 11796484 | tf_op jit(solution)/shard_map/bcd,fd->bcf/dot_general | solution.py:371
  219.6 7.4 %collective-permute-done.36 = bf16[128,1536]{1,0:T(8,128)(2,1)S(1)} collective-permute-done((bf16[128,1536]{1,0:T(8,128)(2,1)S(1)}, bf16[128,1536]{1,0:T(8,128)(2,1)S(1)}, u32[]{:S(2)}, u32[]{:S(2)}) %collective-permute-start.36) | collective-permute-done | bytes 393248 | tf_op jit(solution)/shard_map/ppermute | solution.py:66
  233.9 4.5 fusion.113
  238.5 4.3 convolution_convert_fusion.2
  243.5 6.5 %fusion.22 = f32[16,96,768]{2,1,0:T(8,128)S(1)} fusion(bf16[16,96,1536]{2,1,0:T(8,128)(2,1)S(1)} %convolution_convert_fusion.2, bf16[4,1536,768]{2,1,0:T(8,128)(2,1)} %param.23, s32[]{:T(128)S(6)} %select_n.214), kind=kOutput, calls=%fused_computation.54 | convolution fusion | flops 3623878656 | bytes 11796484 | tf_op jit(solution)/shard_map/bcd,df->bcf/dot_general | solution.py:366
  250.1 12.4 %fusion.9 = (bf16[16,96,768]{2,1,0:T(8,128)(2,1)}, f32[16,96]{1,0:T(8,128)S(1)}, bf16[16,96,768]{2,1,0:T(8,128)(2,1)}, f32[16,96,768]{2,1,0:T(8,128)S(1)}) fusion(f32[16,96,768]{2,1,0:T(8,128)S(1)} %fusion.22, f32[16,96,768]{2,1,0:T(8,128)S(1)} %bitcast.501, f32[16,96]{1,0:T(8,128)S(1)} %bitcast.496, ...), kind=kOutput, calls=%fused_computation.14 | convolution fusion | flops 3656907264 | bytes 25964548 | tf_op jit(solution)/shard_map/bcd,df->bcf/dot_general | solution.py:365
  264.7 5.7 bitcast_convert_fusion
  274.6 3.3 all-to-all-start
  278.2 6.5 %fusion.24 = f32[16,96,1536]{2,1,0:T(8,128)S(1)} fusion(bf16[16,96,768]{2,1,0:T(8,128)(2,1)} %get-tuple-element.48, bf16[4,1536,768]{2,1,0:T(8,128)(2,1)} %param.22, s32[]{:T(128)S(6)} %select_n.214), kind=kOutput, calls=%fused_computation.56 | convolution fusion | flops 3623878656 | bytes 14155780 | tf_op jit(solution)/shard_map/bcf,df->bcd/dot_general | solution.py:380
  284.7 6.6 %add_convert_fusion = bf16[16,96,1536]{2,1,0:T(8,128)(2,1)S(1)} fusion(f32[16,96,1536]{2,1,0:T(8,128)S(1)} %fusion.24, bf16[16,96,768]{2,1,0:T(8,128)(2,1)} %get-tuple-element.50, bf16[4,1536,768]{2,1,0:T(8,128)(2,1)} %param.23, s32[]{:T(128)S(6)} %select_n.214), kind=kOutput, calls=%fused_computation.1 | convolution fusion | flops 3628597248 | bytes 18874372 | tf_op jit(solution)/shard_map/bcf,df->bcd/dot_general | solution.py:381
  296.5 5.3 bitcast_convert_fusion.2
  302.3 9.4 %convolution_convert_fusion = bf16[16,96,1536]{2,1,0:T(8,128)(2,1)S(1)} fusion(bf16[4,768,1536]{2,1,0:T(8,128)(2,1)} %param.24, s32[]{:T(128)S(6)} %select_n.214, f32[16,96]{1,0:T(8,128)S(1)} %bitcast.498, f32[16,96,768]{2,1,0:T(8,128)} %copy-done.81, f32[16,96,768]{2,1,0:T(8,128)} %copy-done.82), kind=kOutput, calls=%fused_computation.21 | convolution fusion | flops 3639214080 | bytes 16521220 | tf_op jit(solution)/shard_map/bcf,fd->bcd/dot_general | solution.py:390
  317.2 5.3 bitcast_convert_fusion.1
  322.5 3.2 constant_dynamic-update-slice_fusion.34
  330.1 4.4 convolution_convert_fusion.4
  337.1 11.4 %collective-permute-done.62 = bf16[256,1536]{1,0:T(8,128)(2,1)} collective-permute-done((bf16[256,1536]{1,0:T(8,128)(2,1)}, bf16[256,1536]{1,0:T(8,128)(2,1)}, u32[]{:S(2)}, u32[]{:S(2)}) %collective-permute-start.62) | collective-permute-done | bytes 786464 | tf_op jit(solution)/shard_map/ppermute | solution.py:66
  350.6 4.1 collective-permute-done.67
  360.0 2.9 fusion.1
  370.1 12.4 %collective-permute-done.56 = bf16[2,128,1536]{2,1,0:T(8,128)(2,1)S(1)} collective-permute-done((bf16[2,128,1536]{2,1,0:T(8,128)(2,1)S(1)}, bf16[2,128,1536]{2,1,0:T(8,128)(2,1)S(1)}, u32[]{:S(2)}, u32[]{:S(2)}) %collective-permute-start.56) | collective-permute-done | bytes 786464 | tf_op jit(solution)/shard_map/ppermute | solution.py:66
  384.9 9.6 %collective-permute-done.59 = bf16[128,1536]{1,0:T(8,128)(2,1)S(1)} collective-permute-done((bf16[128,1536]{1,0:T(8,128)(2,1)S(1)}, bf16[128,1536]{1,0:T(8,128)(2,1)S(1)}, u32[]{:S(2)}, u32[]{:S(2)}) %collective-permute-start.59) | collective-permute-done | bytes 393248 | tf_op jit(solution)/shard_map/ppermute | solution.py:66
  395.0 9.0 %collective-permute-done.57 = bf16[128,1536]{1,0:T(8,128)(2,1)S(1)} collective-permute-done((bf16[128,1536]{1,0:T(8,128)(2,1)S(1)}, bf16[128,1536]{1,0:T(8,128)(2,1)S(1)}, u32[]{:S(2)}, u32[]{:S(2)}) %collective-permute-start.57) | collective-permute-done | bytes 393248 | tf_op jit(solution)/shard_map/ppermute | solution.py:66
  423.3 7.3 %multiply_reduce_fusion.2 = (f32[1536]{0:T(1024)S(1)}, f32[256]{0:T(256)}, f32[256,1536]{1,0:T(8,128)}) fusion(f32[256,1536]{1,0:T(8,128)} %copy.471, f32[256]{0:T(256)} %fusion.103, f32[1536]{0:T(1024)S(1)} %copy-done.61, bf16[256,2,1024]{2,0,1:T(8,128)(2,1)S(1)} %pad_maximum_fusion.2, bf16[2,1536,1024]{2,1,0:T(8,128)(2,1)} %bitcast.31), kind=kOutput, calls=%fused_computation.84 | convolution fusion | flops 1612970240 | bytes 10500096 | tf_op jit(solution)/shard_map/ige,gde->id/dot_general | solution.py:444
  437.7 3.4 all-to-all-start.3
  446.8 3.5 all-to-all-start.2
  458.7 11.5 %all-to-all-done.2 = bf16[8,256,192]{1,2,0:T(8,128)(2,1)S(1)} async-done(((bf16[8,256,192]{1,2,0:T(8,128)(2,1)}), bf16[8,256,192]{1,2,0:T(8,128)(2,1)S(1)}, u32[]{:S(2)}, u32[]{:S(2)}) %all-to-all-start.2) | async-done | bytes 786464 | tf_op jit(solution)/shard_map/all_to_all | solution.py:58
  470.2 4.3 all-to-all-start.1
  476.4 5.0 convolution_convert_fusion.8
  481.4 8.0 %all-to-all-done.1 = bf16[8,256,256]{1,2,0:T(8,128)(2,1)} async-done(((bf16[8,256,256]{1,2,0:T(8,128)(2,1)}), bf16[8,256,256]{1,2,0:T(8,128)(2,1)}, u32[]{:S(2)}, u32[]{:S(2)}) %all-to-all-start.1) | async-done | bytes 1048608 | tf_op jit(solution)/shard_map/all_to_all | solution.py:58
  491.6 4.7 convolution_convert_fusion.7
  506.8 4.1 all-to-all-start.7
  510.9 2.9 add_add_fusion
  513.9 8.2 %all-to-all-done.7 = bf16[4,96,768]{2,1,0:T(8,128)(2,1)} async-done(((bf16[4,96,768]{2,1,0:T(8,128)(2,1)}), bf16[4,96,768]{2,1,0:T(8,128)(2,1)}, u32[]{:S(2)}, u32[]{:S(2)}) %all-to-all-start.7) | async-done | bytes 589856 | tf_op jit(solution)/shard_map/all_to_all | solution.py:58
  522.0 3.5 all-to-all-start.5
  526.8 8.3 %all-to-all-done.5 = bf16[4,96,768]{2,1,0:T(8,128)(2,1)S(1)} async-done(((bf16[4,96,768]{2,1,0:T(8,128)(2,1)}), bf16[4,96,768]{2,1,0:T(8,128)(2,1)S(1)}, u32[]{:S(2)}, u32[]{:S(2)}) %all-to-all-start.5) | async-done | bytes 589856 | tf_op jit(solution)/shard_map/all_to_all | solution.py:58
  535.0 4.4 all-to-all-start.6
  544.6 3.1 copy.474
  551.5 4.2 all-to-all-start.4
  555.8 3.5 add_convert_fusion.1
  564.7 4.5 all-to-all-done.4
  (590 shorter events, 288.4 us)
Async XLA Ops:
  7.2 499.6 %reduce-scatter.11.cloned.1.call-start = ((), (), s32[]{:S(2)}) async-start(), calls=%async_computation.15 | async-start | bytes 2949120 | tf_op jit(solution)/shard_map/reduce_scatter | solution.py:62
  8.0 30.0 %collective-permute-start.2 = (bf16[96,10]{0,1:T(8,128)(2,1)S(1)}, bf16[96,10]{0,1:T(8,128)(2,1)S(1)}, u32[]{:S(2)}, u32[]{:S(2)}) collective-permute-start(bf16[96,10]{0,1:T(8,128)(2,1)S(1)} %pad_maximum_fusion.8), channel_id=1, source_target_pairs={{0,8},{8,16},{16,24},{24,0},{1,9},{9,17},{17,25},{25,1},{2,10},{10... | collective-permute-start | bytes 5768 | tf_op jit(solution)/shard_map/ppermute | solution.py:139
  11.1 25.5 %collective-permute-start.1 = (bf16[96,10]{0,1:T(8,128)(2,1)S(1)}, bf16[96,10]{0,1:T(8,128)(2,1)S(1)}, u32[]{:S(2)}, u32[]{:S(2)}) collective-permute-start(bf16[96,10]{0,1:T(8,128)(2,1)S(1)} %pad_maximum_fusion.8), channel_id=1, source_target_pairs={{0,16},{8,24},{16,0},{24,8},{1,17},{9,25},{17,1},{25,9},{2,18},{10... | collective-permute-start | bytes 5768 | tf_op jit(solution)/shard_map/ppermute | solution.py:139
  13.7 20.0 %collective-permute-start = (bf16[96,10]{0,1:T(8,128)(2,1)S(1)}, bf16[96,10]{0,1:T(8,128)(2,1)S(1)}, u32[]{:S(2)}, u32[]{:S(2)}) collective-permute-start(bf16[96,10]{0,1:T(8,128)(2,1)S(1)} %pad_maximum_fusion.8), channel_id=1, source_target_pairs={{0,24},{8,0},{16,8},{24,16},{1,25},{9,1},{17,9},{25,17},{2,26},{10... | collective-permute-start | bytes 5768 | tf_op jit(solution)/shard_map/ppermute | solution.py:139
  19.0 20.7 %collective-permute-start.5 = (bf16[96,1024]{1,0:T(8,128)(2,1)}, bf16[96,1024]{1,0:T(8,128)(2,1)S(1)}, u32[]{:S(2)}, u32[]{:S(2)}) collective-permute-start(bf16[96,1024]{1,0:T(8,128)(2,1)} %bitcast.386), channel_id=1, source_target_pairs={{0,8},{8,16},{16,24},{24,0},{1,9},{9,17},{17,25},{25,1},{2,10},{10... | collective-permute-start | bytes 589832 | tf_op jit(solution)/shard_map/ppermute | solution.py:139
  19.7 22.0 %collective-permute-start.4 = (bf16[96,1024]{1,0:T(8,128)(2,1)}, bf16[96,1024]{1,0:T(8,128)(2,1)}, u32[]{:S(2)}, u32[]{:S(2)}) collective-permute-start(bf16[96,1024]{1,0:T(8,128)(2,1)} %bitcast.386), channel_id=1, source_target_pairs={{0,16},{8,24},{16,0},{24,8},{1,17},{9,25},{17,1},{25,9},{2,18},{10... | collective-permute-start | bytes 589832 | tf_op jit(solution)/shard_map/ppermute | solution.py:139
  36.6 19.0 %collective-permute-start.7 = (bf16[256,1536]{1,0:T(8,128)(2,1)S(1)}, bf16[256,1536]{1,0:T(8,128)(2,1)}, u32[]{:S(2)}, u32[]{:S(2)}) collective-permute-start(bf16[256,1536]{1,0:T(8,128)(2,1)S(1)} %copy-done.12), channel_id=1, source_target_pairs={{0,4},{4,0},{1,5},{5,1},{2,6},{6,2},{3,7},{7,3},{8,12},{12,8},{9,1... | collective-permute-start | bytes 2359304 | tf_op jit(solution)/shard_map/ppermute | solution.py:66
  38.1 17.7 %collective-permute-start.6 = (bf16[256,1536]{1,0:T(8,128)(2,1)S(1)}, bf16[256,1536]{1,0:T(8,128)(2,1)}, u32[]{:S(2)}, u32[]{:S(2)}) collective-permute-start(bf16[256,1536]{1,0:T(8,128)(2,1)S(1)} %copy-done.12), channel_id=1, source_target_pairs={{0,1},{1,0},{2,3},{3,2},{4,5},{5,4},{6,7},{7,6},{8,9},{9,8},{10,11... | collective-permute-start | bytes 2359304 | tf_op jit(solution)/shard_map/ppermute | solution.py:66
  57.1 19.9 %collective-permute-start.21 = (bf16[96,768]{1,0:T(8,128)(2,1)S(1)}, bf16[96,768]{1,0:T(8,128)(2,1)S(1)}, u32[]{:S(2)}, u32[]{:S(2)}) collective-permute-start(bf16[96,768]{1,0:T(8,128)(2,1)S(1)} %bitcast.461), channel_id=1, source_target_pairs={{0,8},{8,16},{16,24},{24,0},{1,9},{9,17},{17,25},{25,1},{2,10},{10... | collective-permute-start | bytes 442376 | tf_op jit(solution)/shard_map/ppermute | solution.py:139
  57.8 19.4 %collective-permute-start.20 = (bf16[96,768]{1,0:T(8,128)(2,1)S(1)}, bf16[96,768]{1,0:T(8,128)(2,1)S(1)}, u32[]{:S(2)}, u32[]{:S(2)}) collective-permute-start(bf16[96,768]{1,0:T(8,128)(2,1)S(1)} %bitcast.462), channel_id=1, source_target_pairs={{0,16},{8,24},{16,0},{24,8},{1,17},{9,25},{17,1},{25,9},{2,18},{10... | collective-permute-start | bytes 442376 | tf_op jit(solution)/shard_map/ppermute | solution.py:139
  59.0 19.0 %collective-permute-start.19 = (bf16[96,768]{1,0:T(8,128)(2,1)S(1)}, bf16[96,768]{1,0:T(8,128)(2,1)S(1)}, u32[]{:S(2)}, u32[]{:S(2)}) collective-permute-start(bf16[96,768]{1,0:T(8,128)(2,1)S(1)} %bitcast.463), channel_id=1, source_target_pairs={{0,24},{8,0},{16,8},{24,16},{1,25},{9,1},{17,9},{25,17},{2,26},{10... | collective-permute-start | bytes 442376 | tf_op jit(solution)/shard_map/ppermute | solution.py:139
  61.8 26.7 %collective-permute-start.10 = (bf16[384,1024]{1,0:T(8,128)(2,1)}, bf16[384,1024]{1,0:T(8,128)(2,1)}, u32[]{:S(2)}, u32[]{:S(2)}) collective-permute-start(bf16[384,1024]{1,0:T(8,128)(2,1)} %bitcast.15), channel_id=1, source_target_pairs={{0,1},{1,0},{2,3},{3,2},{4,5},{5,4},{6,7},{7,6},{8,9},{9,8},{10,11... | collective-permute-start | bytes 2359304 | tf_op jit(solution)/shard_map/ppermute | solution.py:66
  63.3 27.8 %collective-permute-start.8 = (bf16[384,1024]{1,0:T(8,128)(2,1)}, bf16[384,1024]{1,0:T(8,128)(2,1)}, u32[]{:S(2)}, u32[]{:S(2)}) collective-permute-start(bf16[384,1024]{1,0:T(8,128)(2,1)} %bitcast.15), channel_id=1, source_target_pairs={{0,4},{4,0},{1,5},{5,1},{2,6},{6,2},{3,7},{7,3},{8,12},{12,8},{9,1... | collective-permute-start | bytes 2359304 | tf_op jit(solution)/shard_map/ppermute | solution.py:66
  77.0 115.9 %collective-permute-start.50 = (bf16[256,1536]{1,0:T(8,128)(2,1)S(1)}, bf16[256,1536]{1,0:T(8,128)(2,1)}, u32[]{:S(2)}, u32[]{:S(2)}) collective-permute-start(bf16[256,1536]{1,0:T(8,128)(2,1)S(1)} %copy-done.12), channel_id=1, source_target_pairs={{0,2},{2,0},{1,3},{3,1},{4,6},{6,4},{5,7},{7,5},{8,10},{10,8},{9,1... | collective-permute-start | bytes 2359304 | tf_op jit(solution)/shard_map/ppermute | solution.py:66
  77.2 30.0 %collective-permute-start.14 = (bf16[384,1024]{1,0:T(8,128)(2,1)}, bf16[384,1024]{1,0:T(8,128)(2,1)}, u32[]{:S(2)}, u32[]{:S(2)}) collective-permute-start(bf16[384,1024]{1,0:T(8,128)(2,1)} %bitcast.15), channel_id=1, source_target_pairs={{0,2},{2,0},{1,3},{3,1},{4,6},{6,4},{5,7},{7,5},{8,10},{10,8},{9,1... | collective-permute-start | bytes 2359304 | tf_op jit(solution)/shard_map/ppermute | solution.py:66
  78.0 120.5 %collective-permute-start.52 = (bf16[256,1536]{1,0:T(8,128)(2,1)}, bf16[256,1536]{1,0:T(8,128)(2,1)}, u32[]{:S(2)}, u32[]{:S(2)}) collective-permute-start(bf16[256,1536]{1,0:T(8,128)(2,1)} %collective-permute-done.7), channel_id=1, source_target_pairs={{0,2},{2,0},{1,3},{3,1},{4,6},{6,4},{5,7},{7,5},{8,10},{10,8},{9,1... | collective-permute-start | bytes 2359304 | tf_op jit(solution)/shard_map/ppermute | solution.py:66
  101.1 18.2 %collective-permute-start.15 = (bf16[384,1024]{1,0:T(8,128)(2,1)}, bf16[384,1024]{1,0:T(8,128)(2,1)S(1)}, u32[]{:S(2)}, u32[]{:S(2)}) collective-permute-start(bf16[384,1024]{1,0:T(8,128)(2,1)} %collective-permute-done.10), channel_id=1, source_target_pairs={{0,2},{2,0},{1,3},{3,1},{4,6},{6,4},{5,7},{7,5},{8,10},{10,8},{9,1... | collective-permute-start | bytes 2359304 | tf_op jit(solution)/shard_map/ppermute | solution.py:66
  121.4 41.8 %collective-permute-start.26 = (bf16[384,768]{1,0:T(8,128)(2,1)}, bf16[384,768]{1,0:T(8,128)(2,1)}, u32[]{:S(2)}, u32[]{:S(2)}) collective-permute-start(bf16[384,768]{1,0:T(8,128)(2,1)} %bitcast.48), channel_id=1, source_target_pairs={{0,2},{2,0},{1,3},{3,1},{4,6},{6,4},{5,7},{7,5},{8,10},{10,8},{9,1... | collective-permute-start | bytes 1769480 | tf_op jit(solution)/shard_map/ppermute | solution.py:66
  123.5 25.8 %collective-permute-start.23 = (bf16[384,768]{1,0:T(8,128)(2,1)}, bf16[384,768]{1,0:T(8,128)(2,1)}, u32[]{:S(2)}, u32[]{:S(2)}) collective-permute-start(bf16[384,768]{1,0:T(8,128)(2,1)} %bitcast.48), channel_id=1, source_target_pairs={{0,4},{4,0},{1,5},{5,1},{2,6},{6,2},{3,7},{7,3},{8,12},{12,8},{9,1... | collective-permute-start | bytes 1769480 | tf_op jit(solution)/shard_map/ppermute | solution.py:66
  124.7 27.3 %collective-permute-start.22 = (bf16[384,768]{1,0:T(8,128)(2,1)}, bf16[384,768]{1,0:T(8,128)(2,1)}, u32[]{:S(2)}, u32[]{:S(2)}) collective-permute-start(bf16[384,768]{1,0:T(8,128)(2,1)} %bitcast.48), channel_id=1, source_target_pairs={{0,1},{1,0},{2,3},{3,2},{4,5},{5,4},{6,7},{7,6},{8,9},{9,8},{10,11... | collective-permute-start | bytes 1769480 | tf_op jit(solution)/shard_map/ppermute | solution.py:66
  159.3 37.1 %collective-permute-start.51 = (bf16[256,1536]{1,0:T(8,128)(2,1)}, bf16[256,1536]{1,0:T(8,128)(2,1)}, u32[]{:S(2)}, u32[]{:S(2)}) collective-permute-start(bf16[256,1536]{1,0:T(8,128)(2,1)} %collective-permute-done.6), channel_id=1, source_target_pairs={{0,2},{2,0},{1,3},{3,1},{4,6},{6,4},{5,7},{7,5},{8,10},{10,8},{9,1... | collective-permute-start | bytes 2359304 | tf_op jit(solution)/shard_map/ppermute | solution.py:66
  189.9 39.2 %collective-permute-start.38 = (bf16[256,1536]{1,0:T(8,128)(2,1)S(1)}, bf16[256,1536]{1,0:T(8,128)(2,1)S(1)}, u32[]{:S(2)}, u32[]{:S(2)}) collective-permute-start(bf16[256,1536]{1,0:T(8,128)(2,1)S(1)} %get-tuple-element.45), channel_id=1, source_target_pairs={{0,2},{2,0},{1,3},{3,1},{4,6},{6,4},{5,7},{7,5},{8,10},{10,8},{9,1... | collective-permute-start | bytes 2359304 | tf_op jit(solution)/shard_map/ppermute | solution.py:66
  190.7 25.1 %collective-permute-start.35 = (bf16[256,1536]{1,0:T(8,128)(2,1)S(1)}, bf16[256,1536]{1,0:T(8,128)(2,1)S(1)}, u32[]{:S(2)}, u32[]{:S(2)}) collective-permute-start(bf16[256,1536]{1,0:T(8,128)(2,1)S(1)} %get-tuple-element.45), channel_id=1, source_target_pairs={{0,4},{4,0},{1,5},{5,1},{2,6},{6,2},{3,7},{7,3},{8,12},{12,8},{9,1... | collective-permute-start | bytes 2359304 | tf_op jit(solution)/shard_map/ppermute | solution.py:66
  192.8 23.0 %collective-permute-start.34 = (bf16[256,1536]{1,0:T(8,128)(2,1)S(1)}, bf16[256,1536]{1,0:T(8,128)(2,1)S(1)}, u32[]{:S(2)}, u32[]{:S(2)}) collective-permute-start(bf16[256,1536]{1,0:T(8,128)(2,1)S(1)} %get-tuple-element.45), channel_id=1, source_target_pairs={{0,1},{1,0},{2,3},{3,2},{4,5},{5,4},{6,7},{7,6},{8,9},{9,8},{10,11... | collective-permute-start | bytes 2359304 | tf_op jit(solution)/shard_map/ppermute | solution.py:66
  271.7 85.1 %collective-permute-start.63 = (bf16[512,1536]{1,0:T(8,128)(2,1)}, bf16[512,1536]{1,0:T(8,128)(2,1)}, u32[]{:S(2)}, u32[]{:S(2)}) collective-permute-start(bf16[512,1536]{1,0:T(8,128)(2,1)} %pad_maximum_fusion), channel_id=1, source_target_pairs={{0,2},{2,0},{1,3},{3,1},{4,6},{6,4},{5,7},{7,5},{8,10},{10,8},{9,1... | collective-permute-start | bytes 4718600 | tf_op jit(solution)/shard_map/ppermute | solution.py:66
  271.7 54.1 %collective-permute-start.61 = (bf16[512,1536]{1,0:T(8,128)(2,1)}, bf16[512,1536]{1,0:T(8,128)(2,1)}, u32[]{:S(2)}, u32[]{:S(2)}) collective-permute-start(bf16[512,1536]{1,0:T(8,128)(2,1)} %pad_maximum_fusion), channel_id=1, source_target_pairs={{0,4},{4,0},{1,5},{5,1},{2,6},{6,2},{3,7},{7,3},{8,12},{12,8},{9,1... | collective-permute-start | bytes 4718600 | tf_op jit(solution)/shard_map/ppermute | solution.py:66
  272.4 50.1 %collective-permute-start.60 = (bf16[512,1536]{1,0:T(8,128)(2,1)}, bf16[512,1536]{1,0:T(8,128)(2,1)}, u32[]{:S(2)}, u32[]{:S(2)}) collective-permute-start(bf16[512,1536]{1,0:T(8,128)(2,1)} %pad_maximum_fusion), channel_id=1, source_target_pairs={{0,1},{1,0},{2,3},{3,2},{4,5},{5,4},{6,7},{7,6},{8,9},{9,8},{10,11... | collective-permute-start | bytes 4718600 | tf_op jit(solution)/shard_map/ppermute | solution.py:66
  274.6 59.9 %all-to-all-start = ((f32[8,1,256]{2,1,0:T(1,128)}), f32[8,1,256]{2,1,0:T(1,128)S(1)}, u32[]{:S(2)}, u32[]{:S(2)}) async-start(f32[8,1,256]{2,1,0:T(1,128)} %all_to_all.48), calls=%async_computation | async-start | bytes 16384 | tf_op jit(solution)/shard_map/all_to_all | solution.py:58
  278.0 235.9 %reduce-scatter.7.cloned.1.call-start = ((), (), s32[]{:S(2)}) async-start(), calls=%async_computation.13 | async-start | bytes 2949120 | tf_op jit(solution)/shard_map/reduce_scatter | solution.py:62
  294.7 65.3 %collective-permute-start.55 = (bf16[4,256,1536]{2,1,0:T(8,128)(2,1)}, bf16[4,256,1536]{2,1,0:T(8,128)(2,1)}, u32[]{:S(2)}, u32[]{:S(2)}) collective-permute-start(bf16[4,256,1536]{2,1,0:T(8,128)(2,1)} %bitcast.88), channel_id=1, source_target_pairs={{0,2},{2,0},{1,3},{3,1},{4,6},{6,4},{5,7},{7,5},{8,10},{10,8},{9,1... | collective-permute-start | bytes 9437192 | tf_op jit(solution)/shard_map/ppermute | solution.py:66
  301.9 224.9 %reduce-scatter.9.cloned.1.call-start = ((), (), s32[]{:S(2)}) async-start(), calls=%async_computation.14 | async-start | bytes 2949120 | tf_op jit(solution)/shard_map/reduce_scatter | solution.py:62
  328.5 20.0 %collective-permute-start.62 = (bf16[256,1536]{1,0:T(8,128)(2,1)}, bf16[256,1536]{1,0:T(8,128)(2,1)}, u32[]{:S(2)}, u32[]{:S(2)}) collective-permute-start(bf16[256,1536]{1,0:T(8,128)(2,1)} %get-tuple-element.36), channel_id=1, source_target_pairs={{0,4},{4,0},{1,5},{5,1},{2,6},{6,2},{3,7},{7,3},{8,12},{12,8},{9,1... | collective-permute-start | bytes 2359304 | tf_op jit(solution)/shard_map/ppermute | solution.py:66
  334.5 30.0 %collective-permute-start.43 = (bf16[4,256,1536]{2,1,0:T(8,128)(2,1)}, bf16[4,256,1536]{2,1,0:T(8,128)(2,1)}, u32[]{:S(2)}, u32[]{:S(2)}) collective-permute-start(bf16[4,256,1536]{2,1,0:T(8,128)(2,1)} %bitcast.76), channel_id=1, source_target_pairs={{0,2},{2,0},{1,3},{3,1},{4,6},{6,4},{5,7},{7,5},{8,10},{10,8},{9,1... | collective-permute-start | bytes 9437192 | tf_op jit(solution)/shard_map/ppermute | solution.py:66
  334.7 20.1 %collective-permute-start.67 = (bf16[256,1536]{1,0:T(8,128)(2,1)S(1)}, bf16[256,1536]{1,0:T(8,128)(2,1)}, u32[]{:S(2)}, u32[]{:S(2)}) collective-permute-start(bf16[256,1536]{1,0:T(8,128)(2,1)S(1)} %get-tuple-element.37), channel_id=1, source_target_pairs={{0,1},{1,0},{2,3},{3,2},{4,5},{5,4},{6,7},{7,6},{8,9},{9,8},{10,11... | collective-permute-start | bytes 2359304 | tf_op jit(solution)/shard_map/ppermute | solution.py:66
  348.5 101.9 %collective-permute-start.65 = (bf16[512,1536]{1,0:T(8,128)(2,1)}, bf16[512,1536]{1,0:T(8,128)(2,1)}, u32[]{:S(2)}, u32[]{:S(2)}) collective-permute-start(bf16[512,1536]{1,0:T(8,128)(2,1)} %collective-permute-done.61), channel_id=1, source_target_pairs={{0,2},{2,0},{1,3},{3,1},{4,6},{6,4},{5,7},{7,5},{8,10},{10,8},{9,1... | collective-permute-start | bytes 4718600 | tf_op jit(solution)/shard_map/ppermute | solution.py:66
  354.7 86.3 %collective-permute-start.64 = (bf16[512,1536]{1,0:T(8,128)(2,1)}, bf16[512,1536]{1,0:T(8,128)(2,1)}, u32[]{:S(2)}, u32[]{:S(2)}) collective-permute-start(bf16[512,1536]{1,0:T(8,128)(2,1)} %collective-permute-done.60), channel_id=1, source_target_pairs={{0,2},{2,0},{1,3},{3,1},{4,6},{6,4},{5,7},{7,5},{8,10},{10,8},{9,1... | collective-permute-start | bytes 4718600 | tf_op jit(solution)/shard_map/ppermute | solution.py:66
  356.8 96.2 %collective-permute-start.66 = (bf16[256,1536]{1,0:T(8,128)(2,1)}, bf16[256,1536]{1,0:T(8,128)(2,1)}, u32[]{:S(2)}, u32[]{:S(2)}) collective-permute-start(bf16[256,1536]{1,0:T(8,128)(2,1)} %collective-permute-done.62), channel_id=1, source_target_pairs={{0,2},{2,0},{1,3},{3,1},{4,6},{6,4},{5,7},{7,5},{8,10},{10,8},{9,1... | collective-permute-start | bytes 2359304 | tf_op jit(solution)/shard_map/ppermute | solution.py:66
  363.0 19.5 %collective-permute-start.56 = (bf16[2,128,1536]{2,1,0:T(8,128)(2,1)S(1)}, bf16[2,128,1536]{2,1,0:T(8,128)(2,1)S(1)}, u32[]{:S(2)}, u32[]{:S(2)}) collective-permute-start(bf16[2,128,1536]{2,1,0:T(8,128)(2,1)S(1)} %slice_bitcast_fusion.2), channel_id=1, source_target_pairs={{0,1},{1,0},{2,3},{3,2},{4,5},{5,4},{6,7},{7,6},{8,9},{9,8},{10,11... | collective-permute-start | bytes 2359304 | tf_op jit(solution)/shard_map/ppermute | solution.py:66
  364.6 19.2 %collective-permute-start.58 = (bf16[2,128,1536]{2,1,0:T(8,128)(2,1)S(1)}, bf16[2,128,1536]{2,1,0:T(8,128)(2,1)S(1)}, u32[]{:S(2)}, u32[]{:S(2)}) collective-permute-start(bf16[2,128,1536]{2,1,0:T(8,128)(2,1)S(1)} %slice_bitcast_fusion), channel_id=1, source_target_pairs={{0,4},{4,0},{1,5},{5,1},{2,6},{6,2},{3,7},{7,3},{8,12},{12,8},{9,1... | collective-permute-start | bytes 2359304 | tf_op jit(solution)/shard_map/ppermute | solution.py:66
  382.5 72.7 %collective-permute-start.68 = (bf16[256,1536]{1,0:T(8,128)(2,1)}, bf16[256,1536]{1,0:T(8,128)(2,1)}, u32[]{:S(2)}, u32[]{:S(2)}) collective-permute-start(bf16[256,1536]{1,0:T(8,128)(2,1)} %collective-permute-done.67), channel_id=1, source_target_pairs={{0,2},{2,0},{1,3},{3,1},{4,6},{6,4},{5,7},{7,5},{8,10},{10,8},{9,1... | collective-permute-start | bytes 2359304 | tf_op jit(solution)/shard_map/ppermute | solution.py:66
  404.0 96.7 %collective-permute-start.44 = (bf16[2,128,1536]{2,1,0:T(8,128)(2,1)}, bf16[2,128,1536]{2,1,0:T(8,128)(2,1)}, u32[]{:S(2)}, u32[]{:S(2)}) collective-permute-start(bf16[2,128,1536]{2,1,0:T(8,128)(2,1)} %slice_bitcast_fusion.6), channel_id=1, source_target_pairs={{0,1},{1,0},{2,3},{3,2},{4,5},{5,4},{6,7},{7,6},{8,9},{9,8},{10,11... | collective-permute-start | bytes 2359304 | tf_op jit(solution)/shard_map/ppermute | solution.py:66
  441.1 59.6 %collective-permute-start.46 = (bf16[2,128,1536]{2,1,0:T(8,128)(2,1)}, bf16[2,128,1536]{2,1,0:T(8,128)(2,1)}, u32[]{:S(2)}, u32[]{:S(2)}) collective-permute-start(bf16[2,128,1536]{2,1,0:T(8,128)(2,1)} %slice_bitcast_fusion.4), channel_id=1, source_target_pairs={{0,4},{4,0},{1,5},{5,1},{2,6},{6,2},{3,7},{7,3},{8,12},{12,8},{9,1... | collective-permute-start | bytes 2359304 | tf_op jit(solution)/shard_map/ppermute | solution.py:66
  446.8 23.4 %all-to-all-start.2 = ((bf16[8,256,192]{1,2,0:T(8,128)(2,1)}), bf16[8,256,192]{1,2,0:T(8,128)(2,1)S(1)}, u32[]{:S(2)}, u32[]{:S(2)}) async-start(bf16[8,256,192]{1,2,0:T(8,128)(2,1)} %bitcast.433), calls=%async_computation.2 | async-start | bytes 1572864 | tf_op jit(solution)/shard_map/all_to_all | solution.py:58
  470.2 19.2 %all-to-all-start.1 = ((bf16[8,256,256]{1,2,0:T(8,128)(2,1)}), bf16[8,256,256]{1,2,0:T(8,128)(2,1)}, u32[]{:S(2)}, u32[]{:S(2)}) async-start(bf16[8,256,256]{1,2,0:T(8,128)(2,1)} %bitcast.431), calls=%async_computation.1 | async-start | bytes 2097152 | tf_op jit(solution)/shard_map/all_to_all | solution.py:58
  474.5 73.3 %reduce-scatter.5.cloned.1.call-start = ((), (), s32[]{:S(2)}) async-start(), calls=%async_computation.12 | async-start | bytes 2048000 | tf_op jit(solution)/shard_map/reduce_scatter | solution.py:62
  503.1 22.4 %collective-permute-start.47 = (bf16[128,1536]{1,0:T(8,128)(2,1)S(1)}, bf16[128,1536]{1,0:T(8,128)(2,1)}, u32[]{:S(2)}, u32[]{:S(2)}) collective-permute-start(bf16[128,1536]{1,0:T(8,128)(2,1)S(1)} %slice_bitcast_fusion.12), channel_id=1, source_target_pairs={{0,1},{1,0},{2,3},{3,2},{4,5},{5,4},{6,7},{7,6},{8,9},{9,8},{10,11... | collective-permute-start | bytes 1179656 | tf_op jit(solution)/shard_map/ppermute | solution.py:66
  504.9 34.5 %collective-permute-start.45 = (bf16[128,1536]{1,0:T(8,128)(2,1)}, bf16[128,1536]{1,0:T(8,128)(2,1)}, u32[]{:S(2)}, u32[]{:S(2)}) collective-permute-start(bf16[128,1536]{1,0:T(8,128)(2,1)} %slice_bitcast_fusion.14), channel_id=1, source_target_pairs={{0,4},{4,0},{1,5},{5,1},{2,6},{6,2},{3,7},{7,3},{8,12},{12,8},{9,1... | collective-permute-start | bytes 1179656 | tf_op jit(solution)/shard_map/ppermute | solution.py:66
  551.5 17.8 %all-to-all-start.4 = ((bf16[8,112,448]{2,1,0:T(8,128)(2,1)}), bf16[8,112,448]{2,1,0:T(8,128)(2,1)}, u32[]{:S(2)}, u32[]{:S(2)}) async-start(bf16[8,112,448]{2,1,0:T(8,128)(2,1)} %maximum_maximum_fusion.1), calls=%async_computation.5 | async-start | bytes 1835008 | tf_op jit(solution)/shard_map/all_to_all | solution.py:58
  (126 other events, 1052.1 us)
Sparse Core Ops, SparseCore 0:
  270.5 45.1 reduce-scatter.10
  318.0 47.5 reduce-scatter.6
  367.9 47.5 reduce-scatter.8
  500.8 33.2 reduce-scatter.4
